TPU v7x, 512 devices: a whole 4x8x8 slice. The times are simulated.
512 devices in a mesh: rows: 128 (over y, z, core), cols: 4 (over x).
Axes of the slice: x: 4, y: 8, z: 8, core: 2. Of those that a mesh axis runs over, the one named last changes fastest.
Arguments:
- rhs: bfloat16 [98304, 512], P('rows', 'cols'), may hold values from -6 to 6
- left_butterfly: float32 [2, 2, 98304], P(None, None, 'rows'), may hold values from -4 to 4
- right_butterfly: float32 [2, 2, 98304], P(None, None, 'rows'), may hold values from -4 to 4
- pivots: float32 [98304], P('rows'), may hold values from -2 to 2, as said below
- panels: bfloat16 [2, 98304, 2048], P(None, ('rows', 'cols')), may hold values from -0.125 to 0.125
- inverse_blocks: bfloat16 [2, 2048, 2048], P(None, 'rows'), as said below
Outputs:
- solution: float32 [98304, 512], P('rows', 'cols')
Inputs may be any that keep to these rules, and one draw needn't show every extreme that they name: `pivots`: magnitudes lie from 0.5 to 2, with either sign. `inverse_blocks`: each block is upper triangular with ones on its diagonal.
All inputs are finite; a program needn't handle non-finite values.
Results may differ from a plain program's by a relative error of at most 0.009.
Values may be sent and summed in bfloat16 or wider, within the bound.
No kernel may reach another device: no remote copies, remote signals or barrier semaphores. Data moves between devices by JAX's collectives and lax.ppermute only.
A program may use at most 64 MiB of HBM per device.

v0:
```python
import jax
import jax.numpy as jnp
from jax import lax
from jax.sharding import PartitionSpec as P


def from_partner(block, axis, apart):
    count = lax.axis_size(axis)
    route = []
    for low in range(count):
        high = low | 1 << apart
        if high != low and high < count:
            route += [(low, high), (high, low)]
    return lax.ppermute(block, axis, route)


def apply_level(values, coef, bit_number, transposed):
    own_part = coef[0][:, None]
    cross = coef[1][:, None]
    outgoing = cross * values if transposed else values
    arrived = from_partner(outgoing, "rows", bit_number)
    return own_part * values + (arrived if transposed else cross * arrived)


def solution_total(partial_solve, position, block_rows):
    summed = lax.psum(partial_solve, "rows")
    own_solved = lax.dynamic_slice_in_dim(summed, position * block_rows, block_rows, 0)
    return (own_solved, summed.astype(jnp.bfloat16))


def target_total(partial_target):
    summed = lax.psum(partial_target, "rows")
    return summed.astype(jnp.bfloat16)


def shards(rhs, left_butterfly, right_butterfly, pivots, panels, inverse_blocks):
    contract = (((0,), (0,)), ((), ()))
    row_count, group_width = rhs.shape
    block_rows = inverse_blocks.shape[1]
    band_width = inverse_blocks.shape[2]
    depth_bits = lax.axis_size("rows").bit_length() - 1
    outer_bit = depth_bits - 1
    inner_bit = depth_bits - 2
    position = lax.axis_index("rows")
    gathered = lax.all_gather(panels, "cols", axis=1, tiled=True)
    work = rhs.astype(jnp.float32)
    work = apply_level(work, left_butterfly[0], outer_bit, True)
    work = apply_level(work, left_butterfly[1], inner_bit, True)
    for band_index in range(2):
        low = band_index * block_rows
        high = low + block_rows
        band_in = work[low:high].astype(jnp.bfloat16)
        partial_solve = lax.dot_general(
            inverse_blocks[band_index], band_in, contract, preferred_element_type=jnp.float32
        )
        own_solved, rounded = solution_total(partial_solve, position, block_rows)
        update = jnp.dot(gathered[band_index], rounded, preferred_element_type=jnp.float32)
        work = jnp.concatenate([work[:low], own_solved, work[high:] - update[high:]], axis=0)
    scaled = work / pivots[:, None]
    result = scaled
    for band_index in (1, 0):
        low = band_index * block_rows
        high = low + block_rows
        below = jnp.concatenate(
            [jnp.zeros((high, group_width), jnp.bfloat16), result[high:].astype(jnp.bfloat16)],
            axis=0,
        )
        term = lax.dot_general(
            gathered[band_index], below, contract, preferred_element_type=jnp.float32
        )
        placed = lax.dynamic_update_slice_in_dim(
            jnp.zeros((band_width, group_width), jnp.float32),
            scaled[low:high],
            position * block_rows,
            0,
        )
        target_rounded = target_total(placed - term)
        solved = jnp.dot(
            inverse_blocks[band_index], target_rounded, preferred_element_type=jnp.float32
        )
        result = jnp.concatenate([result[:low], solved, result[high:]], axis=0)
    result = apply_level(result, right_butterfly[1], inner_bit, False)
    result = apply_level(result, right_butterfly[0], outer_bit, False)
    return result


def solution(mesh):
    in_specs = (
        P("rows", "cols"),
        P(None, None, "rows"),
        P(None, None, "rows"),
        P("rows"),
        P(None, ("rows", "cols"), None),
        P(None, "rows", None),
    )
    out_specs = P("rows", "cols")
    return jax.shard_map(shards, mesh=mesh, in_specs=in_specs, out_specs=out_specs, check_vma=False)
```

profile of v0, /device:TPU:1, one launch (start us, length us, event | category | flops | bytes accessed | tf_op | source)
XLA Modules:
  0.0 1514.2 jit_solution(11241928346381372751)
XLA Ops:
  8.2 1.1 copy.7
  9.3 8.4 collective-permute-start
  17.7 11.7 collective-permute-done
  29.5 10.3 collective-permute-start.1
  39.8 17.4 %collective-permute-done.1 = f32[768,128]{0,1:T(8,128)S(1)} collective-permute-done((f32[768,128]{0,1:T(8,128)S(1)}, f32[768,128]{0,1:T(8,128)S(1)}, u32[]{:S(2)}, u32[]{:S(2)}) %collective-permute-start.1) | collective-permute-done | bytes 393248 | tf_op jit(solution)/shard_map/ppermute | solution.py:14
  57.3 2.1 convolution_bitcast_fusion.1
  60.0 197.8 %all-reduce.7.cloned.1.call-done = f32[2048,128]{0,1:T(8,128)} async-done(((f32[2048,128]{0,1:T(8,128)}), f32[2048,128]{0,1:T(8,128)}) %all-reduce.7.cloned.1.call-update) | async-done | bytes 1048592 | tf_op jit(solution)/shard_map/psum | solution.py:26
  257.8 3.4 fusion.9
  261.5 1.3 convolution_bitcast_fusion
  262.9 0.9 constant_dynamic-slice_fusion.1
  263.8 192.3 %all-reduce.9.cloned.1.call-done = f32[2048,128]{0,1:T(8,128)} async-done(((f32[2048,128]{0,1:T(8,128)}), f32[2048,128]{0,1:T(8,128)}) %all-reduce.9.cloned.1.call-update) | async-done | bytes 1048592 | tf_op jit(solution)/shard_map/psum | solution.py:26
  456.1 3.4 fusion.8
  459.7 0.9 constant_dynamic-slice_fusion
  461.4 0.8 dynamic_update_slice.7
  462.2 2.5 fusion.5
  464.8 495.8 %all-reduce.10 = bf16[2048,128]{0,1:T(8,128)(2,1)S(1)} all-reduce(f32[2048,128]{0,1:T(8,128)S(1)} %fusion.5), channel_id=1, replica_groups=mesh['rows'=128,'cols'=4] {'rows'}, use_global_device_ids=true, to_apply=%region_2.0 | all-reduce | flops 262144 | bytes 1572864 | tf_op jit(solution)/shard_map/psum | solution.py:32
  961.0 0.8 dynamic_update_slice.6
  961.8 2.5 fusion.7
  964.4 511.2 %all-reduce.11 = bf16[2048,128]{0,1:T(8,128)(2,1)S(1)} all-reduce(f32[2048,128]{0,1:T(8,128)S(1)} %fusion.7), channel_id=1, replica_groups=mesh['rows'=128,'cols'=4] {'rows'}, use_global_device_ids=true, to_apply=%region_3.0 | all-reduce | flops 262144 | bytes 1572864 | tf_op jit(solution)/shard_map/psum | solution.py:32
  1476.1 1.9 collective-permute-start.2
  1478.1 10.7 collective-permute-done.2
  1488.9 7.4 collective-permute-start.3
  1496.3 9.5 collective-permute-done.3
  1505.9 0.9 copy.10
  (31 shorter events, 4.0 us)
Async XLA Ops:
  7.4 250.4 %all-reduce.7.cloned.1.call-start = ((), (), s32[]{:S(2)}) async-start(), calls=%async_computation | async-start | bytes 2097152 | tf_op jit(solution)/shard_map/psum | solution.py:26
  9.2 252.3 %copy-start = (bf16[2,16,2048]{2,1,0:T(8,128)(2,1)S(1)}, bf16[2,16,2048]{2,1,0:T(8,128)(2,1)}, u32[]{:S(2)}) copy-start(bf16[2,16,2048]{2,1,0:T(8,128)(2,1)} %param.11) | copy-start | bytes 393220
  9.3 20.1 %collective-permute-start = (f32[768,128]{0,1:T(8,128)S(1)}, f32[768,128]{0,1:T(8,128)S(1)}, u32[]{:S(2)}, u32[]{:S(2)}) collective-permute-start(f32[768,128]{0,1:T(8,128)S(1)} %convert_multiply_fusion), channel_id=1, source_target_pairs={{0,256},{256,0},{4,260},{260,4},{8,264},{264,8},{12,268},{268,12},... | collective-permute-start | bytes 1179656 | tf_op jit(solution)/shard_map/ppermute | solution.py:14
  29.5 27.7 %collective-permute-start.1 = (f32[768,128]{0,1:T(8,128)S(1)}, f32[768,128]{0,1:T(8,128)S(1)}, u32[]{:S(2)}, u32[]{:S(2)}) collective-permute-start(f32[768,128]{0,1:T(8,128)S(1)} %fusion.17), channel_id=1, source_target_pairs={{0,128},{128,0},{4,132},{132,4},{8,136},{136,8},{12,140},{140,12},... | collective-permute-start | bytes 1179656 | tf_op jit(solution)/shard_map/ppermute | solution.py:14
  59.4 198.4 %all-gather.2.cloned.1.call-start = ((), (), s32[]{:S(2)}) async-start(), calls=%async_computation.1 | async-start | bytes 7864320 | tf_op jit(solution)/shard_map/all_gather | solution.py:45
  60.0 400.7 %copy-start.2 = (f32[768]{0:T(1024)S(1)}, f32[768]{0:T(1024)}, u32[]{:S(2)}) copy-start(f32[768]{0:T(1024)} %param.9) | copy-start | bytes 9220
  60.0 396.1 %all-reduce.9.cloned.1.call-start = ((), (), s32[]{:S(2)}) async-start(), calls=%async_computation.2 | async-start | bytes 2097152 | tf_op jit(solution)/shard_map/psum | solution.py:26
  464.8 1013.3 %copy-start.1 = (f32[2,2,768]{2,1,0:T(2,128)S(1)}, f32[2,2,768]{2,1,0:T(2,128)}, u32[]{:S(2)}) copy-start(f32[2,2,768]{2,1,0:T(2,128)} %param.8) | copy-start | bytes 36868
  1476.1 12.7 collective-permute-start.2
  1488.9 16.9 %collective-permute-start.3 = (f32[768,128]{0,1:T(8,128)S(1)}, f32[768,128]{0,1:T(8,128)S(1)}, u32[]{:S(2)}, u32[]{:S(2)}) collective-permute-start(f32[768,128]{0,1:T(8,128)S(1)} %multiply_add_fusion.1), channel_id=1, source_target_pairs={{0,256},{256,0},{4,260},{260,4},{8,264},{264,8},{12,268},{268,12},... | collective-permute-start | bytes 1179656 | tf_op jit(solution)/shard_map/ppermute | solution.py:14
Sparse Core Ops, SparseCore 0:
  59.5 198.2 all-reduce.6
  263.0 193.0 all-reduce.8
Sparse Core Ops, SparseCore 1:
  61.9 73.1 all-gather.1
where the time goes:
time: 1520 us; the launch traced here: 1510 us
  blocking collectives  1010 us (66%)
  waiting for transfers between devices  440 us (29%)
  starting transfers between devices  28.1 us (2%)
  matrix products  15.8 us (1%)
    psum x2, blocking collectives, target_total(): summed = lax.psum(partial_target, 'rows')  1010 us
    psum x2, waiting for transfers between devices, solution_total(): summed = lax.psum(partial_solve, 'rows')  390 us
    ppermute x4, waiting for transfers between devices, from_partner(): return lax.ppermute(block, axis, route)  49.3 us
  transfers between devices with their start and end apart: 7, of which 6 were waited for; matrix products, arithmetic and copies ran while one was open for 0% of the time, Pallas kernels for 0%

commit v1 on v0

v1 whole, which is shorter than its diff:
```python
import jax
import jax.numpy as jnp
import numpy as np
from jax import lax
from jax.sharding import Mesh, PartitionSpec as P

BF = jnp.bfloat16
F32 = jnp.float32
ROWS = ("y", "z", "c")
T0 = (((0,), (0,)), ((), ()))


def grid_of(rows):
    z = 8 if rows >= 128 else 2
    return rows // (2 * z), z, 2


def swap_y(v, bit, count):
    return lax.ppermute(v, "y", [(i, i ^ bit) for i in range(count)])


def swap_core(v):
    return lax.ppermute(v, "c", [(0, 1), (1, 0)])


def everyone(block, axes, count):
    return lax.all_to_all(jnp.broadcast_to(block[None], (count,) + block.shape), axes, 0, 0)


def two_parts(v):
    high = v.astype(BF)
    return high, (v - high.astype(F32)).astype(BF)


def total(v):
    return jnp.sum(v.astype(F32), axis=0)


def shards(rhs, left, right, pivots, panels, inverse):
    ny, nz, nx = lax.axis_size("y"), lax.axis_size("z"), lax.axis_size("x")
    nzc = 2 * nz
    rb, band = inverse.shape[1], inverse.shape[2]
    width = rhs.shape[1]
    yb = nzc * rb
    low, core = 2 * rb, lax.axis_index("c")
    outer, inner = ny // 2, ny // 4
    first_core = core == 0

    def gather_all(block):
        mine = everyone(block, ("y", "z"), ny * nz)
        other = swap_core(mine)
        even = jnp.where(first_core, mine, other)
        odd = jnp.where(first_core, other, mine)
        return jnp.stack([even, odd], axis=1).reshape(band, width)

    def reduce_all(part):
        part = part.reshape(ny * nz, 2, rb, width)
        away = jnp.where(first_core, part[:, 1], part[:, 0]).astype(BF)
        mine = jnp.where(first_core, part[:, 0], part[:, 1])
        mine = (mine + swap_core(away).astype(F32)).astype(BF)
        return total(lax.all_to_all(mine, ("y", "z"), 0, 0))

    def reduce_zc(part):
        return total(lax.all_to_all(part.astype(BF).reshape(nzc, rb, width), ("z", "c"), 0, 0))

    cross_rows = lax.all_gather(panels[0, rb:low], ("y", "x"), axis=0, tiled=False)
    cross_rows = cross_rows.reshape(ny, nx, rb, band)[:, 0].reshape(ny * rb, band)
    gathered = lax.all_gather(panels, "x", axis=1, tiled=True)

    def columns(coef):
        v = coef[:, :, :low].reshape(8, rb).T
        return jnp.concatenate(two_parts(v), axis=1)

    table = jnp.concatenate([columns(left), columns(right)], axis=1)
    table = jnp.pad(table, ((0, 0), (0, yb - table.shape[1])))
    raw = jnp.concatenate([rhs[:rb], rhs[rb:low]], axis=1)
    if raw.shape[1] < yb:
        raw = jnp.pad(raw, ((0, 0), (0, yb - raw.shape[1])))
    tiles = inverse.reshape(2, rb, ny, yb).transpose(2, 0, 1, 3)
    shared = jnp.broadcast_to(jnp.stack([raw, table])[None], (ny, 2, rb, yb))
    message = jnp.concatenate([tiles, shared], axis=1)
    arrived = lax.all_to_all(message, "y", 0, 0)
    tile0 = arrived[:, 0].reshape(ny * rb, yb)
    tile1 = arrived[:, 1].reshape(ny * rb, yb)
    raws = arrived[:, 2].astype(F32)
    table = arrived[:, 3].astype(F32)

    def coefs(offset):
        v = table[:, :, offset:offset + 8] + table[:, :, offset + 8:offset + 16]
        return lambda level, which, b: v[:, :, level * 4 + which * 2 + b, None]

    lc, rc = coefs(0), coefs(16)
    pair = lambda v, bit: jnp.concatenate(
        [v[i ^ bit][None] for i in range(ny)], axis=0)

    def rotated(b):
        v = raws[:, :, b * width:(b + 1) * width]
        v = lc(0, 0, b) * v + pair(lc(0, 1, b) * v, outer)
        v = lc(1, 0, b) * v + pair(lc(1, 1, b) * v, inner)
        return v.reshape(ny * rb, width)

    x0, x1 = rotated(0), rotated(1)

    below = rhs[low:].astype(F32)
    c = left[:, :, low:, None]
    below = c[0, 0] * below + swap_y((c[0, 1] * below).astype(BF), outer, ny).astype(F32)
    below = c[1, 0] * below + swap_y((c[1, 1] * below).astype(BF), inner, ny).astype(F32)

    own0 = reduce_zc(lax.dot_general(tile0, x0.astype(BF), T0, preferred_element_type=F32))
    s0 = gather_all(own0.astype(BF))
    x1 = x1 - jnp.dot(cross_rows, s0, preferred_element_type=F32)
    own1 = reduce_zc(lax.dot_general(tile1, x1.astype(BF), T0, preferred_element_type=F32))
    s1 = gather_all(own1.astype(BF))
    s0, s1 = lax.optimization_barrier((s0, s1))

    update = jnp.dot(gathered[0], s0, preferred_element_type=F32)
    update += jnp.dot(gathered[1], s1, preferred_element_type=F32)
    scaled = (below - update[low:]) / pivots[low:, None]
    rounded = scaled.astype(BF)
    padded = jnp.concatenate([jnp.zeros((low, width), BF), rounded], axis=0)
    term1 = lax.dot_general(gathered[1], padded, T0, preferred_element_type=F32)
    term0 = lax.dot_general(gathered[0], padded, T0, preferred_element_type=F32)

    d = right[:, :, low:, None]
    out = d[1, 0] * scaled + d[1, 1] * swap_y(rounded, inner, ny).astype(F32)
    out = d[0, 0] * out + d[0, 1] * swap_y(out.astype(BF), outer, ny).astype(F32)

    target1 = own1 / pivots[rb:low, None] - reduce_all(term1)
    t1 = everyone(target1.astype(BF), ("z", "c"), nzc).reshape(yb, width)
    back1 = jnp.dot(tile1, t1, preferred_element_type=F32)
    term0 += lax.dot_general(cross_rows, back1.astype(BF), T0, preferred_element_type=F32)
    target0 = own0 / pivots[:rb, None] - reduce_all(term0)
    t0 = everyone(target0.astype(BF), ("z", "c"), nzc).reshape(yb, width)
    back0 = jnp.dot(tile0, t0, preferred_element_type=F32)

    def finished(v, b):
        v = v.reshape(ny, rb, width)
        v = rc(1, 0, b) * v + rc(1, 1, b) * pair(v, inner)
        return rc(0, 0, b) * v + rc(0, 1, b) * pair(v, outer)

    last = jnp.concatenate([finished(back0, 0), finished(back1, 1)], axis=1).astype(BF)
    head = total(lax.all_to_all(last, "y", 0, 0))
    return jnp.concatenate([head, out], axis=0)


def solution(mesh):
    rows, cols = mesh.devices.shape
    grid = Mesh(mesh.devices.reshape(grid_of(rows) + (cols,)), ("y", "z", "c", "x"))
    in_specs = (
        P(ROWS, "x"),
        P(None, None, ROWS),
        P(None, None, ROWS),
        P(ROWS),
        P(None, ROWS + ("x",), None),
        P(None, ROWS, None),
    )
    return jax.shard_map(
        shards, mesh=grid, in_specs=in_specs, out_specs=P(ROWS, "x"), check_vma=False)
```

time: 1520 us -> 287 us (0.19)
  blocking collectives: 1010 us -> 75.1 us
  waiting for transfers between devices: 440 us -> 91.9 us
  starting transfers between devices: 28.1 us -> 73.7 us
    psum x2 -> x0, blocking collectives: 1010 us -> none  [target_total(): summed = lax.psum(partial_target, 'rows')]
    psum x2 -> x0, waiting for transfers between devices: 390 us -> none  [solution_total(): summed = lax.psum(partial_solve, 'rows')]
    all_to_all x0 -> x4, blocking collectives: none -> 75.1 us  [the longest x2 40.9 us: reduce_zc(): lax.all_to_all(part.astype(BF).reshape(nzc, rb, width), ('z', 'c'), 0, 0)]
    ppermute x4 -> x8, waiting for transfers between devices: 49.3 us -> 3.28 us  [the longest x4 2.23 us: swap_core(): return lax.ppermute(v, 'c', [(0, 1), (1, 0)])]
    all_gather x1 -> x2, waiting for transfers between devices: 0.01 us -> 44.6 us  [the longest x1 23.3 us: shards(): gathered = lax.all_gather(panels, 'x', axis=1, tiled=True)]
    all_to_all x0 -> x6, waiting for transfers between devices: none -> 43.3 us  [the longest x2 19.1 us: reduce_all(): return total(lax.all_to_all(mine, ('y', 'z'), 0, 0))]
    all_to_all x0 -> x6, starting transfers between devices: none -> 41.6 us  [the longest x2 20.9 us: reduce_all(): return total(lax.all_to_all(mine, ('y', 'z'), 0, 0))]
    ppermute x4 -> x8, starting transfers between devices: 28 us -> 32.1 us  [the longest x4 18.4 us: swap_y(): return lax.ppermute(v, 'y', [(i, i ^ bit) for i in range(count)])]
  transfers between devices with their start and end apart: 7 -> 16, of which waited for: 6 -> 12; matrix products, arithmetic and copies ran while one was open for 0% -> 9% of each run, Pallas kernels for 0% -> 0%
where the time goes in v1:
time: 287 us; the launch traced here: 286 us
  waiting for transfers between devices  91.9 us (32%)
  blocking collectives  75.1 us (26%)
  starting transfers between devices  73.7 us (26%)
  local copies, waits for them, and re-layouts  14.5 us (5%)
  between operations  14.2 us (5%)
  matrix products  10.7 us (4%)
  other arithmetic  6.02 us (2%)
    all_to_all x2, blocking collectives, reduce_zc(): lax.all_to_all(part.astype(BF).reshape(nzc, rb, width), ('z', 'c'), 0, 0)  40.9 us
    all_gather x1, waiting for transfers between devices, shards(): gathered = lax.all_gather(panels, 'x', axis=1, tiled=True)  23.3 us
    all_gather x1, waiting for transfers between devices, shards(): lax.all_gather(panels[0, rb:low], ('y', 'x'), axis=0, tiled=False)  21.3 us
    all_to_all x2, starting transfers between devices, reduce_all(): return total(lax.all_to_all(mine, ('y', 'z'), 0, 0))  20.9 us
    all_to_all x2, waiting for transfers between devices, reduce_all(): return total(lax.all_to_all(mine, ('y', 'z'), 0, 0))  19.1 us
    ppermute x4, starting transfers between devices, swap_y(): return lax.ppermute(v, 'y', [(i, i ^ bit) for i in range(count)])  18.4 us
    all_to_all x1, blocking collectives, everyone(): lax.all_to_all(jnp.broadcast_to(block[None], (count,) + block.shape), axe...  17.5 us
    all_to_all x3, starting transfers between devices, everyone(): lax.all_to_all(jnp.broadcast_to(block[None], (count,) + block.shape), axe...  17.4 us
  transfers between devices with their start and end apart: 16, of which 12 were waited for; matrix products, arithmetic and copies ran while one was open for 9% of the time, Pallas kernels for 0%

profile of v1, /device:TPU:1, one launch (start us, length us, event | category | flops | bytes accessed | tf_op | source)
XLA Modules:
  0.0 286.2 jit_solution(10247756448011529859)
XLA Ops:
  12.2 16.7 %all_to_all.50 = bf16[8,4,16,256]{3,2,1,0:T(8,128)(2,1)S(1)} all-to-all(bf16[8,4,16,256]{3,2,1,0:T(8,128)(2,1)S(1)} %copy.61), channel_id=1, replica_groups=mesh['y'=8,'z'=8,'c'=2,'x'=4] {'y'}, dimensions={0} | all-to-all | bytes 524288 | tf_op jit(solution)/shard_map/all_to_all | solution.py:82
  30.1 21.5 %all_to_all.51 = bf16[16,16,128]{2,1,0:T(8,128)(2,1)S(1)} all-to-all(bf16[16,16,128]{2,1,0:T(8,128)(2,1)S(1)} %bitcast.273), channel_id=1, replica_groups=mesh['y'=8,'z'=8,'c'=2,'x'=4] {'z','c'}, dimensions={0} | all-to-all | bytes 131072 | tf_op jit(solution)/shard_map/all_to_all | solution.py:64
  51.7 17.5 %all_to_all.52 = bf16[64,16,128]{2,1,0:T(8,128)(2,1)S(1)} all-to-all(bf16[64,16,128]{2,1,0:T(8,128)(2,1)S(1)} %broadcast_in_dim.16), channel_id=1, replica_groups=mesh['y'=8,'z'=8,'c'=2,'x'=4] {'y','z'}, dimensions={0} | all-to-all | bytes 524288 | tf_op jit(solution)/shard_map/all_to_all | solution.py:27
  69.2 3.9 %collective-permute-start.2 = (bf16[64,16,128]{2,1,0:T(8,128)(2,1)S(1)}, bf16[64,16,128]{2,1,0:T(8,128)(2,1)S(1)}, u32[]{:S(2)}, u32[]{:S(2)}) collective-permute-start(bf16[64,16,128]{2,1,0:T(8,128)(2,1)S(1)} %all_to_all.52), channel_id=1, source_target_pairs={{0,4},{4,0},{1,5},{5,1},{2,6},{6,2},{3,7},{7,3},{8,12},{12,8},{9,1... | collective-permute-start | bytes 786440 | tf_op jit(solution)/shard_map/ppermute | solution.py:23
  74.3 21.3 %all-gather.3.cloned.1.call-done = bf16[32,16,2048]{2,1,0:T(8,128)(2,1)} async-done(((bf16[1,16,2048]{2,1,0:T(8,128)(2,1)}), bf16[32,16,2048]{2,1,0:T(8,128)(2,1)}) %all-gather.3.cloned.1.call-update) | async-done | bytes 2097168 | tf_op jit(solution)/shard_map/all_gather | solution.py:66
  97.2 19.4 %all_to_all.53 = bf16[16,16,128]{2,1,0:T(8,128)(2,1)S(1)} all-to-all(bf16[16,16,128]{2,1,0:T(8,128)(2,1)S(1)} %bitcast.272), channel_id=1, replica_groups=mesh['y'=8,'z'=8,'c'=2,'x'=4] {'z','c'}, dimensions={0} | all-to-all | bytes 131072 | tf_op jit(solution)/shard_map/all_to_all | solution.py:64
  117.4 5.2 %all-to-all-start.4 = ((bf16[64,16,128]{2,1,0:T(8,128)(2,1)}), bf16[64,16,128]{2,1,0:T(8,128)(2,1)S(1)}, u32[]{:S(2)}, u32[]{:S(2)}) async-start(bf16[64,16,128]{2,1,0:T(8,128)(2,1)} %broadcast_in_dim.17), calls=%async_computation.4 | async-start | bytes 524288 | tf_op jit(solution)/shard_map/all_to_all | solution.py:27
  122.9 6.9 %collective-permute-start = (bf16[736,128]{0,1:T(8,128)(2,1)S(1)}, bf16[736,128]{0,1:T(8,128)(2,1)S(1)}, u32[]{:S(2)}, u32[]{:S(2)}) collective-permute-start(bf16[736,128]{0,1:T(8,128)(2,1)S(1)} %fusion.16), channel_id=1, source_target_pairs={{0,256},{64,320},{128,384},{192,448},{256,0},{320,64},{384,128},{4... | collective-permute-start | bytes 565256 | tf_op jit(solution)/shard_map/ppermute | solution.py:19
  129.8 5.7 %all-to-all-done.4 = bf16[64,16,128]{2,1,0:T(8,128)(2,1)S(1)} async-done(((bf16[64,16,128]{2,1,0:T(8,128)(2,1)}), bf16[64,16,128]{2,1,0:T(8,128)(2,1)S(1)}, u32[]{:S(2)}, u32[]{:S(2)}) %all-to-all-start.4) | async-done | bytes 262176 | tf_op jit(solution)/shard_map/all_to_all | solution.py:27
  135.6 5.2 %collective-permute-start.3 = (bf16[64,16,128]{2,1,0:T(8,128)(2,1)S(1)}, bf16[64,16,128]{2,1,0:T(8,128)(2,1)S(1)}, u32[]{:S(2)}, u32[]{:S(2)}) collective-permute-start(bf16[64,16,128]{2,1,0:T(8,128)(2,1)S(1)} %all-to-all-done.4), channel_id=1, source_target_pairs={{0,4},{4,0},{1,5},{5,1},{2,6},{6,2},{3,7},{7,3},{8,12},{12,8},{9,1... | collective-permute-start | bytes 786440 | tf_op jit(solution)/shard_map/ppermute | solution.py:23
  141.9 4.5 %collective-permute-start.1 = (bf16[736,128]{0,1:T(8,128)(2,1)S(1)}, bf16[736,128]{0,1:T(8,128)(2,1)S(1)}, u32[]{:S(2)}, u32[]{:S(2)}) collective-permute-start(bf16[736,128]{0,1:T(8,128)(2,1)S(1)} %multiply_convert_fusion), channel_id=1, source_target_pairs={{0,128},{64,192},{128,0},{192,64},{256,384},{320,448},{384,256},{4... | collective-permute-start | bytes 565256 | tf_op jit(solution)/shard_map/ppermute | solution.py:19
  146.6 23.3 %all-gather.5.cloned.1.call-done = bf16[2,768,2048]{2,1,0:T(8,128)(2,1)} async-done(((bf16[2,192,2048]{2,1,0:T(8,128)(2,1)}), bf16[2,768,2048]{2,1,0:T(8,128)(2,1)}) %all-gather.5.cloned.1.call-update) | async-done | bytes 6291472 | tf_op jit(solution)/shard_map/all_gather | solution.py:68
  173.0 3.2 %fusion.8 = f32[768,128]{0,1:T(8,128)S(1)} fusion(f32[128,768]{1,0:T(8,128)S(1)} %fusion.1, bf16[2048,128]{1,0:T(8,128)(2,1)S(1)} %bitcast.268, bf16[2,768,2048]{2,1,0:T(8,128)(2,1)} %all-gather.5.cloned.1.call-done), kind=kOutput, calls=%fused_computation.10 | convolution fusion | flops 402751488 | bytes 4456448 | tf_op jit(solution)/shard_map/dot_general | solution.py:117
  182.3 13.0 %all-to-all-start.5 = ((bf16[64,16,128]{2,1,0:T(8,128)(2,1)}), bf16[64,16,128]{2,1,0:T(8,128)(2,1)S(1)}, u32[]{:S(2)}, u32[]{:S(2)}) async-start(bf16[64,16,128]{2,1,0:T(8,128)(2,1)} %fusion.13), calls=%async_computation.5 | async-start | bytes 524288 | tf_op jit(solution)/shard_map/all_to_all | solution.py:61
  197.0 3.8 %collective-permute-start.6 = (bf16[736,128]{0,1:T(8,128)(2,1)S(1)}, bf16[736,128]{0,1:T(8,128)(2,1)S(1)}, u32[]{:S(2)}, u32[]{:S(2)}) collective-permute-start(bf16[736,128]{0,1:T(8,128)(2,1)S(1)} %get-tuple-element.17), channel_id=1, source_target_pairs={{0,128},{64,192},{128,0},{192,64},{256,384},{320,448},{384,256},{4... | collective-permute-start | bytes 565256 | tf_op jit(solution)/shard_map/ppermute | solution.py:19
  200.9 7.4 %all-to-all-done.5 = bf16[64,16,128]{2,1,0:T(8,128)(2,1)S(1)} async-done(((bf16[64,16,128]{2,1,0:T(8,128)(2,1)}), bf16[64,16,128]{2,1,0:T(8,128)(2,1)S(1)}, u32[]{:S(2)}, u32[]{:S(2)}) %all-to-all-start.5) | async-done | bytes 262176 | tf_op jit(solution)/shard_map/all_to_all | solution.py:61
  209.1 6.3 %all-to-all-start.6 = ((bf16[16,16,128]{2,1,0:T(8,128)(2,1)}), bf16[16,16,128]{2,1,0:T(8,128)(2,1)S(1)}, u32[]{:S(2)}, u32[]{:S(2)}) async-start(bf16[16,16,128]{2,1,0:T(8,128)(2,1)} %broadcast_in_dim.18), calls=%async_computation.6 | async-start | bytes 131072 | tf_op jit(solution)/shard_map/all_to_all | solution.py:27
  219.3 3.9 %all-to-all-done.6 = bf16[16,16,128]{2,1,0:T(8,128)(2,1)S(1)} async-done(((bf16[16,16,128]{2,1,0:T(8,128)(2,1)}), bf16[16,16,128]{2,1,0:T(8,128)(2,1)S(1)}, u32[]{:S(2)}, u32[]{:S(2)}) %all-to-all-start.6) | async-done | bytes 65568 | tf_op jit(solution)/shard_map/all_to_all | solution.py:27
  231.0 7.9 %all-to-all-start.7 = ((bf16[64,16,128]{2,1,0:T(8,128)(2,1)}), bf16[64,16,128]{2,1,0:T(8,128)(2,1)S(1)}, u32[]{:S(2)}, u32[]{:S(2)}) async-start(bf16[64,16,128]{2,1,0:T(8,128)(2,1)} %fusion.14), calls=%async_computation.7 | async-start | bytes 524288 | tf_op jit(solution)/shard_map/all_to_all | solution.py:61
  240.4 11.6 %all-to-all-done.7 = bf16[64,16,128]{2,1,0:T(8,128)(2,1)S(1)} async-done(((bf16[64,16,128]{2,1,0:T(8,128)(2,1)}), bf16[64,16,128]{2,1,0:T(8,128)(2,1)S(1)}, u32[]{:S(2)}, u32[]{:S(2)}) %all-to-all-start.7) | async-done | bytes 262176 | tf_op jit(solution)/shard_map/all_to_all | solution.py:61
  252.9 5.9 %all-to-all-start.8 = ((bf16[16,16,128]{2,1,0:T(8,128)(2,1)}), bf16[16,16,128]{2,1,0:T(8,128)(2,1)S(1)}, u32[]{:S(2)}, u32[]{:S(2)}) async-start(bf16[16,16,128]{2,1,0:T(8,128)(2,1)} %broadcast_in_dim.19), calls=%async_computation.8 | async-start | bytes 131072 | tf_op jit(solution)/shard_map/all_to_all | solution.py:27
  258.9 7.7 %all-to-all-done.8 = bf16[16,16,128]{2,1,0:T(8,128)(2,1)S(1)} async-done(((bf16[16,16,128]{2,1,0:T(8,128)(2,1)}), bf16[16,16,128]{2,1,0:T(8,128)(2,1)S(1)}, u32[]{:S(2)}, u32[]{:S(2)}) %all-to-all-start.8) | async-done | bytes 65568 | tf_op jit(solution)/shard_map/all_to_all | solution.py:27
  267.7 3.4 %all-to-all-start.9 = ((bf16[8,32,128]{2,1,0:T(8,128)(2,1)}), bf16[8,32,128]{2,1,0:T(8,128)(2,1)S(1)}, u32[]{:S(2)}, u32[]{:S(2)}) async-start(bf16[8,32,128]{2,1,0:T(8,128)(2,1)} %pad_maximum_fusion.4), calls=%async_computation.9 | async-start | bytes 131072 | tf_op jit(solution)/shard_map/all_to_all | solution.py:142
  271.3 6.9 %all-to-all-done.9 = bf16[8,32,128]{2,1,0:T(8,128)(2,1)S(1)} async-done(((bf16[8,32,128]{2,1,0:T(8,128)(2,1)}), bf16[8,32,128]{2,1,0:T(8,128)(2,1)S(1)}, u32[]{:S(2)}, u32[]{:S(2)}) %all-to-all-start.9) | async-done | bytes 65568 | tf_op jit(solution)/shard_map/all_to_all | solution.py:142
  (147 shorter events, 39.9 us)
Async XLA Ops:
  6.5 89.0 %all-gather.3.cloned.1.call-start = ((), (), s32[]{:S(2)}) async-start(), calls=%async_computation.10 | async-start | bytes 2162688 | tf_op jit(solution)/shard_map/all_gather | solution.py:66
  8.0 161.9 %all-gather.5.cloned.1.call-start = ((), (), s32[]{:S(2)}) async-start(), calls=%async_computation.11 | async-start | bytes 7864320 | tf_op jit(solution)/shard_map/all_gather | solution.py:68
  51.6 70.9 %copy-start.2 = (f32[2,2,768]{2,1,0:T(2,128)S(1)}, f32[2,2,768]{2,1,0:T(2,128)}, u32[]{:S(2)}) copy-start(f32[2,2,768]{2,1,0:T(2,128)} %param.7) | copy-start | bytes 36868
  51.7 71.0 %slice-start = ((bf16[768,128]{1,0:T(8,128)(2,1)}), bf16[736,128]{1,0:T(8,128)(2,1)S(1)}, s32[]{:S(2)}) async-start(bf16[768,128]{1,0:T(8,128)(2,1)} %param.6), calls=%async_computation.12 | async-start | bytes 376832 | tf_op jit(solution)/shard_map/slice | solution.py:104
  69.2 5.0 %collective-permute-start.2 = (bf16[64,16,128]{2,1,0:T(8,128)(2,1)S(1)}, bf16[64,16,128]{2,1,0:T(8,128)(2,1)S(1)}, u32[]{:S(2)}, u32[]{:S(2)}) collective-permute-start(bf16[64,16,128]{2,1,0:T(8,128)(2,1)S(1)} %all_to_all.52), channel_id=1, source_target_pairs={{0,4},{4,0},{1,5},{5,1},{2,6},{6,2},{3,7},{7,3},{8,12},{12,8},{9,1... | collective-permute-start | bytes 786440 | tf_op jit(solution)/shard_map/ppermute | solution.py:23
  73.1 67.6 %copy-start.12 = (f32[768]{0:T(1024)S(1)}, f32[768]{0:T(1024)}, u32[]{:S(2)}) copy-start(f32[768]{0:T(1024)} %param.9) | copy-start | bytes 9220
  117.4 18.2 %all-to-all-start.4 = ((bf16[64,16,128]{2,1,0:T(8,128)(2,1)}), bf16[64,16,128]{2,1,0:T(8,128)(2,1)S(1)}, u32[]{:S(2)}, u32[]{:S(2)}) async-start(bf16[64,16,128]{2,1,0:T(8,128)(2,1)} %broadcast_in_dim.17), calls=%async_computation.4 | async-start | bytes 524288 | tf_op jit(solution)/shard_map/all_to_all | solution.py:27
  122.9 18.9 %collective-permute-start = (bf16[736,128]{0,1:T(8,128)(2,1)S(1)}, bf16[736,128]{0,1:T(8,128)(2,1)S(1)}, u32[]{:S(2)}, u32[]{:S(2)}) collective-permute-start(bf16[736,128]{0,1:T(8,128)(2,1)S(1)} %fusion.16), channel_id=1, source_target_pairs={{0,256},{64,320},{128,384},{192,448},{256,0},{320,64},{384,128},{4... | collective-permute-start | bytes 565256 | tf_op jit(solution)/shard_map/ppermute | solution.py:19
  135.6 10.8 %collective-permute-start.3 = (bf16[64,16,128]{2,1,0:T(8,128)(2,1)S(1)}, bf16[64,16,128]{2,1,0:T(8,128)(2,1)S(1)}, u32[]{:S(2)}, u32[]{:S(2)}) collective-permute-start(bf16[64,16,128]{2,1,0:T(8,128)(2,1)S(1)} %all-to-all-done.4), channel_id=1, source_target_pairs={{0,4},{4,0},{1,5},{5,1},{2,6},{6,2},{3,7},{7,3},{8,12},{12,8},{9,1... | collective-permute-start | bytes 786440 | tf_op jit(solution)/shard_map/ppermute | solution.py:23
  141.9 34.3 %collective-permute-start.1 = (bf16[736,128]{0,1:T(8,128)(2,1)S(1)}, bf16[736,128]{0,1:T(8,128)(2,1)S(1)}, u32[]{:S(2)}, u32[]{:S(2)}) collective-permute-start(bf16[736,128]{0,1:T(8,128)(2,1)S(1)} %multiply_convert_fusion), channel_id=1, source_target_pairs={{0,128},{64,192},{128,0},{192,64},{256,384},{320,448},{384,256},{4... | collective-permute-start | bytes 565256 | tf_op jit(solution)/shard_map/ppermute | solution.py:19
  177.7 3.8 %collective-permute-start.4 = (bf16[64,16,128]{2,1,0:T(8,128)(2,1)S(1)}, bf16[64,16,128]{2,1,0:T(8,128)(2,1)S(1)}, u32[]{:S(2)}, u32[]{:S(2)}) collective-permute-start(bf16[64,16,128]{2,1,0:T(8,128)(2,1)S(1)} %fusion.18), channel_id=1, source_target_pairs={{0,4},{4,0},{1,5},{5,1},{2,6},{6,2},{3,7},{7,3},{8,12},{12,8},{9,1... | collective-permute-start | bytes 786440 | tf_op jit(solution)/shard_map/ppermute | solution.py:23
  182.3 26.0 %all-to-all-start.5 = ((bf16[64,16,128]{2,1,0:T(8,128)(2,1)}), bf16[64,16,128]{2,1,0:T(8,128)(2,1)S(1)}, u32[]{:S(2)}, u32[]{:S(2)}) async-start(bf16[64,16,128]{2,1,0:T(8,128)(2,1)} %fusion.13), calls=%async_computation.5 | async-start | bytes 524288 | tf_op jit(solution)/shard_map/all_to_all | solution.py:61
  197.0 18.3 %collective-permute-start.6 = (bf16[736,128]{0,1:T(8,128)(2,1)S(1)}, bf16[736,128]{0,1:T(8,128)(2,1)S(1)}, u32[]{:S(2)}, u32[]{:S(2)}) collective-permute-start(bf16[736,128]{0,1:T(8,128)(2,1)S(1)} %get-tuple-element.17), channel_id=1, source_target_pairs={{0,128},{64,192},{128,0},{192,64},{256,384},{320,448},{384,256},{4... | collective-permute-start | bytes 565256 | tf_op jit(solution)/shard_map/ppermute | solution.py:19
  209.1 14.1 %all-to-all-start.6 = ((bf16[16,16,128]{2,1,0:T(8,128)(2,1)}), bf16[16,16,128]{2,1,0:T(8,128)(2,1)S(1)}, u32[]{:S(2)}, u32[]{:S(2)}) async-start(bf16[16,16,128]{2,1,0:T(8,128)(2,1)} %broadcast_in_dim.18), calls=%async_computation.6 | async-start | bytes 131072 | tf_op jit(solution)/shard_map/all_to_all | solution.py:27
  216.1 55.0 %collective-permute-start.7 = (bf16[736,128]{0,1:T(8,128)(2,1)}, bf16[736,128]{0,1:T(8,128)(2,1)S(1)}, u32[]{:S(2)}, u32[]{:S(2)}) collective-permute-start(bf16[736,128]{0,1:T(8,128)(2,1)} %fusion.20), channel_id=1, source_target_pairs={{0,256},{64,320},{128,384},{192,448},{256,0},{320,64},{384,128},{4... | collective-permute-start | bytes 565256 | tf_op jit(solution)/shard_map/ppermute | solution.py:19
  226.6 40.2 %copy-start.8 = (f32[8,16]{1,0:T(8,128)S(1)}, f32[8,16]{1,0:T(8,128)}, u32[]{:S(2)}) copy-start(f32[8,16]{1,0:T(8,128)} %get-tuple-element.61) | copy-start | bytes 1540
  226.7 40.3 %copy-start.6 = (f32[8,16]{1,0:T(8,128)S(1)}, f32[8,16]{1,0:T(8,128)}, u32[]{:S(2)}) copy-start(f32[8,16]{1,0:T(8,128)} %get-tuple-element.55) | copy-start | bytes 1540
  226.7 40.3 %copy-start.7 = (f32[8,16]{1,0:T(8,128)S(1)}, f32[8,16]{1,0:T(8,128)}, u32[]{:S(2)}) copy-start(f32[8,16]{1,0:T(8,128)} %get-tuple-element.60) | copy-start | bytes 1540
  226.7 44.4 %copy-start.4 = (f32[736]{0:T(1024)S(1)}, f32[736]{0:T(1024)}, u32[]{:S(2)}) copy-start(f32[736]{0:T(1024)} %get-tuple-element.9) | copy-start | bytes 8836
  226.7 44.4 %copy-start.5 = (f32[736]{0:T(1024)S(1)}, f32[736]{0:T(1024)}, u32[]{:S(2)}) copy-start(f32[736]{0:T(1024)} %get-tuple-element.10) | copy-start | bytes 8836
  226.8 3.4 %collective-permute-start.5 = (bf16[64,16,128]{2,1,0:T(8,128)(2,1)S(1)}, bf16[64,16,128]{2,1,0:T(8,128)(2,1)S(1)}, u32[]{:S(2)}, u32[]{:S(2)}) collective-permute-start(bf16[64,16,128]{2,1,0:T(8,128)(2,1)S(1)} %fusion.19), channel_id=1, source_target_pairs={{0,4},{4,0},{1,5},{5,1},{2,6},{6,2},{3,7},{7,3},{8,12},{12,8},{9,1... | collective-permute-start | bytes 786440 | tf_op jit(solution)/shard_map/ppermute | solution.py:23
  231.0 21.1 %all-to-all-start.7 = ((bf16[64,16,128]{2,1,0:T(8,128)(2,1)}), bf16[64,16,128]{2,1,0:T(8,128)(2,1)S(1)}, u32[]{:S(2)}, u32[]{:S(2)}) async-start(bf16[64,16,128]{2,1,0:T(8,128)(2,1)} %fusion.14), calls=%async_computation.7 | async-start | bytes 524288 | tf_op jit(solution)/shard_map/all_to_all | solution.py:61
  252.9 13.8 %all-to-all-start.8 = ((bf16[16,16,128]{2,1,0:T(8,128)(2,1)}), bf16[16,16,128]{2,1,0:T(8,128)(2,1)S(1)}, u32[]{:S(2)}, u32[]{:S(2)}) async-start(bf16[16,16,128]{2,1,0:T(8,128)(2,1)} %broadcast_in_dim.19), calls=%async_computation.8 | async-start | bytes 131072 | tf_op jit(solution)/shard_map/all_to_all | solution.py:27
  267.7 10.4 %all-to-all-start.9 = ((bf16[8,32,128]{2,1,0:T(8,128)(2,1)}), bf16[8,32,128]{2,1,0:T(8,128)(2,1)S(1)}, u32[]{:S(2)}, u32[]{:S(2)}) async-start(bf16[8,32,128]{2,1,0:T(8,128)(2,1)} %pad_maximum_fusion.4), calls=%async_computation.9 | async-start | bytes 131072 | tf_op jit(solution)/shard_map/all_to_all | solution.py:142
  (7 other events, 140.3 us)
Sparse Core Ops, SparseCore 0:
  10.5 85.0 all-gather.2
  97.7 72.1 all-gather.4

commit v2 on v1

v2 whole, which is shorter than its diff:
```python
import jax
import jax.numpy as jnp
from jax import lax
from jax.experimental import pallas as pl
from jax.experimental.pallas import tpu as pltpu
from jax.sharding import Mesh, PartitionSpec as P

BF = jnp.bfloat16
F32 = jnp.float32
ROWS = ("y", "z", "c")
DOWN = (((0,), (0,)), ((), ()))


def grid_of(rows):
    z = 8 if rows >= 128 else 4
    return rows // (2 * z), z, 2


def swap_y(v, bit, count):
    return lax.ppermute(v, "y", [(i, i ^ bit) for i in range(count)])


def swap_core(v):
    return lax.ppermute(v, "c", [(0, 1), (1, 0)])


def everyone(block, axes, count):
    return lax.all_to_all(jnp.broadcast_to(block[None], (count,) + block.shape), axes, 0, 0)


def two_parts(v):
    high = v.astype(BF)
    return high, (v - high.astype(F32)).astype(BF)


def total(v):
    return jnp.sum(v.astype(F32), axis=0)


def dot(a, b):
    return jnp.dot(a, b, preferred_element_type=F32)


def down(a, b):
    return lax.dot_general(a, b, DOWN, preferred_element_type=F32)


LO, LI, RO, RI, PIV = 0, 2, 4, 6, 8


def column(table, k):
    return table[:, k:k + 1]


def elementwise(body, outs, *args):
    size = sum(a.size * a.dtype.itemsize for a in args)
    return pl.pallas_call(
        body,
        out_shape=outs,
        cost_estimate=pl.CostEstimate(flops=0, bytes_accessed=2 * size, transcendentals=0),
    )(*args)


def left_send(rhs, table, send):
    send[...] = (column(table, LO + 1) * rhs[...].astype(F32)).astype(BF)


def left_middle(rhs, got, table, value, send):
    v = column(table, LO) * rhs[...].astype(F32) + got[...].astype(F32)
    value[...] = column(table, LI) * v
    send[...] = (column(table, LI + 1) * v).astype(BF)


def right_middle(scaled, got, table, value, send):
    v = column(table, RI) * scaled[...] + column(table, RI + 1) * got[...].astype(F32)
    value[...] = column(table, RO) * v
    send[...] = v.astype(BF)


def right_end(value, got, table, out):
    out[...] = value[...] + column(table, RO + 1) * got[...].astype(F32)


def first_update(panel, solved, value, got, base):
    base[...] = value[...] + got[...].astype(F32) - dot(panel[...], solved[...])


def split_term(core, acc, mine, away):
    ny, half, width = mine.shape
    for y in range(ny):
        for h in range(2):
            start = (2 * y + h) * half
            block = acc[:, start:start + half].T

            @pl.when(core[0] == h)
            def _():
                mine[y] = block

            @pl.when(core[0] != h)
            def _():
                away[y] = block.astype(BF)


def middle(low, tile, core, panel, solved, base, table, scaled, rounded, mine, away, acc):
    step = pl.program_id(0)
    v = (base[...] - dot(panel[...], solved[...])) / column(table, PIV)
    scaled[...] = v
    row = lax.broadcasted_iota(jnp.int32, v.shape, 0) + step * tile
    kept = jnp.where(row >= low, v, 0.0)
    rounded[...] = kept.astype(BF)
    add = dot(kept.T.astype(BF), panel[...])

    @pl.when(step == 0)
    def _():
        acc[...] = add

    @pl.when(step > 0)
    def _():
        acc[...] += add

    @pl.when(step == pl.num_programs(0) - 1)
    def _():
        split_term(core, acc, mine, away)


def first_term(core, panel, rounded, mine, away, acc):
    step = pl.program_id(0)
    add = dot(rounded[...].astype(F32).T.astype(BF), panel[...])

    @pl.when(step == 0)
    def _():
        acc[...] = add

    @pl.when(step > 0)
    def _():
        acc[...] += add

    @pl.when(step == pl.num_programs(0) - 1)
    def _():
        split_term(core, acc, mine, away)


def start_bands(ny, outer, inner, coefs, arrived, part, x1):
    rb, width = arrived.shape[2:]
    n = 2 * ny

    def fly(b, i, level, v):
        bit = (outer if level == 0 else inner) * 2
        own = level * 4 + b
        j = i ^ bit
        a = coefs[i][:, own:own + 1] * v[i]
        return a + coefs[j][:, own + 2:own + 3] * v[j]

    both = []
    for b in range(2):
        raw = [arrived[i, 3 + b].astype(F32) for i in range(n)]
        first = [fly(b, i, 0, raw) for i in range(n)]
        both.append([fly(b, i, 1, first) for i in range(n)])
    tile = jnp.concatenate([arrived[i, 0] for i in range(n)], axis=0)
    x0 = jnp.concatenate(both[0], axis=0).astype(BF)
    part[...] = down(tile, x0).astype(BF)
    for i in range(n):
        x1[i] = both[1][i]


def shards(rhs, left, right, pivots, panels, inverse):
    ny, nz = lax.axis_size("y"), lax.axis_size("z")
    rb, band = inverse.shape[1], inverse.shape[2]
    rows, width = rhs.shape
    half = nz * rb
    low = 2 * rb
    core, y, z = lax.axis_index("c"), lax.axis_index("y"), lax.axis_index("z")
    outer, inner = ny // 2, ny // 4
    chunk = ny * 2 * rb
    first_core = core == 0
    once = jnp.where(first_core, 1.0, 0.0).astype(F32)
    core_ref = core.astype(jnp.int32)[None]

    def both_halves(mine):
        other = swap_core(mine)
        even = jnp.where(first_core, mine, other)
        odd = jnp.where(first_core, other, mine)
        return jnp.stack([even, odd], axis=1).reshape(band, width)

    def reduce_y_everywhere_z(mine):
        v = total(lax.all_to_all(mine.astype(BF), "y", 0, 0))
        return total(everyone(v.astype(BF), "z", nz))

    gathered0 = lax.all_gather(panels[0], "x", axis=0, tiled=True)
    gathered1 = lax.all_gather(panels[1], "x", axis=0, tiled=True)

    table = jnp.concatenate([left.reshape(4, rows), right.reshape(4, rows), pivots[None]], axis=0)
    table = jnp.pad(table, ((0, 7), (0, 0))).T

    few = table[:low].reshape(2, rb, 16).transpose(1, 2, 0).reshape(rb, 32)
    few = jnp.concatenate(two_parts(few), axis=1)
    few = jnp.pad(few, ((0, 0), (0, half - few.shape[1])))
    blocks = inverse.reshape(2, rb, ny, 2, half)
    wide0 = blocks[0].transpose(1, 2, 0, 3)[:, :, None]
    wide1 = jnp.broadcast_to(blocks[1].transpose(1, 2, 0, 3)[:, None], (ny, 2, 2, rb, half))
    shared = jnp.concatenate([rhs[:low].reshape(2, rb, half), few[None]], axis=0)
    shared = jnp.broadcast_to(shared[None, None], (ny, 2, 3, rb, half))
    message = jnp.concatenate([wide0, wide1, shared], axis=2).reshape(ny * 2, 6, rb, half)
    arrived = lax.all_to_all(message, ("y", "c"), 0, 0)

    shape = jax.ShapeDtypeStruct
    whole, sent = shape((rows, width), F32), shape((rows, width), BF)
    send = elementwise(left_send, sent, rhs, table)
    value, send = elementwise(
        left_middle, (whole, sent), rhs, swap_y(send, outer, ny), table)
    crossed = swap_y(send, inner, ny)

    small = arrived[:, 5].astype(F32)
    small = small[:, :, :32] + small[:, :, 32:64]
    tile0 = arrived[:, 0].reshape(chunk, half)
    tile1 = jnp.concatenate(
        [arrived[:, 1].reshape(chunk, half), arrived[:, 2].reshape(chunk, half)], axis=1)

    part, x1 = pl.pallas_call(
        lambda *refs: start_bands(ny, outer, inner, *refs),
        out_shape=(shape((half, width), BF), shape((ny * 2, rb, width), F32)),
    )(small, arrived)
    x1 = once * lax.dynamic_slice_in_dim(x1, 2 * y, 2, 0).reshape(low, width)

    few = lax.dynamic_slice_in_dim(arrived[:, 5], 2 * y, 2, 0)
    few = jnp.concatenate(
        [few[c, :, o + 2 * PIV:o + 2 * PIV + 2] for c in (0, 1) for o in (0, 32)], axis=1)
    few = jnp.pad(few, ((0, 0), (0, width - few.shape[1])))
    met = everyone(jnp.concatenate([part, few], axis=0), "z", nz)
    half0 = total(met[:, :half])
    few = lax.dynamic_slice_in_dim(met[:, half:], core * (nz // 2), nz // 2, 0).astype(F32)
    own_pivots = [
        jnp.stack([few[:, :, 4 * c + b] + few[:, :, 4 * c + 2 + b] for c in (0, 1)], axis=1)
        .reshape(half, 1) for b in (0, 1)]
    mine0 = everyone(half0.astype(BF), "y", ny)
    s0 = both_halves(mine0)

    cross = gathered0[rb:low].reshape(rb, ny, 2, half)
    cross_mine = jnp.where(first_core, cross[:, :, 0], cross[:, :, 1]).reshape(rb, ny * half)
    cross_away = jnp.where(first_core, cross[:, :, 1], cross[:, :, 0]).reshape(rb, ny * half)
    cross_got = swap_core(cross_away)
    cross = jnp.concatenate([
        jnp.where(first_core, cross_mine, cross_got),
        jnp.where(first_core, cross_got, cross_mine)], axis=0)
    x1 = x1 - dot(cross, mine0.reshape(ny * half, width))
    x1 = everyone(x1.astype(BF), "y", ny).reshape(chunk, width)
    part = down(tile1, x1).reshape(2, half, width)
    away = swap_core(jnp.where(first_core, part[1], part[0]).astype(BF)).astype(F32)
    part = jnp.where(first_core, part[0], part[1]) + away
    half1 = total(everyone(part.astype(BF), "z", nz))

    tile = rows // 3
    steps = rows // tile
    panel_spec = pl.BlockSpec((tile, band), lambda i: (i, 0))
    solved_spec = pl.BlockSpec((band, width), lambda i: (0, 0))
    row_spec = pl.BlockSpec((tile, width), lambda i: (i, 0))
    table_spec = pl.BlockSpec((tile, 16), lambda i: (i, 0))
    core_spec = pl.BlockSpec(memory_space=pltpu.SMEM)
    half_spec = pl.BlockSpec((ny, half, width), lambda i: (0, 0, 0))
    params = pltpu.CompilerParams(vmem_limit_bytes=40 * 2 ** 20)
    cost = pl.CostEstimate(
        flops=2 * rows * band * width, bytes_accessed=2 * rows * band, transcendentals=0)
    base = pl.pallas_call(
        first_update, out_shape=whole, grid=(steps,),
        in_specs=[panel_spec, solved_spec, row_spec, row_spec], out_specs=row_spec,
        compiler_params=params, cost_estimate=cost,
    )(gathered0, s0, value, crossed)

    s1 = both_halves(everyone(half1.astype(BF), "y", ny))
    halves = (shape((ny, half, width), F32), shape((ny, half, width), BF))
    scaled, rounded, mine1, away1 = pl.pallas_call(
        lambda *refs: middle(low, tile, *refs),
        out_shape=(whole, sent) + halves, grid=(steps,),
        in_specs=[core_spec, panel_spec, solved_spec, row_spec, table_spec],
        out_specs=(row_spec, row_spec, half_spec, half_spec),
        scratch_shapes=[pltpu.VMEM((width, band), F32)],
        compiler_params=params, cost_estimate=cost,
    )(core_ref, gathered1, s1, base, table)
    target1 = half1 / own_pivots[1] - reduce_y_everywhere_z(
        mine1 + swap_core(away1).astype(F32))

    mine0, away0 = pl.pallas_call(
        first_term, out_shape=halves, grid=(steps,),
        in_specs=[core_spec, panel_spec, row_spec], out_specs=(half_spec, half_spec),
        scratch_shapes=[pltpu.VMEM((width, band), F32)],
        compiler_params=params, cost_estimate=cost,
    )(core_ref, gathered0, rounded)
    mine0 = mine0 + swap_core(away0).astype(F32)

    value, send = elementwise(
        right_middle, (whole, sent), scaled, swap_y(rounded, inner, ny), table)
    out = elementwise(right_end, whole, value, swap_y(send, outer, ny), table)

    t1 = target1.astype(BF)
    other = swap_core(t1)
    t1 = jnp.concatenate([
        jnp.where(first_core, t1, other), jnp.where(first_core, other, t1)], axis=0)
    back1 = dot(tile1, t1)
    solved1 = total(lax.all_to_all(back1.astype(BF).reshape(ny, low, width), "y", 0, 0))
    mine0 = mine0 + down(cross, solved1.astype(BF)).reshape(ny, half, width)
    target0 = half0 / own_pivots[0] - reduce_y_everywhere_z(mine0)
    back0 = dot(tile0, target0.astype(BF))

    def pair(v, bit):
        return jnp.concatenate([v[i ^ bit][None] for i in range(ny)], axis=0)

    def finished(v, b):
        v = v.reshape(ny, 2, rb, width)
        k = small.reshape(ny, 2, rb, 32)
        at = lambda column: k[:, :, :, 2 * column + b, None]
        v = at(RI) * v + at(RI + 1) * pair(v, inner)
        return at(RO) * v + at(RO + 1) * pair(v, outer)

    last = jnp.stack([finished(back0, 0), finished(once * back1, 1)], axis=2)
    last = last.astype(BF).reshape(ny * 2, low, width)
    head = total(lax.all_to_all(last, ("y", "c"), 0, 0))
    return lax.dynamic_update_slice(out, head, (0, 0))


def solution(mesh):
    rows, cols = mesh.devices.shape
    grid = Mesh(mesh.devices.reshape(grid_of(rows) + (cols,)), ("y", "z", "c", "x"))
    in_specs = (
        P(ROWS, "x"),
        P(None, None, ROWS),
        P(None, None, ROWS),
        P(ROWS),
        P(None, ROWS + ("x",), None),
        P(None, ROWS, None),
    )
    return jax.shard_map(
        shards, mesh=grid, in_specs=in_specs, out_specs=P(ROWS, "x"), check_vma=False)
```

time: 287 us -> 310 us (1.080); the launches traced: 286 us -> 306 us
  blocking collectives: 75.1 us -> 24.6 us
  starting transfers between devices: 73.7 us -> 100 us
  Pallas kernels: 0 us -> 20 us
  local copies, waits for them, and re-layouts: 14.5 us -> 34.2 us
  other arithmetic: 6.02 us -> 12.4 us
  matrix products: 10.7 us -> 5.2 us
    all_to_all x3 -> x0, blocking collectives: 57.7 us -> none  [the longest x2 40.9 us: reduce_zc(): lax.all_to_all(part.astype(BF).reshape(nzc, rb, width), ('z', 'c'), 0, 0)]
    all_gather x2, waiting for transfers between devices: 44.6 us -> 0.02 us  [the longest x1 0.02 us: shards(): gathered0 = lax.all_gather(panels[0], 'x', axis=0, tiled=True)]
    pallas_call x0 -> x8, Pallas kernels: none -> 20 us  [the longest x4 8.73 us: elementwise(): pl.pallas_call(body, out_shape=outs, cost_estimate=pl.CostEstimate(flops=...]
    ppermute x4, waiting for transfers between devices: 1.05 us -> 19.8 us  [swap_y(): return lax.ppermute(v, 'y', [(i, i ^ bit) for i in range(count)])]
    unnamed x44 -> x116, local copies, waits for them, and re-layouts: 2.7 us -> 19.3 us
    all_to_all x3 -> x5, waiting for transfers between devices: 26 us -> 41.1 us  [the longest x2 20.2 us: reduce_y_everywhere_z(): v = total(lax.all_to_all(mine.astype(BF), 'y', 0, 0))]
    all_to_all x3 -> x5, waiting for transfers between devices: 17.3 us -> 30.5 us  [everyone(): lax.all_to_all(jnp.broadcast_to(block[None], (count,) + block.shape), axe...]
    all_to_all x3 -> x5, starting transfers between devices: 17.4 us -> 27.4 us  [everyone(): lax.all_to_all(jnp.broadcast_to(block[None], (count,) + block.shape), axe...]
  transfers between devices with their start and end apart: 16 -> 23, of which waited for: 12 -> 13; matrix products, arithmetic and copies ran while one was open for 9% -> 12% of each run, Pallas kernels for 0% -> 5%
where the time goes in v2:
time: 310 us; the launch traced here: 306 us
  starting transfers between devices  100 us (32%)
  waiting for transfers between devices  94.2 us (30%)
  local copies, waits for them, and re-layouts  34.2 us (11%)
  blocking collectives  24.6 us (8%)
  Pallas kernels  20 us (6%)
  between operations  14.5 us (5%)
  other arithmetic  12.4 us (4%)
  matrix products  5.2 us (2%)
    all_to_all x5, waiting for transfers between devices, everyone(): lax.all_to_all(jnp.broadcast_to(block[None], (count,) + block.shape), axe...  30.5 us
    all_to_all x5, starting transfers between devices, everyone(): lax.all_to_all(jnp.broadcast_to(block[None], (count,) + block.shape), axe...  27.4 us
    all_to_all x2, blocking collectives, everyone(): lax.all_to_all(jnp.broadcast_to(block[None], (count,) + block.shape), axe...  24.6 us
    ppermute x4, starting transfers between devices, swap_y(): return lax.ppermute(v, 'y', [(i, i ^ bit) for i in range(count)])  23.2 us
    all_to_all x2, waiting for transfers between devices, reduce_y_everywhere_z(): v = total(lax.all_to_all(mine.astype(BF), 'y', 0, 0))  20.2 us
    ppermute x4, waiting for transfers between devices, swap_y(): return lax.ppermute(v, 'y', [(i, i ^ bit) for i in range(count)])  19.8 us
    ppermute x7, starting transfers between devices, swap_core(): return lax.ppermute(v, 'c', [(0, 1), (1, 0)])  19.4 us
    unnamed x116, local copies, waits for them, and re-layouts  19.3 us
  transfers between devices with their start and end apart: 23, of which 13 were waited for; matrix products, arithmetic and copies ran while one was open for 12% of the time, Pallas kernels for 5%

profile of v2, /device:TPU:1, one launch (start us, length us, event | category | flops | bytes accessed | tf_op | source)
XLA Modules:
  0.0 305.7 jit_solution(8439673784271769642)
XLA Ops:
  11.1 10.2 %all-to-all-start = ((bf16[16,6,16,128]{3,2,1,0:T(8,128)(2,1)}), bf16[16,6,16,128]{3,2,1,0:T(8,128)(2,1)S(1)}, u32[]{:S(2)}, u32[]{:S(2)}) async-start(bf16[16,6,16,128]{3,2,1,0:T(8,128)(2,1)} %pad_maximum_fusion.2), calls=%async_computation | async-start | bytes 786432 | tf_op jit(solution)/shard_map/all_to_all | solution.py:204
  22.0 13.8 %all-to-all-done.refs_1_ = bf16[16,6,16,128]{3,2,1,0:T(8,128)(2,1)S(1)} async-done(((bf16[16,6,16,128]{3,2,1,0:T(8,128)(2,1)}), bf16[16,6,16,128]{3,2,1,0:T(8,128)(2,1)S(1)}, u32[]{:S(2)}, u32[]{:S(2)}) %all-to-all-start) | async-done | bytes 393248 | tf_op jit(solution)/shard_map/all_to_all | solution.py:204
  41.2 8.4 %all-to-all-start.1 = ((bf16[8,144,128]{2,1,0:T(8,128)(2,1)}), bf16[8,144,128]{2,1,0:T(8,128)(2,1)S(1)}, u32[]{:S(2)}, u32[]{:S(2)}) async-start(bf16[8,144,128]{2,1,0:T(8,128)(2,1)} %broadcast_in_dim.29), calls=%async_computation.1 | async-start | bytes 589824 | tf_op jit(solution)/shard_map/all_to_all | solution.py:28
  49.6 13.1 %all-to-all-done.1 = bf16[8,144,128]{2,1,0:T(8,128)(2,1)S(1)} async-done(((bf16[8,144,128]{2,1,0:T(8,128)(2,1)}), bf16[8,144,128]{2,1,0:T(8,128)(2,1)S(1)}, u32[]{:S(2)}, u32[]{:S(2)}) %all-to-all-start.1) | async-done | bytes 294944 | tf_op jit(solution)/shard_map/all_to_all | solution.py:28
  63.8 4.1 %all-to-all-start.2 = ((bf16[8,128,128]{2,1,0:T(8,128)(2,1)}), bf16[8,128,128]{2,1,0:T(8,128)(2,1)}, u32[]{:S(2)}, u32[]{:S(2)}) async-start(bf16[8,128,128]{2,1,0:T(8,128)(2,1)} %broadcast_in_dim.30), calls=%async_computation.2 | async-start | bytes 524288 | tf_op jit(solution)/shard_map/all_to_all | solution.py:28
  72.1 8.1 %all-to-all-done.2 = bf16[8,128,128]{2,1,0:T(8,128)(2,1)} async-done(((bf16[8,128,128]{2,1,0:T(8,128)(2,1)}), bf16[8,128,128]{2,1,0:T(8,128)(2,1)}, u32[]{:S(2)}, u32[]{:S(2)}) %all-to-all-start.2) | async-done | bytes 262176 | tf_op jit(solution)/shard_map/all_to_all | solution.py:28
  81.3 9.6 %all_to_all.60 = bf16[8,32,128]{2,1,0:T(8,128)(2,1)S(1)} all-to-all(bf16[8,32,128]{2,1,0:T(8,128)(2,1)S(1)} %broadcast_in_dim.31), channel_id=1, replica_groups=mesh['y'=8,'z'=8,'c'=2,'x'=4] {'y'}, dimensions={0} | all-to-all | bytes 131072 | tf_op jit(solution)/shard_map/all_to_all | solution.py:28
  95.7 15.0 %all_to_all.61 = bf16[8,128,128]{2,1,0:T(8,128)(2,1)S(1)} all-to-all(bf16[8,128,128]{2,1,0:T(8,128)(2,1)S(1)} %broadcast_in_dim.32), channel_id=1, replica_groups=mesh['y'=8,'z'=8,'c'=2,'x'=4] {'z'}, dimensions={0} | all-to-all | bytes 524288 | tf_op jit(solution)/shard_map/all_to_all | solution.py:28
  112.2 4.1 %all-to-all-start.5 = ((bf16[8,128,128]{2,1,0:T(8,128)(2,1)}), bf16[8,128,128]{2,1,0:T(8,128)(2,1)}, u32[]{:S(2)}, u32[]{:S(2)}) async-start(bf16[8,128,128]{2,1,0:T(8,128)(2,1)} %broadcast_in_dim.33), calls=%async_computation.5 | async-start | bytes 524288 | tf_op jit(solution)/shard_map/all_to_all | solution.py:28
  120.6 7.4 %collective-permute-start.4 = (bf16[768,128]{1,0:T(8,128)(2,1)}, bf16[768,128]{1,0:T(8,128)(2,1)S(1)}, u32[]{:S(2)}, u32[]{:S(2)}) collective-permute-start(bf16[768,128]{1,0:T(8,128)(2,1)} %shard_map.65), channel_id=1, source_target_pairs={{0,256},{64,320},{128,384},{192,448},{256,0},{320,64},{384,128},{4... | collective-permute-start | bytes 589832 | tf_op jit(solution)/shard_map/ppermute | solution.py:20
  128.0 7.2 %collective-permute-done.4.got = bf16[768,128]{1,0:T(8,128)(2,1)S(1)} collective-permute-done((bf16[768,128]{1,0:T(8,128)(2,1)}, bf16[768,128]{1,0:T(8,128)(2,1)S(1)}, u32[]{:S(2)}, u32[]{:S(2)}) %collective-permute-start.4) | collective-permute-done | bytes 196640 | tf_op jit(solution)/shard_map/ppermute | solution.py:20
  138.2 6.6 %collective-permute-start.5 = (bf16[768,128]{1,0:T(8,128)(2,1)}, bf16[768,128]{1,0:T(8,128)(2,1)S(1)}, u32[]{:S(2)}, u32[]{:S(2)}) collective-permute-start(bf16[768,128]{1,0:T(8,128)(2,1)} %get-tuple-element.20), channel_id=1, source_target_pairs={{0,128},{64,192},{128,0},{192,64},{256,384},{320,448},{384,256},{4... | collective-permute-start | bytes 589832 | tf_op jit(solution)/shard_map/ppermute | solution.py:20
  148.9 5.7 %collective-permute-done.5.got = bf16[768,128]{1,0:T(8,128)(2,1)S(1)} collective-permute-done((bf16[768,128]{1,0:T(8,128)(2,1)}, bf16[768,128]{1,0:T(8,128)(2,1)S(1)}, u32[]{:S(2)}, u32[]{:S(2)}) %collective-permute-start.5) | collective-permute-done | bytes 196640 | tf_op jit(solution)/shard_map/ppermute | solution.py:20
  164.0 4.1 %shard_map.68 = (f32[768,128]{1,0:T(8,128)S(1)}, bf16[768,128]{1,0:T(8,128)(2,1)S(1)}, f32[8,128,128]{2,1,0:T(8,128)S(1)}, bf16[8,128,128]{2,1,0:T(8,128)(2,1)S(1)}) custom-call(s32[1]{0:T(128)} %bitcast.refs_0_.core, bf16[768,2048]{1,0:T(8,128)(2,1)S(1)} %bitcast.177, bf16[2048,128]{1,0:T(8,128)(2,1)S(1)} %bitcast.178, f32[768,128]{1,0:T(8,128)S(1)} %copy-done.6, ...), custom_call_target="tpu_custom_call" | custom-call | flops 402653184 | bytes 3145728 | tf_op jit(solution)/shard_map/pallas_call | solution.py:271
  174.0 4.7 %all-to-all-start.6 = ((bf16[8,128,128]{2,1,0:T(8,128)(2,1)}), bf16[8,128,128]{2,1,0:T(8,128)(2,1)}, u32[]{:S(2)}, u32[]{:S(2)}) async-start(bf16[8,128,128]{2,1,0:T(8,128)(2,1)} %add_convert_fusion.1), calls=%async_computation.6 | async-start | bytes 524288 | tf_op jit(solution)/shard_map/all_to_all | solution.py:186
  178.8 11.2 %all-to-all-done.6 = bf16[8,128,128]{2,1,0:T(8,128)(2,1)} async-done(((bf16[8,128,128]{2,1,0:T(8,128)(2,1)}), bf16[8,128,128]{2,1,0:T(8,128)(2,1)}, u32[]{:S(2)}, u32[]{:S(2)}) %all-to-all-start.6) | async-done | bytes 262176 | tf_op jit(solution)/shard_map/all_to_all | solution.py:186
  191.7 4.0 %all-to-all-start.7 = ((bf16[8,128,128]{2,1,0:T(8,128)(2,1)}), bf16[8,128,128]{2,1,0:T(8,128)(2,1)}, u32[]{:S(2)}, u32[]{:S(2)}) async-start(bf16[8,128,128]{2,1,0:T(8,128)(2,1)} %broadcast_in_dim.34), calls=%async_computation.7 | async-start | bytes 524288 | tf_op jit(solution)/shard_map/all_to_all | solution.py:28
  230.2 7.1 %all-to-all-done.8 = bf16[8,32,128]{2,1,0:T(8,128)(2,1)S(1)} async-done(((bf16[8,32,128]{2,1,0:T(8,128)(2,1)}), bf16[8,32,128]{2,1,0:T(8,128)(2,1)S(1)}, u32[]{:S(2)}, u32[]{:S(2)}) %all-to-all-start.8) | async-done | bytes 65568 | tf_op jit(solution)/shard_map/all_to_all | solution.py:299
  242.8 9.0 %all-to-all-done.9 = bf16[8,128,128]{2,1,0:T(8,128)(2,1)S(1)} async-done(((bf16[8,128,128]{2,1,0:T(8,128)(2,1)}), bf16[8,128,128]{2,1,0:T(8,128)(2,1)S(1)}, u32[]{:S(2)}, u32[]{:S(2)}) %all-to-all-start.9) | async-done | bytes 262176 | tf_op jit(solution)/shard_map/all_to_all | solution.py:186
  252.6 6.8 %all-to-all-start.10 = ((bf16[8,128,128]{2,1,0:T(8,128)(2,1)}), bf16[8,128,128]{2,1,0:T(8,128)(2,1)S(1)}, u32[]{:S(2)}, u32[]{:S(2)}) async-start(bf16[8,128,128]{2,1,0:T(8,128)(2,1)} %broadcast_in_dim.35), calls=%async_computation.10 | async-start | bytes 524288 | tf_op jit(solution)/shard_map/all_to_all | solution.py:28
  259.6 9.3 %all-to-all-done.10 = bf16[8,128,128]{2,1,0:T(8,128)(2,1)S(1)} async-done(((bf16[8,128,128]{2,1,0:T(8,128)(2,1)}), bf16[8,128,128]{2,1,0:T(8,128)(2,1)S(1)}, u32[]{:S(2)}, u32[]{:S(2)}) %all-to-all-start.10) | async-done | bytes 262176 | tf_op jit(solution)/shard_map/all_to_all | solution.py:28
  270.7 8.2 %all-to-all-start.11 = ((bf16[16,32,128]{2,1,0:T(8,128)(2,1)}), bf16[16,32,128]{2,1,0:T(8,128)(2,1)S(1)}, u32[]{:S(2)}, u32[]{:S(2)}) async-start(bf16[16,32,128]{2,1,0:T(8,128)(2,1)} %bitcast.106), calls=%async_computation.11 | async-start | bytes 262144 | tf_op jit(solution)/shard_map/all_to_all | solution.py:316
  281.3 7.2 %collective-permute-start.7 = (bf16[768,128]{1,0:T(8,128)(2,1)}, bf16[768,128]{1,0:T(8,128)(2,1)S(1)}, u32[]{:S(2)}, u32[]{:S(2)}) collective-permute-start(bf16[768,128]{1,0:T(8,128)(2,1)} %get-tuple-element.24), channel_id=1, source_target_pairs={{0,256},{64,320},{128,384},{192,448},{256,0},{320,64},{384,128},{4... | collective-permute-start | bytes 589832 | tf_op jit(solution)/shard_map/ppermute | solution.py:20
  288.5 6.9 %collective-permute-done.7.got = bf16[768,128]{1,0:T(8,128)(2,1)S(1)} collective-permute-done((bf16[768,128]{1,0:T(8,128)(2,1)}, bf16[768,128]{1,0:T(8,128)(2,1)S(1)}, u32[]{:S(2)}, u32[]{:S(2)}) %collective-permute-start.7) | collective-permute-done | bytes 196640 | tf_op jit(solution)/shard_map/ppermute | solution.py:20
  (251 shorter events, 99.2 us)
Async XLA Ops:
  6.5 61.3 %all-gather.7.cloned.1.call-start = ((), (), s32[]{:S(2)}) async-start(), calls=%async_computation.13 | async-start | bytes 3932160 | tf_op jit(solution)/shard_map/all_gather | solution.py:189
  11.1 24.8 %all-to-all-start = ((bf16[16,6,16,128]{3,2,1,0:T(8,128)(2,1)}), bf16[16,6,16,128]{3,2,1,0:T(8,128)(2,1)S(1)}, u32[]{:S(2)}, u32[]{:S(2)}) async-start(bf16[16,6,16,128]{3,2,1,0:T(8,128)(2,1)} %pad_maximum_fusion.2), calls=%async_computation | async-start | bytes 786432 | tf_op jit(solution)/shard_map/all_to_all | solution.py:204
  21.3 138.8 %all-gather.5.cloned.1.call-start = ((), (), s32[]{:S(2)}) async-start(), calls=%async_computation.12 | async-start | bytes 3932160 | tf_op jit(solution)/shard_map/all_gather | solution.py:190
  41.2 21.5 %all-to-all-start.1 = ((bf16[8,144,128]{2,1,0:T(8,128)(2,1)}), bf16[8,144,128]{2,1,0:T(8,128)(2,1)S(1)}, u32[]{:S(2)}, u32[]{:S(2)}) async-start(bf16[8,144,128]{2,1,0:T(8,128)(2,1)} %broadcast_in_dim.29), calls=%async_computation.1 | async-start | bytes 589824 | tf_op jit(solution)/shard_map/all_to_all | solution.py:28
  63.8 16.4 %all-to-all-start.2 = ((bf16[8,128,128]{2,1,0:T(8,128)(2,1)}), bf16[8,128,128]{2,1,0:T(8,128)(2,1)}, u32[]{:S(2)}, u32[]{:S(2)}) async-start(bf16[8,128,128]{2,1,0:T(8,128)(2,1)} %broadcast_in_dim.30), calls=%async_computation.2 | async-start | bytes 524288 | tf_op jit(solution)/shard_map/all_to_all | solution.py:28
  68.9 3.1 %collective-permute-start = (bf16[16,1024]{1,0:T(8,128)(2,1)S(1)}, bf16[16,1024]{1,0:T(8,128)(2,1)S(1)}, u32[]{:S(2)}, u32[]{:S(2)}) collective-permute-start(bf16[16,1024]{1,0:T(8,128)(2,1)S(1)} %bitcast.240), channel_id=1, source_target_pairs={{0,4},{4,0},{1,5},{5,1},{2,6},{6,2},{3,7},{7,3},{8,12},{12,8},{9,1... | collective-permute-start | bytes 98312 | tf_op jit(solution)/shard_map/ppermute | solution.py:24
  72.1 66.1 %copy-start.24 = (bf16[16,1024]{1,0:T(8,128)(2,1)}, bf16[16,1024]{1,0:T(8,128)(2,1)S(1)}, u32[]{:S(2)}) copy-start(bf16[16,1024]{1,0:T(8,128)(2,1)S(1)} %get-tuple-element.83) | copy-start | bytes 98308
  91.2 4.4 %collective-permute-start.1 = (bf16[128,128]{1,0:T(8,128)(2,1)S(1)}, bf16[128,128]{1,0:T(8,128)(2,1)S(1)}, u32[]{:S(2)}, u32[]{:S(2)}) collective-permute-start(bf16[128,128]{1,0:T(8,128)(2,1)S(1)} %select_convert_fusion), channel_id=1, source_target_pairs={{0,4},{4,0},{1,5},{5,1},{2,6},{6,2},{3,7},{7,3},{8,12},{12,8},{9,1... | collective-permute-start | bytes 98312 | tf_op jit(solution)/shard_map/ppermute | solution.py:24
  112.2 32.6 %all-to-all-start.5 = ((bf16[8,128,128]{2,1,0:T(8,128)(2,1)}), bf16[8,128,128]{2,1,0:T(8,128)(2,1)}, u32[]{:S(2)}, u32[]{:S(2)}) async-start(bf16[8,128,128]{2,1,0:T(8,128)(2,1)} %broadcast_in_dim.33), calls=%async_computation.5 | async-start | bytes 524288 | tf_op jit(solution)/shard_map/all_to_all | solution.py:28
  116.2 31.4 %collective-permute-start.3 = (bf16[8,128,128]{2,1,0:T(8,128)(2,1)}, bf16[8,128,128]{2,1,0:T(8,128)(2,1)}, u32[]{:S(2)}, u32[]{:S(2)}) collective-permute-start(bf16[8,128,128]{2,1,0:T(8,128)(2,1)} %all-to-all-done.2), channel_id=1, source_target_pairs={{0,4},{4,0},{1,5},{5,1},{2,6},{6,2},{3,7},{7,3},{8,12},{12,8},{9,1... | collective-permute-start | bytes 786440 | tf_op jit(solution)/shard_map/ppermute | solution.py:24
  120.6 14.6 %collective-permute-start.4 = (bf16[768,128]{1,0:T(8,128)(2,1)}, bf16[768,128]{1,0:T(8,128)(2,1)S(1)}, u32[]{:S(2)}, u32[]{:S(2)}) collective-permute-start(bf16[768,128]{1,0:T(8,128)(2,1)} %shard_map.65), channel_id=1, source_target_pairs={{0,256},{64,320},{128,384},{192,448},{256,0},{320,64},{384,128},{4... | collective-permute-start | bytes 589832 | tf_op jit(solution)/shard_map/ppermute | solution.py:20
  138.2 16.3 %collective-permute-start.5 = (bf16[768,128]{1,0:T(8,128)(2,1)}, bf16[768,128]{1,0:T(8,128)(2,1)S(1)}, u32[]{:S(2)}, u32[]{:S(2)}) collective-permute-start(bf16[768,128]{1,0:T(8,128)(2,1)} %get-tuple-element.20), channel_id=1, source_target_pairs={{0,128},{64,192},{128,0},{192,64},{256,384},{320,448},{384,256},{4... | collective-permute-start | bytes 589832 | tf_op jit(solution)/shard_map/ppermute | solution.py:20
  144.8 13.4 %collective-permute-start.2 = (bf16[8,128,128]{2,1,0:T(8,128)(2,1)}, bf16[8,128,128]{2,1,0:T(8,128)(2,1)S(1)}, u32[]{:S(2)}, u32[]{:S(2)}) collective-permute-start(bf16[8,128,128]{2,1,0:T(8,128)(2,1)} %all-to-all-done.5), channel_id=1, source_target_pairs={{0,4},{4,0},{1,5},{5,1},{2,6},{6,2},{3,7},{7,3},{8,12},{12,8},{9,1... | collective-permute-start | bytes 786440 | tf_op jit(solution)/shard_map/ppermute | solution.py:24
  169.6 3.7 %collective-permute-start.9 = (bf16[8,128,128]{2,1,0:T(8,128)(2,1)S(1)}, bf16[8,128,128]{2,1,0:T(8,128)(2,1)S(1)}, u32[]{:S(2)}, u32[]{:S(2)}) collective-permute-start(bf16[8,128,128]{2,1,0:T(8,128)(2,1)S(1)} %get-tuple-element.28), channel_id=1, source_target_pairs={{0,4},{4,0},{1,5},{5,1},{2,6},{6,2},{3,7},{7,3},{8,12},{12,8},{9,1... | collective-permute-start | bytes 786440 | tf_op jit(solution)/shard_map/ppermute | solution.py:24
  174.0 15.9 %all-to-all-start.6 = ((bf16[8,128,128]{2,1,0:T(8,128)(2,1)}), bf16[8,128,128]{2,1,0:T(8,128)(2,1)}, u32[]{:S(2)}, u32[]{:S(2)}) async-start(bf16[8,128,128]{2,1,0:T(8,128)(2,1)} %add_convert_fusion.1), calls=%async_computation.6 | async-start | bytes 524288 | tf_op jit(solution)/shard_map/all_to_all | solution.py:186
  191.7 20.5 %all-to-all-start.7 = ((bf16[8,128,128]{2,1,0:T(8,128)(2,1)}), bf16[8,128,128]{2,1,0:T(8,128)(2,1)}, u32[]{:S(2)}, u32[]{:S(2)}) async-start(bf16[8,128,128]{2,1,0:T(8,128)(2,1)} %broadcast_in_dim.34), calls=%async_computation.7 | async-start | bytes 524288 | tf_op jit(solution)/shard_map/all_to_all | solution.py:28
  210.3 68.6 %collective-permute-start.6 = (bf16[768,128]{1,0:T(8,128)(2,1)S(1)}, bf16[768,128]{1,0:T(8,128)(2,1)}, u32[]{:S(2)}, u32[]{:S(2)}) collective-permute-start(bf16[768,128]{1,0:T(8,128)(2,1)S(1)} %copy-done.13), channel_id=1, source_target_pairs={{0,128},{64,192},{128,0},{192,64},{256,384},{320,448},{384,256},{4... | collective-permute-start | bytes 589832 | tf_op jit(solution)/shard_map/ppermute | solution.py:20
  214.2 10.2 %collective-permute-start.10 = (bf16[128,128]{1,0:T(8,128)(2,1)S(1)}, bf16[128,128]{1,0:T(8,128)(2,1)S(1)}, u32[]{:S(2)}, u32[]{:S(2)}) collective-permute-start(bf16[128,128]{1,0:T(8,128)(2,1)S(1)} %subtract_convert_fusion.1), channel_id=1, source_target_pairs={{0,4},{4,0},{1,5},{5,1},{2,6},{6,2},{3,7},{7,3},{8,12},{12,8},{9,1... | collective-permute-start | bytes 98312 | tf_op jit(solution)/shard_map/ppermute | solution.py:24
  222.3 14.9 %collective-permute-start.8 = (bf16[8,128,128]{2,1,0:T(8,128)(2,1)}, bf16[8,128,128]{2,1,0:T(8,128)(2,1)S(1)}, u32[]{:S(2)}, u32[]{:S(2)}) collective-permute-start(bf16[8,128,128]{2,1,0:T(8,128)(2,1)} %get-tuple-element.26), channel_id=1, source_target_pairs={{0,4},{4,0},{1,5},{5,1},{2,6},{6,2},{3,7},{7,3},{8,12},{12,8},{9,1... | collective-permute-start | bytes 786440 | tf_op jit(solution)/shard_map/ppermute | solution.py:24
  226.1 11.2 %all-to-all-start.8 = ((bf16[8,32,128]{2,1,0:T(8,128)(2,1)}), bf16[8,32,128]{2,1,0:T(8,128)(2,1)S(1)}, u32[]{:S(2)}, u32[]{:S(2)}) async-start(bf16[8,32,128]{2,1,0:T(8,128)(2,1)} %bitcast.38), calls=%async_computation.8 | async-start | bytes 131072 | tf_op jit(solution)/shard_map/all_to_all | solution.py:299
  239.3 12.5 %all-to-all-start.9 = ((bf16[8,128,128]{2,1,0:T(8,128)(2,1)}), bf16[8,128,128]{2,1,0:T(8,128)(2,1)S(1)}, u32[]{:S(2)}, u32[]{:S(2)}) async-start(bf16[8,128,128]{2,1,0:T(8,128)(2,1)} %add_convert_fusion), calls=%async_computation.9 | async-start | bytes 524288 | tf_op jit(solution)/shard_map/all_to_all | solution.py:186
  252.6 16.3 %all-to-all-start.10 = ((bf16[8,128,128]{2,1,0:T(8,128)(2,1)}), bf16[8,128,128]{2,1,0:T(8,128)(2,1)S(1)}, u32[]{:S(2)}, u32[]{:S(2)}) async-start(bf16[8,128,128]{2,1,0:T(8,128)(2,1)} %broadcast_in_dim.35), calls=%async_computation.10 | async-start | bytes 524288 | tf_op jit(solution)/shard_map/all_to_all | solution.py:28
  270.7 27.6 %all-to-all-start.11 = ((bf16[16,32,128]{2,1,0:T(8,128)(2,1)}), bf16[16,32,128]{2,1,0:T(8,128)(2,1)S(1)}, u32[]{:S(2)}, u32[]{:S(2)}) async-start(bf16[16,32,128]{2,1,0:T(8,128)(2,1)} %bitcast.106), calls=%async_computation.11 | async-start | bytes 262144 | tf_op jit(solution)/shard_map/all_to_all | solution.py:316
  281.3 14.2 %collective-permute-start.7 = (bf16[768,128]{1,0:T(8,128)(2,1)}, bf16[768,128]{1,0:T(8,128)(2,1)S(1)}, u32[]{:S(2)}, u32[]{:S(2)}) collective-permute-start(bf16[768,128]{1,0:T(8,128)(2,1)} %get-tuple-element.24), channel_id=1, source_target_pairs={{0,256},{64,320},{128,384},{192,448},{256,0},{320,64},{384,128},{4... | collective-permute-start | bytes 589832 | tf_op jit(solution)/shard_map/ppermute | solution.py:20
  (40 other events, 888.5 us)
Sparse Core Ops, SparseCore 0:
  9.6 50.3 all-gather.6
  62.1 45.1 all-gather.4

commit v3 on v2

--- a/solution.py
+++ b/solution.py
@@ -81,7 +81,26 @@
     out[...] = value[...] + column(table, RO + 1) * got[...].astype(F32)
 
 
-def first_update(panel, solved, value, got, base):
+def assemble(core, mine, other, solved):
+    ny, half, _ = mine.shape
+    for y in range(ny):
+        for h in range(2):
+            start = (2 * y + h) * half
+
+            @pl.when(core[0] == h)
+            def _():
+                solved[start:start + half] = mine[y]
+
+            @pl.when(core[0] != h)
+            def _():
+                solved[start:start + half] = other[y]
+
+
+def first_update(core, panel, mine, other, value, got, base, solved):
+    @pl.when(pl.program_id(0) == 0)
+    def _():
+        assemble(core, mine, other, solved)
+
     base[...] = value[...] + got[...].astype(F32) - dot(panel[...], solved[...])
 
 
@@ -101,8 +120,14 @@
                 away[y] = block.astype(BF)
 
 
-def middle(low, tile, core, panel, solved, base, table, scaled, rounded, mine, away, acc):
+def middle(
+        low, tile, core, panel, own, other, base, table, scaled, rounded, mine, away, acc, solved):
     step = pl.program_id(0)
+
+    @pl.when(step == 0)
+    def _():
+        assemble(core, own, other, solved)
+
     v = (base[...] - dot(panel[...], solved[...])) / column(table, PIV)
     scaled[...] = v
     row = lax.broadcasted_iota(jnp.int32, v.shape, 0) + step * tile
@@ -138,6 +163,78 @@
     @pl.when(step == pl.num_programs(0) - 1)
     def _():
         split_term(core, acc, mine, away)
+
+
+def second_input(core, x1, mine_rows, other_rows, solved, spread, rows):
+    ny, half, width = solved.shape
+    rb = mine_rows.shape[0]
+    first = jnp.where(core[0] == 0, 1.0, 0.0)
+
+    @pl.when(core[0] == 0)
+    def _():
+        rows[:rb] = mine_rows[...]
+        rows[rb:] = other_rows[...]
+
+    @pl.when(core[0] != 0)
+    def _():
+        rows[:rb] = other_rows[...]
+        rows[rb:] = mine_rows[...]
+
+    v = first * x1[...]
+    for y in range(ny):
+        start = pl.multiple_of((2 * y + core[0]) * half, half)
+        v = v - dot(rows[:, pl.ds(start, half)], solved[y])
+    v = v.astype(BF)
+    for y in range(ny):
+        spread[y] = v
+
+
+def cross_back(core, tile, target, cross, term, away, back, out):
+    ny, half, _ = term.shape
+    v = dot(tile[...], target[...])
+    back[...] = v
+    turned = v.T.astype(BF)
+    for y in range(ny):
+        start = pl.multiple_of((2 * y + core[0]) * half, half)
+        share = dot(turned, cross[:, pl.ds(start, half)]).T
+        out[y] = (term[y] + away[y].astype(F32) + share).astype(BF)
+
+
+def end_bands(ny, outer, inner, core, coefs, tile, target, back1, last):
+    n, rb = coefs.shape[:2]
+    first = jnp.where(core[0] == 0, 1.0, 0.0)
+    values = [dot(tile[...], target[...]), first * back1[...]]
+    for b in range(2):
+        v = [values[b][i * rb:(i + 1) * rb] for i in range(n)]
+        for level, bit in ((RI, 2 * inner), (RO, 2 * outer)):
+            k = 2 * level + b
+            v = [coefs[i][:, k:k + 1] * v[i] + coefs[i][:, k + 2:k + 3] * v[i ^ bit]
+                 for i in range(n)]
+        for i in range(n):
+            last[i, b * rb:(b + 1) * rb] = v[i].astype(BF)
+
+
+def spread_sum(arrived, count, base=None, pivots=None):
+    rb, width = arrived.shape[1:]
+
+    def body(*refs):
+        own, spread = refs[-2:]
+        v = jnp.sum(refs[0][...].astype(F32), axis=0)
+        if base is not None:
+            v = refs[1][...] / refs[2][...] - v
+        own[...] = v
+        v = v.astype(BF)
+        for i in range(count):
+            spread[i] = v
+
+    args = (arrived,) if base is None else (arrived, base, pivots)
+    return pl.pallas_call(
+        body,
+        out_shape=(jax.ShapeDtypeStruct((rb, width), F32),
+                   jax.ShapeDtypeStruct((count, rb, width), BF)),
+        cost_estimate=pl.CostEstimate(
+            flops=0, bytes_accessed=2 * arrived.size, transcendentals=0),
+    )(*args)
 
 
 def start_bands(ny, outer, inner, coefs, arrived, part, x1):
@@ -169,25 +266,18 @@
     rows, width = rhs.shape
     half = nz * rb
     low = 2 * rb
-    core, y, z = lax.axis_index("c"), lax.axis_index("y"), lax.axis_index("z")
+    core, y = lax.axis_index("c"), lax.axis_index("y")
     outer, inner = ny // 2, ny // 4
     chunk = ny * 2 * rb
-    first_core = core == 0
-    once = jnp.where(first_core, 1.0, 0.0).astype(F32)
     core_ref = core.astype(jnp.int32)[None]
 
-    def both_halves(mine):
-        other = swap_core(mine)
-        even = jnp.where(first_core, mine, other)
-        odd = jnp.where(first_core, other, mine)
-        return jnp.stack([even, odd], axis=1).reshape(band, width)
-
-    def reduce_y_everywhere_z(mine):
-        v = total(lax.all_to_all(mine.astype(BF), "y", 0, 0))
-        return total(everyone(v.astype(BF), "z", nz))
+    def reduce_yz(mine):
+        return lax.all_to_all(mine.astype(BF).reshape(ny * nz, rb, width), ("y", "z"), 0, 0)
+
+    def gather_yz(spread):
+        return lax.all_to_all(spread, ("y", "z"), 0, 0).reshape(ny, half, width)
 
     gathered0 = lax.all_gather(panels[0], "x", axis=0, tiled=True)
-    gathered1 = lax.all_gather(panels[1], "x", axis=0, tiled=True)
 
     table = jnp.concatenate([left.reshape(4, rows), right.reshape(4, rows), pivots[None]], axis=0)
     table = jnp.pad(table, ((0, 7), (0, 0))).T
@@ -203,11 +293,16 @@
     message = jnp.concatenate([wide0, wide1, shared], axis=2).reshape(ny * 2, 6, rb, half)
     arrived = lax.all_to_all(message, ("y", "c"), 0, 0)
 
+    to_owner = [(i, (i % nz) * 2 + i // nz) for i in range(2 * nz)]
+    own_pivots = lax.ppermute(
+        jnp.broadcast_to(table[:low, PIV:PIV + 1], (low, width)), ("z", "c"), to_owner)
+
     shape = jax.ShapeDtypeStruct
     whole, sent = shape((rows, width), F32), shape((rows, width), BF)
     send = elementwise(left_send, sent, rhs, table)
-    value, send = elementwise(
-        left_middle, (whole, sent), rhs, swap_y(send, outer, ny), table)
+    got = swap_y(send, outer, ny)
+    arrived, got, own_pivots = lax.optimization_barrier((arrived, got, own_pivots))
+    value, send = elementwise(left_middle, (whole, sent), rhs, got, table)
     crossed = swap_y(send, inner, ny)
 
     small = arrived[:, 5].astype(F32)
@@ -220,99 +315,91 @@
         lambda *refs: start_bands(ny, outer, inner, *refs),
         out_shape=(shape((half, width), BF), shape((ny * 2, rb, width), F32)),
     )(small, arrived)
-    x1 = once * lax.dynamic_slice_in_dim(x1, 2 * y, 2, 0).reshape(low, width)
-
-    few = lax.dynamic_slice_in_dim(arrived[:, 5], 2 * y, 2, 0)
-    few = jnp.concatenate(
-        [few[c, :, o + 2 * PIV:o + 2 * PIV + 2] for c in (0, 1) for o in (0, 32)], axis=1)
-    few = jnp.pad(few, ((0, 0), (0, width - few.shape[1])))
-    met = everyone(jnp.concatenate([part, few], axis=0), "z", nz)
-    half0 = total(met[:, :half])
-    few = lax.dynamic_slice_in_dim(met[:, half:], core * (nz // 2), nz // 2, 0).astype(F32)
-    own_pivots = [
-        jnp.stack([few[:, :, 4 * c + b] + few[:, :, 4 * c + 2 + b] for c in (0, 1)], axis=1)
-        .reshape(half, 1) for b in (0, 1)]
-    mine0 = everyone(half0.astype(BF), "y", ny)
-    s0 = both_halves(mine0)
-
-    cross = gathered0[rb:low].reshape(rb, ny, 2, half)
-    cross_mine = jnp.where(first_core, cross[:, :, 0], cross[:, :, 1]).reshape(rb, ny * half)
-    cross_away = jnp.where(first_core, cross[:, :, 1], cross[:, :, 0]).reshape(rb, ny * half)
-    cross_got = swap_core(cross_away)
-    cross = jnp.concatenate([
-        jnp.where(first_core, cross_mine, cross_got),
-        jnp.where(first_core, cross_got, cross_mine)], axis=0)
-    x1 = x1 - dot(cross, mine0.reshape(ny * half, width))
-    x1 = everyone(x1.astype(BF), "y", ny).reshape(chunk, width)
-    part = down(tile1, x1).reshape(2, half, width)
-    away = swap_core(jnp.where(first_core, part[1], part[0]).astype(BF)).astype(F32)
-    part = jnp.where(first_core, part[0], part[1]) + away
-    half1 = total(everyone(part.astype(BF), "z", nz))
+    x1 = lax.dynamic_slice_in_dim(x1, 2 * y, 2, 0).reshape(low, width)
+
+    own0, spread = spread_sum(lax.all_to_all(part.reshape(nz, rb, width), "z", 0, 0), ny * nz)
+    spread, second = lax.optimization_barrier((spread, panels[1]))
+    gathered1 = lax.all_gather(second, "x", axis=0, tiled=True)
+    mine0 = gather_yz(spread)
+    mine0, crossed = lax.optimization_barrier((mine0, crossed))
+
+    core_spec = pl.BlockSpec(memory_space=pltpu.SMEM)
+    vmem = pl.BlockSpec(memory_space=pltpu.VMEM)
+    cross = gathered0[rb:low]
+    spread = pl.pallas_call(
+        second_input, out_shape=shape((ny, low, width), BF),
+        in_specs=[core_spec] + [vmem] * 4, out_specs=vmem,
+        scratch_shapes=[pltpu.VMEM((low, band), BF)],
+    )(core_ref, x1, cross, swap_core(cross), mine0)
+    x1 = lax.all_to_all(spread, "y", 0, 0).reshape(chunk, width)
+    other0 = swap_core(mine0)
+    part = down(tile1, x1).astype(BF).reshape(2 * nz, rb, width)
+    met = lax.all_to_all(part, ("c", "z"), 0, 0)
+    met, other0 = lax.optimization_barrier((met, other0))
+    own1, spread = spread_sum(met, ny * nz)
 
     tile = rows // 3
     steps = rows // tile
     panel_spec = pl.BlockSpec((tile, band), lambda i: (i, 0))
-    solved_spec = pl.BlockSpec((band, width), lambda i: (0, 0))
     row_spec = pl.BlockSpec((tile, width), lambda i: (i, 0))
     table_spec = pl.BlockSpec((tile, 16), lambda i: (i, 0))
-    core_spec = pl.BlockSpec(memory_space=pltpu.SMEM)
     half_spec = pl.BlockSpec((ny, half, width), lambda i: (0, 0, 0))
     params = pltpu.CompilerParams(vmem_limit_bytes=40 * 2 ** 20)
     cost = pl.CostEstimate(
         flops=2 * rows * band * width, bytes_accessed=2 * rows * band, transcendentals=0)
+    solved_ref = pltpu.VMEM((band, width), BF)
     base = pl.pallas_call(
         first_update, out_shape=whole, grid=(steps,),
-        in_specs=[panel_spec, solved_spec, row_spec, row_spec], out_specs=row_spec,
+        in_specs=[core_spec, panel_spec, half_spec, half_spec, row_spec, row_spec],
+        out_specs=row_spec, scratch_shapes=[solved_ref],
         compiler_params=params, cost_estimate=cost,
-    )(gathered0, s0, value, crossed)
-
-    s1 = both_halves(everyone(half1.astype(BF), "y", ny))
+    )(core_ref, gathered0, mine0, other0, value, crossed)
+
+    mine1 = gather_yz(spread)
+    mine1, base, cross = lax.optimization_barrier((mine1, base, cross))
+    cross = lax.all_gather(cross, ("y", "c"), axis=0, tiled=True)
+    other1 = swap_core(mine1)
     halves = (shape((ny, half, width), F32), shape((ny, half, width), BF))
-    scaled, rounded, mine1, away1 = pl.pallas_call(
+    scaled, rounded, term1, away1 = pl.pallas_call(
         lambda *refs: middle(low, tile, *refs),
         out_shape=(whole, sent) + halves, grid=(steps,),
-        in_specs=[core_spec, panel_spec, solved_spec, row_spec, table_spec],
+        in_specs=[core_spec, panel_spec, half_spec, half_spec, row_spec, table_spec],
         out_specs=(row_spec, row_spec, half_spec, half_spec),
-        scratch_shapes=[pltpu.VMEM((width, band), F32)],
+        scratch_shapes=[pltpu.VMEM((width, band), F32), solved_ref],
         compiler_params=params, cost_estimate=cost,
-    )(core_ref, gathered1, s1, base, table)
-    target1 = half1 / own_pivots[1] - reduce_y_everywhere_z(
-        mine1 + swap_core(away1).astype(F32))
-
-    mine0, away0 = pl.pallas_call(
+    )(core_ref, gathered1, mine1, other1, base, table)
+    met = reduce_yz(term1 + swap_core(away1).astype(F32))
+
+    got = swap_y(rounded, inner, ny)
+    term0, away0 = pl.pallas_call(
         first_term, out_shape=halves, grid=(steps,),
         in_specs=[core_spec, panel_spec, row_spec], out_specs=(half_spec, half_spec),
         scratch_shapes=[pltpu.VMEM((width, band), F32)],
         compiler_params=params, cost_estimate=cost,
     )(core_ref, gathered0, rounded)
-    mine0 = mine0 + swap_core(away0).astype(F32)
-
-    value, send = elementwise(
-        right_middle, (whole, sent), scaled, swap_y(rounded, inner, ny), table)
-    out = elementwise(right_end, whole, value, swap_y(send, outer, ny), table)
-
-    t1 = target1.astype(BF)
-    other = swap_core(t1)
-    t1 = jnp.concatenate([
-        jnp.where(first_core, t1, other), jnp.where(first_core, other, t1)], axis=0)
-    back1 = dot(tile1, t1)
-    solved1 = total(lax.all_to_all(back1.astype(BF).reshape(ny, low, width), "y", 0, 0))
-    mine0 = mine0 + down(cross, solved1.astype(BF)).reshape(ny, half, width)
-    target0 = half0 / own_pivots[0] - reduce_y_everywhere_z(mine0)
-    back0 = dot(tile0, target0.astype(BF))
-
-    def pair(v, bit):
-        return jnp.concatenate([v[i ^ bit][None] for i in range(ny)], axis=0)
-
-    def finished(v, b):
-        v = v.reshape(ny, 2, rb, width)
-        k = small.reshape(ny, 2, rb, 32)
-        at = lambda column: k[:, :, :, 2 * column + b, None]
-        v = at(RI) * v + at(RI + 1) * pair(v, inner)
-        return at(RO) * v + at(RO + 1) * pair(v, outer)
-
-    last = jnp.stack([finished(back0, 0), finished(once * back1, 1)], axis=2)
-    last = last.astype(BF).reshape(ny * 2, low, width)
+    away0 = swap_core(away0)
+    met, got, term0, away0, cross = lax.optimization_barrier((met, got, term0, away0, cross))
+    _, spread = spread_sum(met, 2 * nz, own1, own_pivots[rb:])
+
+    value, send = elementwise(right_middle, (whole, sent), scaled, got, table)
+    got = swap_y(send, outer, ny)
+    t1 = lax.all_to_all(spread, ("c", "z"), 0, 0).reshape(2 * half, width)
+    back1, term0 = pl.pallas_call(
+        cross_back, out_shape=(shape((chunk, width), F32), shape((ny, half, width), BF)),
+        in_specs=[core_spec] + [vmem] * 5, out_specs=(vmem, vmem),
+        compiler_params=params,
+    )(core_ref, tile1, t1, cross, term0, away0)
+    met = reduce_yz(term0)
+    met, got = lax.optimization_barrier((met, got))
+    _, spread = spread_sum(met, nz, own0, own_pivots[:rb])
+    out = elementwise(right_end, whole, value, got, table)
+    t0 = lax.all_to_all(spread, "z", 0, 0).reshape(half, width)
+    t0, out = lax.optimization_barrier((t0, out))
+    last = pl.pallas_call(
+        lambda *refs: end_bands(ny, outer, inner, *refs),
+        out_shape=shape((ny * 2, low, width), BF),
+        in_specs=[core_spec] + [vmem] * 4, out_specs=vmem,
+    )(core_ref, small, tile0, t0, back1)
     head = total(lax.all_to_all(last, ("y", "c"), 0, 0))
     return lax.dynamic_update_slice(out, head, (0, 0))
 

time: 310 us -> 275 us (0.89)
  waiting for transfers between devices: 94.2 us -> 62.1 us
  Pallas kernels: 20 us -> 32.6 us
  local copies, waits for them, and re-layouts: 34.2 us -> 23.2 us
  blocking collectives: 24.6 us -> 33.7 us
  other arithmetic: 12.4 us -> 3.41 us
  matrix products: 5.2 us -> 0.86 us
    all_to_all x9 -> x8, waiting for transfers between devices: 57.8 us -> 29 us  [the longest x2 9.23 us: gather_yz(): return lax.all_to_all(spread, ('y', 'z'), 0, 0).reshape(ny, half, width)]
    all_to_all x1, waiting for transfers between devices: 13.8 us -> 0.01 us  [shards(): arrived = lax.all_to_all(message, ('y', 'c'), 0, 0)]
    pallas_call x1 -> x8, Pallas kernels: 1.28 us -> 13.3 us  [the longest x4 6.45 us: spread_sum(): pl.pallas_call(body, out_shape=(jax.ShapeDtypeStruct((rb, width), F32), j...]
    all_to_all x2, blocking collectives: 24.6 us -> 33.7 us  [the longest x1 18.3 us: shards(): head = total(lax.all_to_all(last, ('y', 'c'), 0, 0))]
    ppermute x0 -> x1, waiting for transfers between devices: none -> 8.34 us  [shards(): lax.ppermute(jnp.broadcast_to(table[:low, PIV:PIV + 1], (low, width)), ('...]
    unnamed x116 -> x66, local copies, waits for them, and re-layouts: 19.3 us -> 14.8 us
    another operation x8 -> x0, other arithmetic: 4.01 us -> none  [the longest x4 2.98 us: both_halves(): return jnp.stack([even, odd], axis=1).reshape(band, width)]
    broadcast_in_dim x7 -> x1, local copies, waits for them, and re-layouts: 3.79 us -> 0.07 us  [shards(): jnp.broadcast_to(table[:low, PIV:PIV + 1], (low, width))]
  transfers between devices with their start and end apart: 23 -> 22, of which waited for: 13 -> 13; matrix products, arithmetic and copies ran while one was open for 12% -> 3% of each run, Pallas kernels for 5% -> 9%
where the time goes in v3:
time: 275 us; the launch traced here: 273 us
  starting transfers between devices  103 us (37%)
  waiting for transfers between devices  62.1 us (23%)
  blocking collectives  33.7 us (12%)
  Pallas kernels  32.6 us (12%)
  local copies, waits for them, and re-layouts  23.2 us (8%)
  between operations  13.6 us (5%)
  other arithmetic  3.41 us (1%)
    ppermute x4, waiting for transfers between devices, swap_y(): return lax.ppermute(v, 'y', [(i, i ^ bit) for i in range(count)])  22.1 us
    ppermute x4, starting transfers between devices, swap_y(): return lax.ppermute(v, 'y', [(i, i ^ bit) for i in range(count)])  20.1 us
    ppermute x5, starting transfers between devices, swap_core(): return lax.ppermute(v, 'c', [(0, 1), (1, 0)])  19 us
    all_to_all x1, blocking collectives, shards(): head = total(lax.all_to_all(last, ('y', 'c'), 0, 0))  18.3 us
    all_to_all x1, blocking collectives, shards(): lax.all_to_all(part.reshape(nz, rb, width), 'z', 0, 0)  15.5 us
    unnamed x66, local copies, waits for them, and re-layouts  14.8 us
    all_to_all x2, starting transfers between devices, reduce_yz(): lax.all_to_all(mine.astype(BF).reshape(ny * nz, rb, width), ('y', 'z'), 0...  13.9 us
    all_to_all x2, starting transfers between devices, gather_yz(): return lax.all_to_all(spread, ('y', 'z'), 0, 0).reshape(ny, half, width)  10.4 us
  transfers between devices with their start and end apart: 22, of which 13 were waited for; matrix products, arithmetic and copies ran while one was open for 3% of the time, Pallas kernels for 9%

profile of v3, /device:TPU:1, one launch (start us, length us, event | category | flops | bytes accessed | tf_op | source)
XLA Modules:
  0.0 272.6 jit_solution(2225924824350627476)
XLA Ops:
  11.0 10.2 %all-to-all-start = ((bf16[16,6,16,128]{3,2,1,0:T(8,128)(2,1)}), bf16[16,6,16,128]{3,2,1,0:T(8,128)(2,1)S(1)}, u32[]{:S(2)}, u32[]{:S(2)}) async-start(bf16[16,6,16,128]{3,2,1,0:T(8,128)(2,1)} %pad_maximum_fusion), calls=%async_computation | async-start | bytes 786432 | tf_op jit(solution)/shard_map/all_to_all | solution.py:294
  23.2 7.2 %collective-permute-start = (bf16[768,128]{1,0:T(8,128)(2,1)}, bf16[768,128]{1,0:T(8,128)(2,1)S(1)}, u32[]{:S(2)}, u32[]{:S(2)}) collective-permute-start(bf16[768,128]{1,0:T(8,128)(2,1)} %shard_map.64), channel_id=1, source_target_pairs={{0,256},{64,320},{128,384},{192,448},{256,0},{320,64},{384,128},{4... | collective-permute-start | bytes 589832 | tf_op jit(solution)/shard_map/ppermute | solution.py:20
  34.3 8.3 %collective-permute-done.1 = f32[32,128]{1,0:T(8,128)S(1)} collective-permute-done((f32[32,128]{1,0:T(8,128)S(1)}, f32[32,128]{1,0:T(8,128)S(1)}, u32[]{:S(2)}, u32[]{:S(2)}) %collective-permute-start.1) | collective-permute-done | bytes 16416 | tf_op jit(solution)/shard_map/ppermute | solution.py:297
  47.7 15.5 %all_to_all.55.refs_0_ = bf16[8,16,128]{2,1,0:T(8,128)(2,1)} all-to-all(bf16[8,16,128]{2,1,0:T(8,128)(2,1)} %bitcast.59), channel_id=1, replica_groups=mesh['y'=8,'z'=8,'c'=2,'x'=4] {'z'}, dimensions={0} | all-to-all | bytes 65536 | tf_op jit(solution)/shard_map/all_to_all | solution.py:320
  69.0 4.9 %all-to-all-start.2 = ((bf16[64,16,128]{2,1,0:T(8,128)(2,1)}), bf16[64,16,128]{2,1,0:T(8,128)(2,1)S(1)}, u32[]{:S(2)}, u32[]{:S(2)}) async-start(bf16[64,16,128]{2,1,0:T(8,128)(2,1)} %get-tuple-element.51), calls=%async_computation.2 | async-start | bytes 524288 | tf_op jit(solution)/shard_map/all_to_all | solution.py:278
  74.8 4.3 %collective-permute-start.2 = (bf16[16,2048]{1,0:T(8,128)(2,1)S(1)}, bf16[16,2048]{1,0:T(8,128)(2,1)S(1)}, u32[]{:S(2)}, u32[]{:S(2)}) collective-permute-start(bf16[16,2048]{1,0:T(8,128)(2,1)S(1)} %slice_bitcast_fusion.1.mine_rows), channel_id=1, source_target_pairs={{0,4},{4,0},{1,5},{5,1},{2,6},{6,2},{3,7},{7,3},{8,12},{12,8},{9,1... | collective-permute-start | bytes 196616 | tf_op jit(solution)/shard_map/ppermute | solution.py:24
  93.6 5.0 %collective-permute-start.4 = (bf16[8,128,128]{2,1,0:T(8,128)(2,1)}, bf16[8,128,128]{2,1,0:T(8,128)(2,1)S(1)}, u32[]{:S(2)}, u32[]{:S(2)}) collective-permute-start(bf16[8,128,128]{2,1,0:T(8,128)(2,1)} %bitcast.42), channel_id=1, source_target_pairs={{0,4},{4,0},{1,5},{5,1},{2,6},{6,2},{3,7},{7,3},{8,12},{12,8},{9,1... | collective-permute-start | bytes 786440 | tf_op jit(solution)/shard_map/ppermute | solution.py:24
  101.0 8.6 %all-to-all-start.4 = ((bf16[16,16,128]{2,1,0:T(8,128)(2,1)}), bf16[16,16,128]{2,1,0:T(8,128)(2,1)S(1)}, u32[]{:S(2)}, u32[]{:S(2)}) async-start(bf16[16,16,128]{2,1,0:T(8,128)(2,1)} %bitcast.22), calls=%async_computation.4 | async-start | bytes 131072 | tf_op jit(solution)/shard_map/all_to_all | solution.py:337
  109.7 7.2 %all-to-all-done.4.refs_0_ = bf16[16,16,128]{2,1,0:T(8,128)(2,1)S(1)} async-done(((bf16[16,16,128]{2,1,0:T(8,128)(2,1)}), bf16[16,16,128]{2,1,0:T(8,128)(2,1)S(1)}, u32[]{:S(2)}, u32[]{:S(2)}) %all-to-all-start.4) | async-done | bytes 65568 | tf_op jit(solution)/shard_map/all_to_all | solution.py:337
  119.0 5.5 %all-to-all-start.5 = ((bf16[64,16,128]{2,1,0:T(8,128)(2,1)}), bf16[64,16,128]{2,1,0:T(8,128)(2,1)}, u32[]{:S(2)}, u32[]{:S(2)}) async-start(bf16[64,16,128]{2,1,0:T(8,128)(2,1)} %get-tuple-element.56), calls=%async_computation.5 | async-start | bytes 524288 | tf_op jit(solution)/shard_map/all_to_all | solution.py:278
  130.6 6.4 %all-to-all-done.5 = bf16[64,16,128]{2,1,0:T(8,128)(2,1)} async-done(((bf16[64,16,128]{2,1,0:T(8,128)(2,1)}), bf16[64,16,128]{2,1,0:T(8,128)(2,1)}, u32[]{:S(2)}, u32[]{:S(2)}) %all-to-all-start.5) | async-done | bytes 262176 | tf_op jit(solution)/shard_map/all_to_all | solution.py:278
  137.1 5.2 %collective-permute-start.5 = (bf16[8,128,128]{2,1,0:T(8,128)(2,1)}, bf16[8,128,128]{2,1,0:T(8,128)(2,1)}, u32[]{:S(2)}, u32[]{:S(2)}) collective-permute-start(bf16[8,128,128]{2,1,0:T(8,128)(2,1)} %bitcast.23.refs_2_), channel_id=1, source_target_pairs={{0,4},{4,0},{1,5},{5,1},{2,6},{6,2},{3,7},{7,3},{8,12},{12,8},{9,1... | collective-permute-start | bytes 786440 | tf_op jit(solution)/shard_map/ppermute | solution.py:24
  146.7 5.4 %shard_map.71 = (f32[768,128]{1,0:T(8,128)S(1)}, bf16[768,128]{1,0:T(8,128)(2,1)S(1)}, f32[8,128,128]{2,1,0:T(8,128)S(1)}, bf16[8,128,128]{2,1,0:T(8,128)(2,1)S(1)}) custom-call(s32[1]{0:T(128)} %bitcast.core.refs_0_, bf16[768,2048]{1,0:T(8,128)(2,1)S(1)} %copy-done.4, bf16[8,128,128]{2,1,0:T(8,128)(2,1)} %bitcast.23.refs_2_, ...), custom_call_target="tpu_custom_call" | custom-call | flops 402653184 | bytes 3145728 | tf_op jit(solution)/shard_map/pallas_call | solution.py:363
  156.3 5.5 %all-to-all-start.6 = ((bf16[64,16,128]{2,1,0:T(8,128)(2,1)}), bf16[64,16,128]{2,1,0:T(8,128)(2,1)}, u32[]{:S(2)}, u32[]{:S(2)}) async-start(bf16[64,16,128]{2,1,0:T(8,128)(2,1)} %bitcast.25), calls=%async_computation.6 | async-start | bytes 524288 | tf_op jit(solution)/shard_map/all_to_all | solution.py:275
  168.7 4.0 %collective-permute-start.7 = (bf16[768,128]{1,0:T(8,128)(2,1)S(1)}, bf16[768,128]{1,0:T(8,128)(2,1)S(1)}, u32[]{:S(2)}, u32[]{:S(2)}) collective-permute-start(bf16[768,128]{1,0:T(8,128)(2,1)S(1)} %copy-done.15), channel_id=1, source_target_pairs={{0,128},{64,192},{128,0},{192,64},{256,384},{320,448},{384,256},{4... | collective-permute-start | bytes 589832 | tf_op jit(solution)/shard_map/ppermute | solution.py:20
  173.3 8.7 %collective-permute-done.7.got = bf16[768,128]{1,0:T(8,128)(2,1)S(1)} collective-permute-done((bf16[768,128]{1,0:T(8,128)(2,1)S(1)}, bf16[768,128]{1,0:T(8,128)(2,1)S(1)}, u32[]{:S(2)}, u32[]{:S(2)}) %collective-permute-start.7) | collective-permute-done | bytes 196640 | tf_op jit(solution)/shard_map/ppermute | solution.py:20
  183.8 7.6 %all-to-all-start.7 = ((bf16[16,16,128]{2,1,0:T(8,128)(2,1)}), bf16[16,16,128]{2,1,0:T(8,128)(2,1)S(1)}, u32[]{:S(2)}, u32[]{:S(2)}) async-start(bf16[16,16,128]{2,1,0:T(8,128)(2,1)} %get-tuple-element.71), calls=%async_computation.7 | async-start | bytes 131072 | tf_op jit(solution)/shard_map/all_to_all | solution.py:386
  192.3 6.3 %all-to-all-done.7 = bf16[16,16,128]{2,1,0:T(8,128)(2,1)S(1)} async-done(((bf16[16,16,128]{2,1,0:T(8,128)(2,1)}), bf16[16,16,128]{2,1,0:T(8,128)(2,1)S(1)}, u32[]{:S(2)}, u32[]{:S(2)}) %all-to-all-start.7) | async-done | bytes 65568 | tf_op jit(solution)/shard_map/all_to_all | solution.py:386
  202.8 8.5 %all-to-all-start.8 = ((bf16[64,16,128]{2,1,0:T(8,128)(2,1)}), bf16[64,16,128]{2,1,0:T(8,128)(2,1)S(1)}, u32[]{:S(2)}, u32[]{:S(2)}) async-start(bf16[64,16,128]{2,1,0:T(8,128)(2,1)} %bitcast.27), calls=%async_computation.8 | async-start | bytes 524288 | tf_op jit(solution)/shard_map/all_to_all | solution.py:275
  213.7 6.9 %collective-permute-start.9 = (bf16[768,128]{1,0:T(8,128)(2,1)}, bf16[768,128]{1,0:T(8,128)(2,1)S(1)}, u32[]{:S(2)}, u32[]{:S(2)}) collective-permute-start(bf16[768,128]{1,0:T(8,128)(2,1)} %get-tuple-element.78), channel_id=1, source_target_pairs={{0,256},{64,320},{128,384},{192,448},{256,0},{320,64},{384,128},{4... | collective-permute-start | bytes 589832 | tf_op jit(solution)/shard_map/ppermute | solution.py:20
  220.6 8.2 %collective-permute-done.9.got = bf16[768,128]{1,0:T(8,128)(2,1)S(1)} collective-permute-done((bf16[768,128]{1,0:T(8,128)(2,1)}, bf16[768,128]{1,0:T(8,128)(2,1)S(1)}, u32[]{:S(2)}, u32[]{:S(2)}) %collective-permute-start.9) | collective-permute-done | bytes 196640 | tf_op jit(solution)/shard_map/ppermute | solution.py:20
  231.1 6.4 %all-to-all-start.9 = ((bf16[8,16,128]{2,1,0:T(8,128)(2,1)}), bf16[8,16,128]{2,1,0:T(8,128)(2,1)S(1)}, u32[]{:S(2)}, u32[]{:S(2)}) async-start(bf16[8,16,128]{2,1,0:T(8,128)(2,1)} %get-tuple-element.81), calls=%async_computation.9 | async-start | bytes 65536 | tf_op jit(solution)/shard_map/all_to_all | solution.py:396
  239.7 4.7 %all-to-all-done.9 = bf16[8,16,128]{2,1,0:T(8,128)(2,1)S(1)} async-done(((bf16[8,16,128]{2,1,0:T(8,128)(2,1)}), bf16[8,16,128]{2,1,0:T(8,128)(2,1)S(1)}, u32[]{:S(2)}, u32[]{:S(2)}) %all-to-all-start.9) | async-done | bytes 32800 | tf_op jit(solution)/shard_map/all_to_all | solution.py:396
  247.2 18.3 %all_to_all.56 = bf16[16,32,128]{2,1,0:T(8,128)(2,1)S(1)} all-to-all(bf16[16,32,128]{2,1,0:T(8,128)(2,1)} %shard_map.78), channel_id=1, replica_groups=mesh['y'=8,'z'=8,'c'=2,'x'=4] {'y','c'}, dimensions={0} | all-to-all | bytes 262144 | tf_op jit(solution)/shard_map/all_to_all | solution.py:403
  (142 shorter events, 80.3 us)
Async XLA Ops:
  6.5 67.4 %all-gather.9.cloned.1.call-start = ((), (), s32[]{:S(2)}) async-start(), calls=%async_computation.13 | async-start | bytes 3932160 | tf_op jit(solution)/shard_map/all_gather | solution.py:280
  11.0 33.6 %all-to-all-start = ((bf16[16,6,16,128]{3,2,1,0:T(8,128)(2,1)}), bf16[16,6,16,128]{3,2,1,0:T(8,128)(2,1)S(1)}, u32[]{:S(2)}, u32[]{:S(2)}) async-start(bf16[16,6,16,128]{3,2,1,0:T(8,128)(2,1)} %pad_maximum_fusion), calls=%async_computation | async-start | bytes 786432 | tf_op jit(solution)/shard_map/all_to_all | solution.py:294
  21.2 121.1 %all-gather.5.cloned.1.call-start = ((), (), s32[]{:S(2)}) async-start(), calls=%async_computation.11 | async-start | bytes 3932160 | tf_op jit(solution)/shard_map/all_gather | solution.py:322
  23.2 21.4 %collective-permute-start = (bf16[768,128]{1,0:T(8,128)(2,1)}, bf16[768,128]{1,0:T(8,128)(2,1)S(1)}, u32[]{:S(2)}, u32[]{:S(2)}) collective-permute-start(bf16[768,128]{1,0:T(8,128)(2,1)} %shard_map.64), channel_id=1, source_target_pairs={{0,256},{64,320},{128,384},{192,448},{256,0},{320,64},{384,128},{4... | collective-permute-start | bytes 589832 | tf_op jit(solution)/shard_map/ppermute | solution.py:20
  31.5 11.2 %collective-permute-start.1 = (f32[32,128]{1,0:T(8,128)S(1)}, f32[32,128]{1,0:T(8,128)S(1)}, u32[]{:S(2)}, u32[]{:S(2)}) collective-permute-start(f32[32,128]{1,0:T(8,128)S(1)} %broadcast_in_dim.35), channel_id=1, source_target_pairs={{0,0},{4,8},{8,16},{12,24},{16,32},{20,40},{24,48},{28,56},{32,4},... | collective-permute-start | bytes 49160 | tf_op jit(solution)/shard_map/ppermute | solution.py:297
  47.7 45.2 %copy-start.18 = (bf16[16,6,16,128]{3,2,1,0:T(8,128)(2,1)S(1)}, bf16[16,6,16,128]{3,2,1,0:T(8,128)(2,1)}, u32[]{:S(2)}) copy-start(bf16[16,6,16,128]{3,2,1,0:T(8,128)(2,1)} %copy-done.17) | copy-start | bytes 1179652
  67.1 16.6 %collective-permute-start.3 = (bf16[768,128]{1,0:T(8,128)(2,1)}, bf16[768,128]{1,0:T(8,128)(2,1)S(1)}, u32[]{:S(2)}, u32[]{:S(2)}) collective-permute-start(bf16[768,128]{1,0:T(8,128)(2,1)} %get-tuple-element.53), channel_id=1, source_target_pairs={{0,128},{64,192},{128,0},{192,64},{256,384},{320,448},{384,256},{4... | collective-permute-start | bytes 589832 | tf_op jit(solution)/shard_map/ppermute | solution.py:20
  69.0 17.5 %all-to-all-start.2 = ((bf16[64,16,128]{2,1,0:T(8,128)(2,1)}), bf16[64,16,128]{2,1,0:T(8,128)(2,1)S(1)}, u32[]{:S(2)}, u32[]{:S(2)}) async-start(bf16[64,16,128]{2,1,0:T(8,128)(2,1)} %get-tuple-element.51), calls=%async_computation.2 | async-start | bytes 524288 | tf_op jit(solution)/shard_map/all_to_all | solution.py:278
  74.8 11.7 %collective-permute-start.2 = (bf16[16,2048]{1,0:T(8,128)(2,1)S(1)}, bf16[16,2048]{1,0:T(8,128)(2,1)S(1)}, u32[]{:S(2)}, u32[]{:S(2)}) collective-permute-start(bf16[16,2048]{1,0:T(8,128)(2,1)S(1)} %slice_bitcast_fusion.1.mine_rows), channel_id=1, source_target_pairs={{0,4},{4,0},{1,5},{5,1},{2,6},{6,2},{3,7},{7,3},{8,12},{12,8},{9,1... | collective-permute-start | bytes 196616 | tf_op jit(solution)/shard_map/ppermute | solution.py:24
  89.0 54.7 %copy-start.1 = (f32[768,16]{1,0:T(8,128)S(1)}, f32[768,16]{1,0:T(8,128)}, u32[]{:S(2)}) copy-start(f32[768,16]{1,0:T(8,128)} %copy-done) | copy-start | bytes 147460
  89.0 11.1 %all-to-all-start.3 = ((bf16[8,32,128]{2,1,0:T(8,128)(2,1)}), bf16[8,32,128]{2,1,0:T(8,128)(2,1)S(1)}, u32[]{:S(2)}, u32[]{:S(2)}) async-start(bf16[8,32,128]{2,1,0:T(8,128)(2,1)} %shard_map.68), calls=%async_computation.3 | async-start | bytes 131072 | tf_op jit(solution)/shard_map/all_to_all | solution.py:334
  93.6 16.1 %collective-permute-start.4 = (bf16[8,128,128]{2,1,0:T(8,128)(2,1)}, bf16[8,128,128]{2,1,0:T(8,128)(2,1)S(1)}, u32[]{:S(2)}, u32[]{:S(2)}) collective-permute-start(bf16[8,128,128]{2,1,0:T(8,128)(2,1)} %bitcast.42), channel_id=1, source_target_pairs={{0,4},{4,0},{1,5},{5,1},{2,6},{6,2},{3,7},{7,3},{8,12},{12,8},{9,1... | collective-permute-start | bytes 786440 | tf_op jit(solution)/shard_map/ppermute | solution.py:24
  101.0 15.8 %all-to-all-start.4 = ((bf16[16,16,128]{2,1,0:T(8,128)(2,1)}), bf16[16,16,128]{2,1,0:T(8,128)(2,1)S(1)}, u32[]{:S(2)}, u32[]{:S(2)}) async-start(bf16[16,16,128]{2,1,0:T(8,128)(2,1)} %bitcast.22), calls=%async_computation.4 | async-start | bytes 131072 | tf_op jit(solution)/shard_map/all_to_all | solution.py:337
  119.0 18.1 %all-to-all-start.5 = ((bf16[64,16,128]{2,1,0:T(8,128)(2,1)}), bf16[64,16,128]{2,1,0:T(8,128)(2,1)}, u32[]{:S(2)}, u32[]{:S(2)}) async-start(bf16[64,16,128]{2,1,0:T(8,128)(2,1)} %get-tuple-element.56), calls=%async_computation.5 | async-start | bytes 524288 | tf_op jit(solution)/shard_map/all_to_all | solution.py:278
  124.5 57.6 %all-gather.7.cloned.1.call-start = ((), (), s32[]{:S(2)}) async-start(), calls=%async_computation.12 | async-start | bytes 1114112 | tf_op jit(solution)/shard_map/all_gather | solution.py:360
  137.1 6.7 %collective-permute-start.5 = (bf16[8,128,128]{2,1,0:T(8,128)(2,1)}, bf16[8,128,128]{2,1,0:T(8,128)(2,1)}, u32[]{:S(2)}, u32[]{:S(2)}) collective-permute-start(bf16[8,128,128]{2,1,0:T(8,128)(2,1)} %bitcast.23.refs_2_), channel_id=1, source_target_pairs={{0,4},{4,0},{1,5},{5,1},{2,6},{6,2},{3,7},{7,3},{8,12},{12,8},{9,1... | collective-permute-start | bytes 786440 | tf_op jit(solution)/shard_map/ppermute | solution.py:24
  152.1 3.4 %collective-permute-start.6 = (bf16[8,128,128]{2,1,0:T(8,128)(2,1)S(1)}, bf16[8,128,128]{2,1,0:T(8,128)(2,1)S(1)}, u32[]{:S(2)}, u32[]{:S(2)}) collective-permute-start(bf16[8,128,128]{2,1,0:T(8,128)(2,1)S(1)} %get-tuple-element.63), channel_id=1, source_target_pairs={{0,4},{4,0},{1,5},{5,1},{2,6},{6,2},{3,7},{7,3},{8,12},{12,8},{9,1... | collective-permute-start | bytes 786440 | tf_op jit(solution)/shard_map/ppermute | solution.py:24
  156.3 25.8 %all-to-all-start.6 = ((bf16[64,16,128]{2,1,0:T(8,128)(2,1)}), bf16[64,16,128]{2,1,0:T(8,128)(2,1)}, u32[]{:S(2)}, u32[]{:S(2)}) async-start(bf16[64,16,128]{2,1,0:T(8,128)(2,1)} %bitcast.25), calls=%async_computation.6 | async-start | bytes 524288 | tf_op jit(solution)/shard_map/all_to_all | solution.py:275
  166.5 15.6 %collective-permute-start.8 = (bf16[8,128,128]{2,1,0:T(8,128)(2,1)S(1)}, bf16[8,128,128]{2,1,0:T(8,128)(2,1)S(1)}, u32[]{:S(2)}, u32[]{:S(2)}) collective-permute-start(bf16[8,128,128]{2,1,0:T(8,128)(2,1)S(1)} %get-tuple-element.66), channel_id=1, source_target_pairs={{0,4},{4,0},{1,5},{5,1},{2,6},{6,2},{3,7},{7,3},{8,12},{12,8},{9,1... | collective-permute-start | bytes 786440 | tf_op jit(solution)/shard_map/ppermute | solution.py:24
  168.7 13.3 %collective-permute-start.7 = (bf16[768,128]{1,0:T(8,128)(2,1)S(1)}, bf16[768,128]{1,0:T(8,128)(2,1)S(1)}, u32[]{:S(2)}, u32[]{:S(2)}) collective-permute-start(bf16[768,128]{1,0:T(8,128)(2,1)S(1)} %copy-done.15), channel_id=1, source_target_pairs={{0,128},{64,192},{128,0},{192,64},{256,384},{320,448},{384,256},{4... | collective-permute-start | bytes 589832 | tf_op jit(solution)/shard_map/ppermute | solution.py:20
  183.8 14.8 %all-to-all-start.7 = ((bf16[16,16,128]{2,1,0:T(8,128)(2,1)}), bf16[16,16,128]{2,1,0:T(8,128)(2,1)S(1)}, u32[]{:S(2)}, u32[]{:S(2)}) async-start(bf16[16,16,128]{2,1,0:T(8,128)(2,1)} %get-tuple-element.71), calls=%async_computation.7 | async-start | bytes 131072 | tf_op jit(solution)/shard_map/all_to_all | solution.py:386
  202.8 25.9 %all-to-all-start.8 = ((bf16[64,16,128]{2,1,0:T(8,128)(2,1)}), bf16[64,16,128]{2,1,0:T(8,128)(2,1)S(1)}, u32[]{:S(2)}, u32[]{:S(2)}) async-start(bf16[64,16,128]{2,1,0:T(8,128)(2,1)} %bitcast.27), calls=%async_computation.8 | async-start | bytes 524288 | tf_op jit(solution)/shard_map/all_to_all | solution.py:275
  213.7 15.1 %collective-permute-start.9 = (bf16[768,128]{1,0:T(8,128)(2,1)}, bf16[768,128]{1,0:T(8,128)(2,1)S(1)}, u32[]{:S(2)}, u32[]{:S(2)}) collective-permute-start(bf16[768,128]{1,0:T(8,128)(2,1)} %get-tuple-element.78), channel_id=1, source_target_pairs={{0,256},{64,320},{128,384},{192,448},{256,0},{320,64},{384,128},{4... | collective-permute-start | bytes 589832 | tf_op jit(solution)/shard_map/ppermute | solution.py:20
  231.1 13.2 %all-to-all-start.9 = ((bf16[8,16,128]{2,1,0:T(8,128)(2,1)}), bf16[8,16,128]{2,1,0:T(8,128)(2,1)S(1)}, u32[]{:S(2)}, u32[]{:S(2)}) async-start(bf16[8,16,128]{2,1,0:T(8,128)(2,1)} %get-tuple-element.81), calls=%async_computation.9 | async-start | bytes 65536 | tf_op jit(solution)/shard_map/all_to_all | solution.py:396
  (32 other events, 215.0 us)
Sparse Core Ops, SparseCore 0:
  9.5 50.3 all-gather.8
  64.9 42.2 all-gather.4
  137.2 36.4 all-gather.6

commit v4 on v3

--- a/solution.py
+++ b/solution.py
@@ -96,12 +96,18 @@
                 solved[start:start + half] = other[y]
 
 
-def first_update(core, panel, mine, other, value, got, base, solved):
-    @pl.when(pl.program_id(0) == 0)
-    def _():
-        assemble(core, mine, other, solved)
-
-    base[...] = value[...] + got[...].astype(F32) - dot(panel[...], solved[...])
+def pieces(band, quarters, rows, panel, left, right, opposite):
+    held = (panel[band], left[band], right[band], opposite[...])
+    return [(pl.ds(pl.multiple_of(quarters[i] * rows, rows), rows), v)
+            for i, v in enumerate(held)]
+
+
+def first_update(
+        core, quarters, panel, left, right, opposite, mine, other, value, got, base, solved):
+    assemble(core, mine, other, solved)
+    rows = opposite.shape[0]
+    for at, held in pieces(0, quarters, rows, panel, left, right, opposite):
+        base[at] = value[at] + got[at].astype(F32) - dot(held, solved[...])
 
 
 def split_term(core, acc, mine, away):
@@ -121,51 +127,32 @@
 
 
 def middle(
-        low, tile, core, panel, own, other, base, table, scaled, rounded, mine, away, acc, solved):
-    step = pl.program_id(0)
-
-    @pl.when(step == 0)
-    def _():
-        assemble(core, own, other, solved)
-
-    v = (base[...] - dot(panel[...], solved[...])) / column(table, PIV)
-    scaled[...] = v
-    row = lax.broadcasted_iota(jnp.int32, v.shape, 0) + step * tile
-    kept = jnp.where(row >= low, v, 0.0)
-    rounded[...] = kept.astype(BF)
-    add = dot(kept.T.astype(BF), panel[...])
-
-    @pl.when(step == 0)
-    def _():
-        acc[...] = add
-
-    @pl.when(step > 0)
-    def _():
-        acc[...] += add
-
-    @pl.when(step == pl.num_programs(0) - 1)
-    def _():
-        split_term(core, acc, mine, away)
-
-
-def first_term(core, panel, rounded, mine, away, acc):
-    step = pl.program_id(0)
-    add = dot(rounded[...].astype(F32).T.astype(BF), panel[...])
-
-    @pl.when(step == 0)
-    def _():
-        acc[...] = add
-
-    @pl.when(step > 0)
-    def _():
-        acc[...] += add
-
-    @pl.when(step == pl.num_programs(0) - 1)
-    def _():
-        split_term(core, acc, mine, away)
-
-
-def second_input(core, x1, mine_rows, other_rows, solved, spread, rows):
+        low, core, quarters, panel, left, right, opposite, own, other, base, table,
+        scaled, rounded, mine, away, acc, solved):
+    assemble(core, own, other, solved)
+    rows = opposite.shape[0]
+    parts = pieces(1, quarters, rows, panel, left, right, opposite)
+    for i, (at, held) in enumerate(parts):
+        v = (base[at] - dot(held, solved[...])) / table[at, PIV:PIV + 1]
+        scaled[at] = v
+        row = lax.broadcasted_iota(jnp.int32, v.shape, 0) + quarters[i] * rows
+        kept = jnp.where(row >= low, v, 0.0)
+        rounded[at] = kept.astype(BF)
+        add = dot(kept.T.astype(BF), held)
+        acc[...] = add if i == 0 else acc[...] + add
+    split_term(core, acc, mine, away)
+
+
+def first_term(core, quarters, panel, left, right, opposite, rounded, mine, away, acc):
+    rows = opposite.shape[0]
+    parts = pieces(0, quarters, rows, panel, left, right, opposite)
+    for i, (at, held) in enumerate(parts):
+        add = dot(rounded[at].astype(F32).T.astype(BF), held)
+        acc[...] = add if i == 0 else acc[...] + add
+    split_term(core, acc, mine, away)
+
+
+def second_input(core, x1, mine_rows, other_rows, solved, spread, cross, rows):
     ny, half, width = solved.shape
     rb = mine_rows.shape[0]
     first = jnp.where(core[0] == 0, 1.0, 0.0)
@@ -183,20 +170,24 @@
     v = first * x1[...]
     for y in range(ny):
         start = pl.multiple_of((2 * y + core[0]) * half, half)
-        v = v - dot(rows[:, pl.ds(start, half)], solved[y])
+        share = rows[:, pl.ds(start, half)]
+        cross[:, y * half:(y + 1) * half] = share
+        v = v - dot(share, solved[y])
     v = v.astype(BF)
     for y in range(ny):
         spread[y] = v
 
 
-def cross_back(core, tile, target, cross, term, away, back, out):
+def cross_back(core, tile, target, cross, term, away, back, out, turned):
     ny, half, _ = term.shape
-    v = dot(tile[...], target[...])
-    back[...] = v
-    turned = v.T.astype(BF)
+    back[...] = dot(tile[...], target[...])
+    low = back.shape[0] // ny
+    for k in range(ny):
+        at = pl.ds(pl.multiple_of((core[1] ^ k) * low, low), low)
+        turned[k * low:(k + 1) * low] = back[at]
+    v = turned[...].T.astype(BF)
     for y in range(ny):
-        start = pl.multiple_of((2 * y + core[0]) * half, half)
-        share = dot(turned, cross[:, pl.ds(start, half)]).T
+        share = dot(v, cross[:, y * half:(y + 1) * half]).T
         out[y] = (term[y] + away[y].astype(F32) + share).astype(BF)
 
 
@@ -269,7 +260,7 @@
     core, y = lax.axis_index("c"), lax.axis_index("y")
     outer, inner = ny // 2, ny // 4
     chunk = ny * 2 * rb
-    core_ref = core.astype(jnp.int32)[None]
+    core_ref = jnp.stack([core, y]).astype(jnp.int32)
 
     def reduce_yz(mine):
         return lax.all_to_all(mine.astype(BF).reshape(ny * nz, rb, width), ("y", "z"), 0, 0)
@@ -277,8 +268,12 @@
     def gather_yz(spread):
         return lax.all_to_all(spread, ("y", "z"), 0, 0).reshape(ny, half, width)
 
-    gathered0 = lax.all_gather(panels[0], "x", axis=0, tiled=True)
-
+    x, nx = lax.axis_index("x"), lax.axis_size("x")
+    forward = [(i, (i + 1) % nx) for i in range(nx)]
+    backward = [(i, (i - 1) % nx) for i in range(nx)]
+    from_left = lax.ppermute(panels, "x", forward)
+    from_right = lax.ppermute(panels, "x", backward)
+    quarters = jnp.stack([x, x + nx - 1, x + 1, x + 2]).astype(jnp.int32) % nx
     table = jnp.concatenate([left.reshape(4, rows), right.reshape(4, rows), pivots[None]], axis=0)
     table = jnp.pad(table, ((0, 7), (0, 0))).T
 
@@ -300,10 +295,8 @@
     shape = jax.ShapeDtypeStruct
     whole, sent = shape((rows, width), F32), shape((rows, width), BF)
     send = elementwise(left_send, sent, rhs, table)
+    arrived, send, own_pivots = lax.optimization_barrier((arrived, send, own_pivots))
     got = swap_y(send, outer, ny)
-    arrived, got, own_pivots = lax.optimization_barrier((arrived, got, own_pivots))
-    value, send = elementwise(left_middle, (whole, sent), rhs, got, table)
-    crossed = swap_y(send, inner, ny)
 
     small = arrived[:, 5].astype(F32)
     small = small[:, :, :32] + small[:, :, 32:64]
@@ -318,89 +311,96 @@
     x1 = lax.dynamic_slice_in_dim(x1, 2 * y, 2, 0).reshape(low, width)
 
     own0, spread = spread_sum(lax.all_to_all(part.reshape(nz, rb, width), "z", 0, 0), ny * nz)
-    spread, second = lax.optimization_barrier((spread, panels[1]))
-    gathered1 = lax.all_gather(second, "x", axis=0, tiled=True)
+    spread, from_left, from_right = lax.optimization_barrier((spread, from_left, from_right))
+    held = (panels, from_left, from_right)
+    opposite0 = lax.ppermute(from_left[0], "x", forward)
+    opposite1 = lax.ppermute(from_right[1], "x", backward)
     mine0 = gather_yz(spread)
-    mine0, crossed = lax.optimization_barrier((mine0, crossed))
+    mine0, got = lax.optimization_barrier((mine0, got))
+    value, send = elementwise(left_middle, (whole, sent), rhs, got, table)
+    crossed = swap_y(send, inner, ny)
 
     core_spec = pl.BlockSpec(memory_space=pltpu.SMEM)
     vmem = pl.BlockSpec(memory_space=pltpu.VMEM)
-    cross = gathered0[rb:low]
-    spread = pl.pallas_call(
-        second_input, out_shape=shape((ny, low, width), BF),
-        in_specs=[core_spec] + [vmem] * 4, out_specs=vmem,
+    cross = opposite0[rb:low]
+    for quarter, source in ((0, panels), (1, from_left), (nx - 1, from_right)):
+        cross = jnp.where(x == quarter, source[0, rb:low], cross)
+    spread, cross = pl.pallas_call(
+        second_input,
+        out_shape=(shape((ny, low, width), BF), shape((low, ny * half), BF)),
+        in_specs=[core_spec] + [vmem] * 4, out_specs=(vmem, vmem),
         scratch_shapes=[pltpu.VMEM((low, band), BF)],
     )(core_ref, x1, cross, swap_core(cross), mine0)
     x1 = lax.all_to_all(spread, "y", 0, 0).reshape(chunk, width)
+    def doubled(v, bit):
+        return jnp.concatenate([v, swap_y(v, bit, ny)], axis=0)
+
+    cross = doubled(cross, 1)
     other0 = swap_core(mine0)
     part = down(tile1, x1).astype(BF).reshape(2 * nz, rb, width)
     met = lax.all_to_all(part, ("c", "z"), 0, 0)
-    met, other0 = lax.optimization_barrier((met, other0))
+    met, other0, cross, crossed = lax.optimization_barrier((met, other0, cross, crossed))
     own1, spread = spread_sum(met, ny * nz)
 
-    tile = rows // 3
-    steps = rows // tile
-    panel_spec = pl.BlockSpec((tile, band), lambda i: (i, 0))
-    row_spec = pl.BlockSpec((tile, width), lambda i: (i, 0))
-    table_spec = pl.BlockSpec((tile, 16), lambda i: (i, 0))
-    half_spec = pl.BlockSpec((ny, half, width), lambda i: (0, 0, 0))
     params = pltpu.CompilerParams(vmem_limit_bytes=40 * 2 ** 20)
     cost = pl.CostEstimate(
         flops=2 * rows * band * width, bytes_accessed=2 * rows * band, transcendentals=0)
     solved_ref = pltpu.VMEM((band, width), BF)
     base = pl.pallas_call(
-        first_update, out_shape=whole, grid=(steps,),
-        in_specs=[core_spec, panel_spec, half_spec, half_spec, row_spec, row_spec],
-        out_specs=row_spec, scratch_shapes=[solved_ref],
+        first_update, out_shape=whole,
+        in_specs=[core_spec] * 2 + [vmem] * 8, out_specs=vmem, scratch_shapes=[solved_ref],
         compiler_params=params, cost_estimate=cost,
-    )(core_ref, gathered0, mine0, other0, value, crossed)
+    )(core_ref, quarters, *held, opposite0, mine0, other0, value, crossed)
 
     mine1 = gather_yz(spread)
-    mine1, base, cross = lax.optimization_barrier((mine1, base, cross))
-    cross = lax.all_gather(cross, ("y", "c"), axis=0, tiled=True)
+    cross = doubled(cross, 2)
+    mine1, base, opposite1, cross = lax.optimization_barrier((mine1, base, opposite1, cross))
     other1 = swap_core(mine1)
     halves = (shape((ny, half, width), F32), shape((ny, half, width), BF))
     scaled, rounded, term1, away1 = pl.pallas_call(
-        lambda *refs: middle(low, tile, *refs),
-        out_shape=(whole, sent) + halves, grid=(steps,),
-        in_specs=[core_spec, panel_spec, half_spec, half_spec, row_spec, table_spec],
-        out_specs=(row_spec, row_spec, half_spec, half_spec),
+        lambda *refs: middle(low, *refs),
+        out_shape=(whole, sent) + halves,
+        in_specs=[core_spec] * 2 + [vmem] * 8, out_specs=(vmem,) * 4,
         scratch_shapes=[pltpu.VMEM((width, band), F32), solved_ref],
         compiler_params=params, cost_estimate=cost,
-    )(core_ref, gathered1, mine1, other1, base, table)
+    )(core_ref, quarters, *held, opposite1, mine1, other1, base, table)
     met = reduce_yz(term1 + swap_core(away1).astype(F32))
 
-    got = swap_y(rounded, inner, ny)
     term0, away0 = pl.pallas_call(
-        first_term, out_shape=halves, grid=(steps,),
-        in_specs=[core_spec, panel_spec, row_spec], out_specs=(half_spec, half_spec),
+        first_term, out_shape=halves,
+        in_specs=[core_spec] * 2 + [vmem] * 5, out_specs=(vmem,) * 2,
         scratch_shapes=[pltpu.VMEM((width, band), F32)],
         compiler_params=params, cost_estimate=cost,
-    )(core_ref, gathered0, rounded)
+    )(core_ref, quarters, *held, opposite0, rounded)
     away0 = swap_core(away0)
-    met, got, term0, away0, cross = lax.optimization_barrier((met, got, term0, away0, cross))
+    if ny > 4:
+        cross = doubled(cross, 4)
+    met, rounded, term0, away0, cross = lax.optimization_barrier(
+        (met, rounded, term0, away0, cross))
     _, spread = spread_sum(met, 2 * nz, own1, own_pivots[rb:])
 
-    value, send = elementwise(right_middle, (whole, sent), scaled, got, table)
-    got = swap_y(send, outer, ny)
+    got = swap_y(rounded, inner, ny)
     t1 = lax.all_to_all(spread, ("c", "z"), 0, 0).reshape(2 * half, width)
+    t1, got = lax.optimization_barrier((t1, got))
     back1, term0 = pl.pallas_call(
         cross_back, out_shape=(shape((chunk, width), F32), shape((ny, half, width), BF)),
         in_specs=[core_spec] + [vmem] * 5, out_specs=(vmem, vmem),
-        compiler_params=params,
+        scratch_shapes=[pltpu.VMEM((chunk, width), F32)], compiler_params=params,
     )(core_ref, tile1, t1, cross, term0, away0)
     met = reduce_yz(term0)
-    met, got = lax.optimization_barrier((met, got))
+    value, send = elementwise(right_middle, (whole, sent), scaled, got, table)
+    met, send = lax.optimization_barrier((met, send))
     _, spread = spread_sum(met, nz, own0, own_pivots[:rb])
+    t0 = lax.all_to_all(spread, "z", 0, 0).reshape(half, width)
+    t0, got = lax.optimization_barrier((t0, swap_y(send, outer, ny)))
     out = elementwise(right_end, whole, value, got, table)
-    t0 = lax.all_to_all(spread, "z", 0, 0).reshape(half, width)
-    t0, out = lax.optimization_barrier((t0, out))
     last = pl.pallas_call(
         lambda *refs: end_bands(ny, outer, inner, *refs),
         out_shape=shape((ny * 2, low, width), BF),
         in_specs=[core_spec] + [vmem] * 4, out_specs=vmem,
     )(core_ref, small, tile0, t0, back1)
-    head = total(lax.all_to_all(last, ("y", "c"), 0, 0))
+    met, out = lax.optimization_barrier((lax.all_to_all(last, ("y", "c"), 0, 0), out))
+    head = total(met)
     return lax.dynamic_update_slice(out, head, (0, 0))
 
 

time: 275 us -> 286 us (1.040)
  starting transfers between devices: 103 us -> 123 us
  between operations: 13.6 us -> 0.52 us
  blocking collectives: 33.7 us -> 27.1 us
  other arithmetic: 3.41 us -> 9.85 us
  local copies, waits for them, and re-layouts: 23.2 us -> 28 us
  waiting for transfers between devices: 62.1 us -> 58.7 us
    ppermute x4 -> x7, waiting for transfers between devices: 22.1 us -> 8.09 us  [swap_y(): return lax.ppermute(v, 'y', [(i, i ^ bit) for i in range(count)])]
    ppermute x0 -> x4, starting transfers between devices: none -> 13.4 us  [the longest x1 5.34 us: shards(): from_right = lax.ppermute(panels, 'x', backward)]
    all_to_all x2, waiting for transfers between devices: 0.01 us -> 10.5 us  [reduce_yz(): lax.all_to_all(mine.astype(BF).reshape(ny * nz, rb, width), ('y', 'z'), 0...]
    all_to_all x2, waiting for transfers between devices: 9.23 us -> 0.01 us  [gather_yz(): return lax.all_to_all(spread, ('y', 'z'), 0, 0).reshape(ny, half, width)]
    ppermute x0 -> x4, waiting for transfers between devices: none -> 8.58 us  [the longest x1 8.58 us: shards(): opposite0 = lax.ppermute(from_left[0], 'x', forward)]
    all_to_all x1, blocking collectives: 18.3 us -> 10.9 us  [shards(): t0 = lax.all_to_all(spread, 'z', 0, 0).reshape(half, width)]
    ppermute x4 -> x7, starting transfers between devices: 20.1 us -> 27.3 us  [swap_y(): return lax.ppermute(v, 'y', [(i, i ^ bit) for i in range(count)])]
    all_to_all x1, starting transfers between devices: 8.62 us -> 3.89 us  [shards(): met = lax.all_to_all(part, ('c', 'z'), 0, 0)]
  transfers between devices with their start and end apart: 22 -> 26, of which waited for: 13 -> 11; matrix products, arithmetic and copies ran while one was open for 3% -> 9% of each run, Pallas kernels for 9% -> 8%
where the time goes in v4:
time: 286 us; the launch traced here: 284 us
  starting transfers between devices  123 us (43%)
  waiting for transfers between devices  58.7 us (21%)
  Pallas kernels  34.8 us (12%)
  local copies, waits for them, and re-layouts  28 us (10%)
  blocking collectives  27.1 us (9%)
  other arithmetic  9.85 us (3%)
    ppermute x7, starting transfers between devices, swap_y(): return lax.ppermute(v, 'y', [(i, i ^ bit) for i in range(count)])  27.3 us
    all_to_all x2, starting transfers between devices, reduce_yz(): lax.all_to_all(mine.astype(BF).reshape(ny * nz, rb, width), ('y', 'z'), 0...  16.8 us
    ppermute x5, starting transfers between devices, swap_core(): return lax.ppermute(v, 'c', [(0, 1), (1, 0)])  16.4 us
    all_to_all x1, blocking collectives, shards(): lax.all_to_all(part.reshape(nz, rb, width), 'z', 0, 0)  16.2 us
    all_to_all x2, starting transfers between devices, gather_yz(): return lax.all_to_all(spread, ('y', 'z'), 0, 0).reshape(ny, half, width)  13.1 us
    unnamed x58, local copies, waits for them, and re-layouts  11 us
    all_to_all x1, blocking collectives, shards(): t0 = lax.all_to_all(spread, 'z', 0, 0).reshape(half, width)  10.9 us
    all_to_all x2, waiting for transfers between devices, reduce_yz(): lax.all_to_all(mine.astype(BF).reshape(ny * nz, rb, width), ('y', 'z'), 0...  10.5 us
  transfers between devices with their start and end apart: 26, of which 11 were waited for; matrix products, arithmetic and copies ran while one was open for 9% of the time, Pallas kernels for 8%

profile of v4, /device:TPU:1, one launch (start us, length us, event | category | flops | bytes accessed | tf_op | source)
XLA Modules:
  0.0 283.7 jit_solution(8792806987873425788)
XLA Ops:
  0.0 5.3 %collective-permute-start.2 = (bf16[2,192,2048]{2,1,0:T(8,128)(2,1)}, bf16[2,192,2048]{2,1,0:T(8,128)(2,1)S(1)}, u32[]{:S(2)}, u32[]{:S(2)}) collective-permute-start(bf16[2,192,2048]{2,1,0:T(8,128)(2,1)} %panel.3), channel_id=1, source_target_pairs={{0,3},{1,0},{2,1},{3,2},{4,7},{5,4},{6,5},{7,6},{8,11},{9,8},{10,9... | collective-permute-start | bytes 4718600 | tf_op jit(solution)/shard_map/ppermute | solution.py:275
  19.1 9.5 %all-to-all-start = ((bf16[16,6,16,128]{3,2,1,0:T(8,128)(2,1)}), bf16[16,6,16,128]{3,2,1,0:T(8,128)(2,1)}, u32[]{:S(2)}, u32[]{:S(2)}) async-start(bf16[16,6,16,128]{3,2,1,0:T(8,128)(2,1)} %pad_maximum_fusion.1), calls=%async_computation | async-start | bytes 786432 | tf_op jit(solution)/shard_map/all_to_all | solution.py:289
  34.0 6.3 %collective-permute-done = f32[32,128]{1,0:T(8,128)S(1)} collective-permute-done((f32[32,128]{1,0:T(8,128)}, f32[32,128]{1,0:T(8,128)S(1)}, u32[]{:S(2)}, u32[]{:S(2)}) %collective-permute-start) | collective-permute-done | bytes 16416 | tf_op jit(solution)/shard_map/ppermute | solution.py:292
  47.1 16.2 %all_to_all.55.refs_0_ = bf16[8,16,128]{2,1,0:T(8,128)(2,1)} all-to-all(bf16[8,16,128]{2,1,0:T(8,128)(2,1)} %bitcast.67), channel_id=1, replica_groups=mesh['y'=8,'z'=8,'c'=2,'x'=4] {'z'}, dimensions={0} | all-to-all | bytes 65536 | tf_op jit(solution)/shard_map/all_to_all | solution.py:313
  72.6 7.3 %all-to-all-start.2 = ((bf16[64,16,128]{2,1,0:T(8,128)(2,1)}), bf16[64,16,128]{2,1,0:T(8,128)(2,1)S(1)}, u32[]{:S(2)}, u32[]{:S(2)}) async-start(bf16[64,16,128]{2,1,0:T(8,128)(2,1)} %get-tuple-element.62), calls=%async_computation.2 | async-start | bytes 524288 | tf_op jit(solution)/shard_map/all_to_all | solution.py:269
  79.9 8.6 %collective-permute-done.3.opposite = bf16[192,2048]{1,0:T(8,128)(2,1)} collective-permute-done((bf16[192,2048]{1,0:T(8,128)(2,1)}, bf16[192,2048]{1,0:T(8,128)(2,1)}, u32[]{:S(2)}, u32[]{:S(2)}) %collective-permute-start.3) | collective-permute-done | bytes 786464 | tf_op jit(solution)/shard_map/ppermute | solution.py:316
  96.1 4.1 %all-to-all-start.3 = ((bf16[8,32,128]{2,1,0:T(8,128)(2,1)}), bf16[8,32,128]{2,1,0:T(8,128)(2,1)}, u32[]{:S(2)}, u32[]{:S(2)}) async-start(bf16[8,32,128]{2,1,0:T(8,128)(2,1)} %get-tuple-element.65), calls=%async_computation.3 | async-start | bytes 131072 | tf_op jit(solution)/shard_map/all_to_all | solution.py:334
  105.0 5.1 %collective-permute-start.6 = (bf16[8,128,128]{2,1,0:T(8,128)(2,1)S(1)}, bf16[8,128,128]{2,1,0:T(8,128)(2,1)}, u32[]{:S(2)}, u32[]{:S(2)}) collective-permute-start(bf16[8,128,128]{2,1,0:T(8,128)(2,1)S(1)} %bitcast.50), channel_id=1, source_target_pairs={{0,4},{4,0},{1,5},{5,1},{2,6},{6,2},{3,7},{7,3},{8,12},{12,8},{9,1... | collective-permute-start | bytes 786440 | tf_op jit(solution)/shard_map/ppermute | solution.py:24
  112.4 4.4 %collective-permute-start.8 = (bf16[768,128]{1,0:T(8,128)(2,1)}, bf16[768,128]{1,0:T(8,128)(2,1)}, u32[]{:S(2)}, u32[]{:S(2)}) collective-permute-start(bf16[768,128]{1,0:T(8,128)(2,1)} %get-tuple-element.68), channel_id=1, source_target_pairs={{0,128},{64,192},{128,0},{192,64},{256,384},{320,448},{384,256},{4... | collective-permute-start | bytes 589832 | tf_op jit(solution)/shard_map/ppermute | solution.py:20
  121.6 3.9 %all-to-all-start.4 = ((bf16[16,16,128]{2,1,0:T(8,128)(2,1)}), bf16[16,16,128]{2,1,0:T(8,128)(2,1)S(1)}, u32[]{:S(2)}, u32[]{:S(2)}) async-start(bf16[16,16,128]{2,1,0:T(8,128)(2,1)} %bitcast.64), calls=%async_computation.4 | async-start | bytes 131072 | tf_op jit(solution)/shard_map/all_to_all | solution.py:341
  127.1 5.6 %all-to-all-done.4.refs_0_ = bf16[16,16,128]{2,1,0:T(8,128)(2,1)S(1)} async-done(((bf16[16,16,128]{2,1,0:T(8,128)(2,1)}), bf16[16,16,128]{2,1,0:T(8,128)(2,1)S(1)}, u32[]{:S(2)}, u32[]{:S(2)}) %all-to-all-start.4) | async-done | bytes 65568 | tf_op jit(solution)/shard_map/all_to_all | solution.py:341
  134.9 5.8 %all-to-all-start.5 = ((bf16[64,16,128]{2,1,0:T(8,128)(2,1)}), bf16[64,16,128]{2,1,0:T(8,128)(2,1)}, u32[]{:S(2)}, u32[]{:S(2)}) async-start(bf16[64,16,128]{2,1,0:T(8,128)(2,1)} %get-tuple-element.70), calls=%async_computation.5 | async-start | bytes 524288 | tf_op jit(solution)/shard_map/all_to_all | solution.py:269
  162.6 5.2 %shard_map.71 = (f32[768,128]{1,0:T(8,128)S(1)}, bf16[768,128]{1,0:T(8,128)(2,1)S(1)}, f32[8,128,128]{2,1,0:T(8,128)S(1)}, bf16[8,128,128]{2,1,0:T(8,128)(2,1)S(1)}) custom-call(s32[2]{0:T(128)S(1)} %copy-done.18, s32[4]{0:T(128)S(1)} %and_select_fusion.quarters.refs_1_, bf16[2,192,2048]{2,1,0:T(8,128)(2,1)S(1)} %copy-done.3, ...), custom_call_target="tpu_custom_call" | custom-call | flops 402653184 | bytes 3145728 | tf_op jit(solution)/shard_map/pallas_call | solution.py:360
  172.1 10.7 %all-to-all-start.6 = ((bf16[64,16,128]{2,1,0:T(8,128)(2,1)}), bf16[64,16,128]{2,1,0:T(8,128)(2,1)}, u32[]{:S(2)}, u32[]{:S(2)}) async-start(bf16[64,16,128]{2,1,0:T(8,128)(2,1)} %bitcast.33), calls=%async_computation.6 | async-start | bytes 524288 | tf_op jit(solution)/shard_map/all_to_all | solution.py:266
  182.8 6.9 %collective-permute-start.14 = (bf16[128,1024]{1,0:T(8,128)(2,1)}, bf16[128,1024]{1,0:T(8,128)(2,1)S(1)}, u32[]{:S(2)}, u32[]{:S(2)}) collective-permute-start(bf16[128,1024]{1,0:T(8,128)(2,1)} %pad_maximum_fusion.2), channel_id=1, source_target_pairs={{0,256},{64,320},{128,384},{192,448},{256,0},{320,64},{384,128},{4... | collective-permute-start | bytes 786440 | tf_op jit(solution)/shard_map/ppermute | solution.py:20
  199.7 5.0 %collective-permute-done.14 = bf16[128,1024]{1,0:T(8,128)(2,1)S(1)} collective-permute-done((bf16[128,1024]{1,0:T(8,128)(2,1)}, bf16[128,1024]{1,0:T(8,128)(2,1)S(1)}, u32[]{:S(2)}, u32[]{:S(2)}) %collective-permute-start.14) | collective-permute-done | bytes 262176 | tf_op jit(solution)/shard_map/ppermute | solution.py:20
  209.9 7.9 %all-to-all-start.7 = ((bf16[16,16,128]{2,1,0:T(8,128)(2,1)}), bf16[16,16,128]{2,1,0:T(8,128)(2,1)S(1)}, u32[]{:S(2)}, u32[]{:S(2)}) async-start(bf16[16,16,128]{2,1,0:T(8,128)(2,1)} %get-tuple-element.87), calls=%async_computation.7 | async-start | bytes 131072 | tf_op jit(solution)/shard_map/all_to_all | solution.py:383
  217.8 7.1 %all-to-all-done.7 = bf16[16,16,128]{2,1,0:T(8,128)(2,1)S(1)} async-done(((bf16[16,16,128]{2,1,0:T(8,128)(2,1)}), bf16[16,16,128]{2,1,0:T(8,128)(2,1)S(1)}, u32[]{:S(2)}, u32[]{:S(2)}) %all-to-all-start.7) | async-done | bytes 65568 | tf_op jit(solution)/shard_map/all_to_all | solution.py:383
  226.9 6.1 %all-to-all-start.8 = ((bf16[64,16,128]{2,1,0:T(8,128)(2,1)}), bf16[64,16,128]{2,1,0:T(8,128)(2,1)S(1)}, u32[]{:S(2)}, u32[]{:S(2)}) async-start(bf16[64,16,128]{2,1,0:T(8,128)(2,1)} %bitcast.35), calls=%async_computation.8 | async-start | bytes 524288 | tf_op jit(solution)/shard_map/all_to_all | solution.py:266
  235.4 10.5 %all-to-all-done.8.refs_0_ = bf16[64,16,128]{2,1,0:T(8,128)(2,1)S(1)} async-done(((bf16[64,16,128]{2,1,0:T(8,128)(2,1)}), bf16[64,16,128]{2,1,0:T(8,128)(2,1)S(1)}, u32[]{:S(2)}, u32[]{:S(2)}) %all-to-all-start.8) | async-done | bytes 262176 | tf_op jit(solution)/shard_map/all_to_all | solution.py:266
  245.9 5.0 %collective-permute-start.16 = (bf16[768,128]{1,0:T(8,128)(2,1)}, bf16[768,128]{1,0:T(8,128)(2,1)S(1)}, u32[]{:S(2)}, u32[]{:S(2)}) collective-permute-start(bf16[768,128]{1,0:T(8,128)(2,1)} %get-tuple-element.100), channel_id=1, source_target_pairs={{0,256},{64,320},{128,384},{192,448},{256,0},{320,64},{384,128},{4... | collective-permute-start | bytes 589832 | tf_op jit(solution)/shard_map/ppermute | solution.py:20
  252.5 10.9 %all_to_all.56 = bf16[8,16,128]{2,1,0:T(8,128)(2,1)} all-to-all(bf16[8,16,128]{2,1,0:T(8,128)(2,1)} %get-tuple-element.99), channel_id=1, replica_groups=mesh['y'=8,'z'=8,'c'=2,'x'=4] {'z'}, dimensions={0} | all-to-all | bytes 65536 | tf_op jit(solution)/shard_map/all_to_all | solution.py:394
  265.6 8.2 %all-to-all-start.10 = ((bf16[16,32,128]{2,1,0:T(8,128)(2,1)}), bf16[16,32,128]{2,1,0:T(8,128)(2,1)S(1)}, u32[]{:S(2)}, u32[]{:S(2)}) async-start(bf16[16,32,128]{2,1,0:T(8,128)(2,1)} %shard_map.77), calls=%async_computation.10 | async-start | bytes 262144 | tf_op jit(solution)/shard_map/all_to_all | solution.py:402
  276.0 7.0 %all-to-all-done.10 = bf16[16,32,128]{2,1,0:T(8,128)(2,1)S(1)} async-done(((bf16[16,32,128]{2,1,0:T(8,128)(2,1)}), bf16[16,32,128]{2,1,0:T(8,128)(2,1)S(1)}, u32[]{:S(2)}, u32[]{:S(2)}) %all-to-all-start.10) | async-done | bytes 131104 | tf_op jit(solution)/shard_map/all_to_all | solution.py:402
  (145 shorter events, 110.5 us)
Async XLA Ops:
  0.0 64.7 %collective-permute-start.2 = (bf16[2,192,2048]{2,1,0:T(8,128)(2,1)}, bf16[2,192,2048]{2,1,0:T(8,128)(2,1)S(1)}, u32[]{:S(2)}, u32[]{:S(2)}) collective-permute-start(bf16[2,192,2048]{2,1,0:T(8,128)(2,1)} %panel.3), channel_id=1, source_target_pairs={{0,3},{1,0},{2,1},{3,2},{4,7},{5,4},{6,5},{7,6},{8,11},{9,8},{10,9... | collective-permute-start | bytes 4718600 | tf_op jit(solution)/shard_map/ppermute | solution.py:275
  5.3 59.4 %collective-permute-start.1 = (bf16[2,192,2048]{2,1,0:T(8,128)(2,1)}, bf16[2,192,2048]{2,1,0:T(8,128)(2,1)S(1)}, u32[]{:S(2)}, u32[]{:S(2)}) collective-permute-start(bf16[2,192,2048]{2,1,0:T(8,128)(2,1)} %panel.3), channel_id=1, source_target_pairs={{0,1},{1,2},{2,3},{3,0},{4,5},{5,6},{6,7},{7,4},{8,9},{9,10},{10,1... | collective-permute-start | bytes 4718600 | tf_op jit(solution)/shard_map/ppermute | solution.py:274
  19.1 24.2 %all-to-all-start = ((bf16[16,6,16,128]{3,2,1,0:T(8,128)(2,1)}), bf16[16,6,16,128]{3,2,1,0:T(8,128)(2,1)}, u32[]{:S(2)}, u32[]{:S(2)}) async-start(bf16[16,6,16,128]{3,2,1,0:T(8,128)(2,1)} %pad_maximum_fusion.1), calls=%async_computation | async-start | bytes 786432 | tf_op jit(solution)/shard_map/all_to_all | solution.py:289
  29.5 10.8 %collective-permute-start = (f32[32,128]{1,0:T(8,128)}, f32[32,128]{1,0:T(8,128)S(1)}, u32[]{:S(2)}, u32[]{:S(2)}) collective-permute-start(f32[32,128]{1,0:T(8,128)} %broadcast_in_dim.31), channel_id=1, source_target_pairs={{0,0},{4,8},{8,16},{12,24},{16,32},{20,40},{24,48},{28,56},{32,4},... | collective-permute-start | bytes 49160 | tf_op jit(solution)/shard_map/ppermute | solution.py:292
  65.7 22.7 %collective-permute-start.3 = (bf16[192,2048]{1,0:T(8,128)(2,1)}, bf16[192,2048]{1,0:T(8,128)(2,1)}, u32[]{:S(2)}, u32[]{:S(2)}) collective-permute-start(bf16[192,2048]{1,0:T(8,128)(2,1)} %slice_bitcast_fusion.1), channel_id=1, source_target_pairs={{0,1},{1,2},{2,3},{3,0},{4,5},{5,6},{6,7},{7,4},{8,9},{9,10},{10,1... | collective-permute-start | bytes 2359304 | tf_op jit(solution)/shard_map/ppermute | solution.py:316
  68.7 24.8 %collective-permute-start.5 = (bf16[768,128]{1,0:T(8,128)(2,1)}, bf16[768,128]{1,0:T(8,128)(2,1)}, u32[]{:S(2)}, u32[]{:S(2)}) collective-permute-start(bf16[768,128]{1,0:T(8,128)(2,1)} %shard_map.64), channel_id=1, source_target_pairs={{0,256},{64,320},{128,384},{192,448},{256,0},{320,64},{384,128},{4... | collective-permute-start | bytes 589832 | tf_op jit(solution)/shard_map/ppermute | solution.py:20
  72.6 20.9 %all-to-all-start.2 = ((bf16[64,16,128]{2,1,0:T(8,128)(2,1)}), bf16[64,16,128]{2,1,0:T(8,128)(2,1)S(1)}, u32[]{:S(2)}, u32[]{:S(2)}) async-start(bf16[64,16,128]{2,1,0:T(8,128)(2,1)} %get-tuple-element.62), calls=%async_computation.2 | async-start | bytes 524288 | tf_op jit(solution)/shard_map/all_to_all | solution.py:269
  96.1 23.8 %all-to-all-start.3 = ((bf16[8,32,128]{2,1,0:T(8,128)(2,1)}), bf16[8,32,128]{2,1,0:T(8,128)(2,1)}, u32[]{:S(2)}, u32[]{:S(2)}) async-start(bf16[8,32,128]{2,1,0:T(8,128)(2,1)} %get-tuple-element.65), calls=%async_computation.3 | async-start | bytes 131072 | tf_op jit(solution)/shard_map/all_to_all | solution.py:334
  101.2 54.7 %collective-permute-start.9 = (bf16[192,2048]{1,0:T(8,128)(2,1)}, bf16[192,2048]{1,0:T(8,128)(2,1)}, u32[]{:S(2)}, u32[]{:S(2)}) collective-permute-start(bf16[192,2048]{1,0:T(8,128)(2,1)} %slice_bitcast_fusion), channel_id=1, source_target_pairs={{0,3},{1,0},{2,1},{3,2},{4,7},{5,4},{6,5},{7,6},{8,11},{9,8},{10,9... | collective-permute-start | bytes 2359304 | tf_op jit(solution)/shard_map/ppermute | solution.py:317
  105.0 22.1 %collective-permute-start.6 = (bf16[8,128,128]{2,1,0:T(8,128)(2,1)S(1)}, bf16[8,128,128]{2,1,0:T(8,128)(2,1)}, u32[]{:S(2)}, u32[]{:S(2)}) collective-permute-start(bf16[8,128,128]{2,1,0:T(8,128)(2,1)S(1)} %bitcast.50), channel_id=1, source_target_pairs={{0,4},{4,0},{1,5},{5,1},{2,6},{6,2},{3,7},{7,3},{8,12},{12,8},{9,1... | collective-permute-start | bytes 786440 | tf_op jit(solution)/shard_map/ppermute | solution.py:24
  112.4 14.7 %collective-permute-start.8 = (bf16[768,128]{1,0:T(8,128)(2,1)}, bf16[768,128]{1,0:T(8,128)(2,1)}, u32[]{:S(2)}, u32[]{:S(2)}) collective-permute-start(bf16[768,128]{1,0:T(8,128)(2,1)} %get-tuple-element.68), channel_id=1, source_target_pairs={{0,128},{64,192},{128,0},{192,64},{256,384},{320,448},{384,256},{4... | collective-permute-start | bytes 589832 | tf_op jit(solution)/shard_map/ppermute | solution.py:20
  116.8 8.7 %collective-permute-start.7 = (bf16[32,1024]{1,0:T(8,128)(2,1)}, bf16[32,1024]{1,0:T(8,128)(2,1)}, u32[]{:S(2)}, u32[]{:S(2)}) collective-permute-start(bf16[32,1024]{1,0:T(8,128)(2,1)} %get-tuple-element.66), channel_id=1, source_target_pairs={{0,64},{64,0},{128,192},{192,128},{256,320},{320,256},{384,448},{4... | collective-permute-start | bytes 196616 | tf_op jit(solution)/shard_map/ppermute | solution.py:20
  121.6 11.1 %all-to-all-start.4 = ((bf16[16,16,128]{2,1,0:T(8,128)(2,1)}), bf16[16,16,128]{2,1,0:T(8,128)(2,1)S(1)}, u32[]{:S(2)}, u32[]{:S(2)}) async-start(bf16[16,16,128]{2,1,0:T(8,128)(2,1)} %bitcast.64), calls=%async_computation.4 | async-start | bytes 131072 | tf_op jit(solution)/shard_map/all_to_all | solution.py:341
  134.9 21.0 %all-to-all-start.5 = ((bf16[64,16,128]{2,1,0:T(8,128)(2,1)}), bf16[64,16,128]{2,1,0:T(8,128)(2,1)}, u32[]{:S(2)}, u32[]{:S(2)}) async-start(bf16[64,16,128]{2,1,0:T(8,128)(2,1)} %get-tuple-element.70), calls=%async_computation.5 | async-start | bytes 524288 | tf_op jit(solution)/shard_map/all_to_all | solution.py:269
  140.8 13.5 %collective-permute-start.10 = (bf16[64,1024]{1,0:T(8,128)(2,1)}, bf16[64,1024]{1,0:T(8,128)(2,1)S(1)}, u32[]{:S(2)}, u32[]{:S(2)}) collective-permute-start(bf16[64,1024]{1,0:T(8,128)(2,1)} %pad_maximum_fusion.4), channel_id=1, source_target_pairs={{0,128},{64,192},{128,0},{192,64},{256,384},{320,448},{384,256},{4... | collective-permute-start | bytes 393224 | tf_op jit(solution)/shard_map/ppermute | solution.py:20
  155.9 4.3 %collective-permute-start.11 = (bf16[8,128,128]{2,1,0:T(8,128)(2,1)}, bf16[8,128,128]{2,1,0:T(8,128)(2,1)S(1)}, u32[]{:S(2)}, u32[]{:S(2)}) collective-permute-start(bf16[8,128,128]{2,1,0:T(8,128)(2,1)} %bitcast.31.refs_6_), channel_id=1, source_target_pairs={{0,4},{4,0},{1,5},{5,1},{2,6},{6,2},{3,7},{7,3},{8,12},{12,8},{9,1... | collective-permute-start | bytes 786440 | tf_op jit(solution)/shard_map/ppermute | solution.py:24
  172.1 33.6 %all-to-all-start.6 = ((bf16[64,16,128]{2,1,0:T(8,128)(2,1)}), bf16[64,16,128]{2,1,0:T(8,128)(2,1)}, u32[]{:S(2)}, u32[]{:S(2)}) async-start(bf16[64,16,128]{2,1,0:T(8,128)(2,1)} %bitcast.33), calls=%async_computation.6 | async-start | bytes 524288 | tf_op jit(solution)/shard_map/all_to_all | solution.py:266
  182.8 21.9 %collective-permute-start.14 = (bf16[128,1024]{1,0:T(8,128)(2,1)}, bf16[128,1024]{1,0:T(8,128)(2,1)S(1)}, u32[]{:S(2)}, u32[]{:S(2)}) collective-permute-start(bf16[128,1024]{1,0:T(8,128)(2,1)} %pad_maximum_fusion.2), channel_id=1, source_target_pairs={{0,256},{64,320},{128,384},{192,448},{256,0},{320,64},{384,128},{4... | collective-permute-start | bytes 786440 | tf_op jit(solution)/shard_map/ppermute | solution.py:20
  196.5 9.2 %collective-permute-start.13 = (bf16[8,128,128]{2,1,0:T(8,128)(2,1)S(1)}, bf16[8,128,128]{2,1,0:T(8,128)(2,1)S(1)}, u32[]{:S(2)}, u32[]{:S(2)}) collective-permute-start(bf16[8,128,128]{2,1,0:T(8,128)(2,1)S(1)} %get-tuple-element.82), channel_id=1, source_target_pairs={{0,4},{4,0},{1,5},{5,1},{2,6},{6,2},{3,7},{7,3},{8,12},{12,8},{9,1... | collective-permute-start | bytes 786440 | tf_op jit(solution)/shard_map/ppermute | solution.py:24
  205.7 19.3 %collective-permute-start.15 = (bf16[768,128]{1,0:T(8,128)(2,1)S(1)}, bf16[768,128]{1,0:T(8,128)(2,1)S(1)}, u32[]{:S(2)}, u32[]{:S(2)}) collective-permute-start(bf16[768,128]{1,0:T(8,128)(2,1)S(1)} %copy-done.16), channel_id=1, source_target_pairs={{0,128},{64,192},{128,0},{192,64},{256,384},{320,448},{384,256},{4... | collective-permute-start | bytes 589832 | tf_op jit(solution)/shard_map/ppermute | solution.py:20
  209.9 15.0 %all-to-all-start.7 = ((bf16[16,16,128]{2,1,0:T(8,128)(2,1)}), bf16[16,16,128]{2,1,0:T(8,128)(2,1)S(1)}, u32[]{:S(2)}, u32[]{:S(2)}) async-start(bf16[16,16,128]{2,1,0:T(8,128)(2,1)} %get-tuple-element.87), calls=%async_computation.7 | async-start | bytes 131072 | tf_op jit(solution)/shard_map/all_to_all | solution.py:383
  226.9 19.0 %all-to-all-start.8 = ((bf16[64,16,128]{2,1,0:T(8,128)(2,1)}), bf16[64,16,128]{2,1,0:T(8,128)(2,1)S(1)}, u32[]{:S(2)}, u32[]{:S(2)}) async-start(bf16[64,16,128]{2,1,0:T(8,128)(2,1)} %bitcast.35), calls=%async_computation.8 | async-start | bytes 524288 | tf_op jit(solution)/shard_map/all_to_all | solution.py:266
  245.9 17.5 %collective-permute-start.16 = (bf16[768,128]{1,0:T(8,128)(2,1)}, bf16[768,128]{1,0:T(8,128)(2,1)S(1)}, u32[]{:S(2)}, u32[]{:S(2)}) collective-permute-start(bf16[768,128]{1,0:T(8,128)(2,1)} %get-tuple-element.100), channel_id=1, source_target_pairs={{0,256},{64,320},{128,384},{192,448},{256,0},{320,64},{384,128},{4... | collective-permute-start | bytes 589832 | tf_op jit(solution)/shard_map/ppermute | solution.py:20
  265.6 17.4 %all-to-all-start.10 = ((bf16[16,32,128]{2,1,0:T(8,128)(2,1)}), bf16[16,32,128]{2,1,0:T(8,128)(2,1)S(1)}, u32[]{:S(2)}, u32[]{:S(2)}) async-start(bf16[16,32,128]{2,1,0:T(8,128)(2,1)} %shard_map.77), calls=%async_computation.10 | async-start | bytes 262144 | tf_op jit(solution)/shard_map/all_to_all | solution.py:402
  (32 other events, 380.8 us)

commit v5 on v3

--- a/solution.py
+++ b/solution.py
@@ -11,6 +11,10 @@
 DOWN = (((0,), (0,)), ((), ()))
 
 
+def limit(mib):
+    return pltpu.CompilerParams(vmem_limit_bytes=mib * 2 ** 20)
+
+
 def grid_of(rows):
     z = 8 if rows >= 128 else 4
     return rows // (2 * z), z, 2
@@ -57,6 +61,7 @@
     return pl.pallas_call(
         body,
         out_shape=outs,
+        compiler_params=limit(6),
         cost_estimate=pl.CostEstimate(flops=0, bytes_accessed=2 * size, transcendentals=0),
     )(*args)
 
@@ -234,6 +239,7 @@
                    jax.ShapeDtypeStruct((count, rb, width), BF)),
         cost_estimate=pl.CostEstimate(
             flops=0, bytes_accessed=2 * arrived.size, transcendentals=0),
+        compiler_params=limit(4),
     )(*args)
 
 
@@ -300,10 +306,8 @@
     shape = jax.ShapeDtypeStruct
     whole, sent = shape((rows, width), F32), shape((rows, width), BF)
     send = elementwise(left_send, sent, rhs, table)
+    arrived, own_pivots, send = lax.optimization_barrier((arrived, own_pivots, send))
     got = swap_y(send, outer, ny)
-    arrived, got, own_pivots = lax.optimization_barrier((arrived, got, own_pivots))
-    value, send = elementwise(left_middle, (whole, sent), rhs, got, table)
-    crossed = swap_y(send, inner, ny)
 
     small = arrived[:, 5].astype(F32)
     small = small[:, :, :32] + small[:, :, 32:64]
@@ -314,14 +318,19 @@
     part, x1 = pl.pallas_call(
         lambda *refs: start_bands(ny, outer, inner, *refs),
         out_shape=(shape((half, width), BF), shape((ny * 2, rb, width), F32)),
+        compiler_params=limit(8),
     )(small, arrived)
     x1 = lax.dynamic_slice_in_dim(x1, 2 * y, 2, 0).reshape(low, width)
 
-    own0, spread = spread_sum(lax.all_to_all(part.reshape(nz, rb, width), "z", 0, 0), ny * nz)
+    met = lax.all_to_all(part.reshape(nz, rb, width), "z", 0, 0)
+    met, got = lax.optimization_barrier((met, got))
+    own0, spread = spread_sum(met, ny * nz)
     spread, second = lax.optimization_barrier((spread, panels[1]))
     gathered1 = lax.all_gather(second, "x", axis=0, tiled=True)
     mine0 = gather_yz(spread)
-    mine0, crossed = lax.optimization_barrier((mine0, crossed))
+    mine0, got = lax.optimization_barrier((mine0, got))
+    value, send = elementwise(left_middle, (whole, sent), rhs, got, table)
+    crossed = swap_y(send, inner, ny)
 
     core_spec = pl.BlockSpec(memory_space=pltpu.SMEM)
     vmem = pl.BlockSpec(memory_space=pltpu.VMEM)
@@ -329,7 +338,7 @@
     spread = pl.pallas_call(
         second_input, out_shape=shape((ny, low, width), BF),
         in_specs=[core_spec] + [vmem] * 4, out_specs=vmem,
-        scratch_shapes=[pltpu.VMEM((low, band), BF)],
+        scratch_shapes=[pltpu.VMEM((low, band), BF)], compiler_params=limit(6),
     )(core_ref, x1, cross, swap_core(cross), mine0)
     x1 = lax.all_to_all(spread, "y", 0, 0).reshape(chunk, width)
     other0 = swap_core(mine0)
@@ -344,7 +353,7 @@
     row_spec = pl.BlockSpec((tile, width), lambda i: (i, 0))
     table_spec = pl.BlockSpec((tile, 16), lambda i: (i, 0))
     half_spec = pl.BlockSpec((ny, half, width), lambda i: (0, 0, 0))
-    params = pltpu.CompilerParams(vmem_limit_bytes=40 * 2 ** 20)
+    params = limit(20)
     cost = pl.CostEstimate(
         flops=2 * rows * band * width, bytes_accessed=2 * rows * band, transcendentals=0)
     solved_ref = pltpu.VMEM((band, width), BF)
@@ -356,7 +365,7 @@
     )(core_ref, gathered0, mine0, other0, value, crossed)
 
     mine1 = gather_yz(spread)
-    mine1, base, cross = lax.optimization_barrier((mine1, base, cross))
+    mine1, base, cross, gathered1 = lax.optimization_barrier((mine1, base, cross, gathered1))
     cross = lax.all_gather(cross, ("y", "c"), axis=0, tiled=True)
     other1 = swap_core(mine1)
     halves = (shape((ny, half, width), F32), shape((ny, half, width), BF))
@@ -370,7 +379,6 @@
     )(core_ref, gathered1, mine1, other1, base, table)
     met = reduce_yz(term1 + swap_core(away1).astype(F32))
 
-    got = swap_y(rounded, inner, ny)
     term0, away0 = pl.pallas_call(
         first_term, out_shape=halves, grid=(steps,),
         in_specs=[core_spec, panel_spec, row_spec], out_specs=(half_spec, half_spec),
@@ -378,29 +386,31 @@
         compiler_params=params, cost_estimate=cost,
     )(core_ref, gathered0, rounded)
     away0 = swap_core(away0)
-    met, got, term0, away0, cross = lax.optimization_barrier((met, got, term0, away0, cross))
+    met, rounded, term0, away0 = lax.optimization_barrier((met, rounded, term0, away0))
     _, spread = spread_sum(met, 2 * nz, own1, own_pivots[rb:])
 
+    got = swap_y(rounded, inner, ny)
+    t1 = lax.all_to_all(spread, ("c", "z"), 0, 0).reshape(2 * half, width)
+    t1, got, cross = lax.optimization_barrier((t1, got, cross))
     value, send = elementwise(right_middle, (whole, sent), scaled, got, table)
-    got = swap_y(send, outer, ny)
-    t1 = lax.all_to_all(spread, ("c", "z"), 0, 0).reshape(2 * half, width)
     back1, term0 = pl.pallas_call(
         cross_back, out_shape=(shape((chunk, width), F32), shape((ny, half, width), BF)),
         in_specs=[core_spec] + [vmem] * 5, out_specs=(vmem, vmem),
         compiler_params=params,
     )(core_ref, tile1, t1, cross, term0, away0)
     met = reduce_yz(term0)
-    met, got = lax.optimization_barrier((met, got))
+    met, send = lax.optimization_barrier((met, send))
     _, spread = spread_sum(met, nz, own0, own_pivots[:rb])
+    t0 = lax.all_to_all(spread, "z", 0, 0).reshape(half, width)
+    t0, got = lax.optimization_barrier((t0, swap_y(send, outer, ny)))
     out = elementwise(right_end, whole, value, got, table)
-    t0 = lax.all_to_all(spread, "z", 0, 0).reshape(half, width)
-    t0, out = lax.optimization_barrier((t0, out))
     last = pl.pallas_call(
         lambda *refs: end_bands(ny, outer, inner, *refs),
         out_shape=shape((ny * 2, low, width), BF),
-        in_specs=[core_spec] + [vmem] * 4, out_specs=vmem,
+        in_specs=[core_spec] + [vmem] * 4, out_specs=vmem, compiler_params=limit(8),
     )(core_ref, small, tile0, t0, back1)
-    head = total(lax.all_to_all(last, ("y", "c"), 0, 0))
+    met, out = lax.optimization_barrier((lax.all_to_all(last, ("y", "c"), 0, 0), out))
+    head = total(met)
     return lax.dynamic_update_slice(out, head, (0, 0))
 
 

time: 275 us -> 254 us (0.924)
  waiting for transfers between devices: 62.1 us -> 79.5 us
  Pallas kernels: 32.6 us -> 19.3 us
  blocking collectives: 33.7 us -> 23.6 us
  starting transfers between devices: 103 us -> 96.3 us
  local copies, waits for them, and re-layouts: 23.2 us -> 16.7 us
    all_to_all x2, waiting for transfers between devices: 0.01 us -> 18.5 us  [reduce_yz(): lax.all_to_all(mine.astype(BF).reshape(ny * nz, rb, width), ('y', 'z'), 0...]
    all_to_all x2, blocking collectives: 33.7 us -> 23.6 us  [the longest x1 14.4 us: shards(): met = lax.all_to_all(part.reshape(nz, rb, width), 'z', 0, 0)]
    ppermute x4, waiting for transfers between devices: 22.1 us -> 12.1 us  [swap_y(): return lax.ppermute(v, 'y', [(i, i ^ bit) for i in range(count)])]
    pallas_call x4, Pallas kernels: 8.75 us -> 1.84 us  [elementwise(): pl.pallas_call(body, out_shape=outs, compiler_params=limit(6), cost_estim...]
    unnamed x66 -> x48, local copies, waits for them, and re-layouts: 14.8 us -> 10.2 us
    ppermute x5, starting transfers between devices: 19 us -> 14.7 us  [swap_core(): return lax.ppermute(v, 'c', [(0, 1), (1, 0)])]
    all_to_all x1, waiting for transfers between devices: 0.01 us -> 3.81 us  [shards(): arrived = lax.all_to_all(message, ('y', 'c'), 0, 0)]
    ppermute x4, starting transfers between devices: 20.1 us -> 16.5 us  [swap_y(): return lax.ppermute(v, 'y', [(i, i ^ bit) for i in range(count)])]
  transfers between devices with their start and end apart: 22 -> 22, of which waited for: 13 -> 13; matrix products, arithmetic and copies ran while one was open for 3% -> 3% of each run, Pallas kernels for 9% -> 7%
where the time goes in v5:
time: 254 us; the launch traced here: 252 us
  starting transfers between devices  96.3 us (38%)
  waiting for transfers between devices  79.5 us (31%)
  blocking collectives  23.6 us (9%)
  Pallas kernels  19.3 us (8%)
  local copies, waits for them, and re-layouts  16.7 us (7%)
  between operations  13.6 us (5%)
  other arithmetic  2.69 us (1%)
    all_to_all x2, waiting for transfers between devices, reduce_yz(): lax.all_to_all(mine.astype(BF).reshape(ny * nz, rb, width), ('y', 'z'), 0...  18.5 us
    ppermute x4, starting transfers between devices, swap_y(): return lax.ppermute(v, 'y', [(i, i ^ bit) for i in range(count)])  16.5 us
    all_to_all x2, starting transfers between devices, reduce_yz(): lax.all_to_all(mine.astype(BF).reshape(ny * nz, rb, width), ('y', 'z'), 0...  15.4 us
    ppermute x5, starting transfers between devices, swap_core(): return lax.ppermute(v, 'c', [(0, 1), (1, 0)])  14.7 us
    all_to_all x1, blocking collectives, shards(): met = lax.all_to_all(part.reshape(nz, rb, width), 'z', 0, 0)  14.4 us
    all_to_all x2, starting transfers between devices, gather_yz(): return lax.all_to_all(spread, ('y', 'z'), 0, 0).reshape(ny, half, width)  12.8 us
    ppermute x4, waiting for transfers between devices, swap_y(): return lax.ppermute(v, 'y', [(i, i ^ bit) for i in range(count)])  12.1 us
    all_to_all x1, starting transfers between devices, shards(): arrived = lax.all_to_all(message, ('y', 'c'), 0, 0)  10.2 us
  transfers between devices with their start and end apart: 22, of which 13 were waited for; matrix products, arithmetic and copies ran while one was open for 3% of the time, Pallas kernels for 7%

profile of v5, /device:TPU:1, one launch (start us, length us, event | category | flops | bytes accessed | tf_op | source)
XLA Modules:
  0.0 252.5 jit_solution(4478329136231507062)
XLA Ops:
  11.1 10.2 %all-to-all-start = ((bf16[16,6,16,128]{3,2,1,0:T(8,128)(2,1)}), bf16[16,6,16,128]{3,2,1,0:T(8,128)(2,1)S(1)}, u32[]{:S(2)}, u32[]{:S(2)}) async-start(bf16[16,6,16,128]{3,2,1,0:T(8,128)(2,1)} %pad_maximum_fusion), calls=%async_computation | async-start | bytes 786432 | tf_op jit(solution)/shard_map/all_to_all | solution.py:300
  24.2 7.9 %collective-permute-done = f32[32,128]{1,0:T(8,128)S(1)} collective-permute-done((f32[32,128]{1,0:T(8,128)S(1)}, f32[32,128]{1,0:T(8,128)S(1)}, u32[]{:S(2)}, u32[]{:S(2)}) %collective-permute-start) | collective-permute-done | bytes 16416 | tf_op jit(solution)/shard_map/ppermute | solution.py:303
  32.0 3.8 %all-to-all-done.refs_1_ = bf16[16,6,16,128]{3,2,1,0:T(8,128)(2,1)S(1)} async-done(((bf16[16,6,16,128]{3,2,1,0:T(8,128)(2,1)}), bf16[16,6,16,128]{3,2,1,0:T(8,128)(2,1)S(1)}, u32[]{:S(2)}, u32[]{:S(2)}) %all-to-all-start) | async-done | bytes 393248 | tf_op jit(solution)/shard_map/all_to_all | solution.py:300
  40.8 14.4 %all_to_all.55.refs_0_ = bf16[8,16,128]{2,1,0:T(8,128)(2,1)S(1)} all-to-all(bf16[8,16,128]{2,1,0:T(8,128)(2,1)S(1)} %bitcast.49), channel_id=1, replica_groups=mesh['y'=8,'z'=8,'c'=2,'x'=4] {'z'}, dimensions={0} | all-to-all | bytes 65536 | tf_op jit(solution)/shard_map/all_to_all | solution.py:325
  55.9 7.3 %all-to-all-start.2 = ((bf16[64,16,128]{2,1,0:T(8,128)(2,1)}), bf16[64,16,128]{2,1,0:T(8,128)(2,1)S(1)}, u32[]{:S(2)}, u32[]{:S(2)}) async-start(bf16[64,16,128]{2,1,0:T(8,128)(2,1)} %get-tuple-element.59), calls=%async_computation.2 | async-start | bytes 524288 | tf_op jit(solution)/shard_map/all_to_all | solution.py:284
  66.9 9.2 %all-to-all-done.2 = bf16[64,16,128]{2,1,0:T(8,128)(2,1)S(1)} async-done(((bf16[64,16,128]{2,1,0:T(8,128)(2,1)}), bf16[64,16,128]{2,1,0:T(8,128)(2,1)S(1)}, u32[]{:S(2)}, u32[]{:S(2)}) %all-to-all-start.2) | async-done | bytes 262176 | tf_op jit(solution)/shard_map/all_to_all | solution.py:284
  76.9 4.3 %all-to-all-start.3 = ((bf16[8,32,128]{2,1,0:T(8,128)(2,1)}), bf16[8,32,128]{2,1,0:T(8,128)(2,1)S(1)}, u32[]{:S(2)}, u32[]{:S(2)}) async-start(bf16[8,32,128]{2,1,0:T(8,128)(2,1)} %shard_map.67), calls=%async_computation.3 | async-start | bytes 131072 | tf_op jit(solution)/shard_map/all_to_all | solution.py:343
  81.9 4.0 %collective-permute-start.3 = (bf16[8,128,128]{2,1,0:T(8,128)(2,1)S(1)}, bf16[8,128,128]{2,1,0:T(8,128)(2,1)S(1)}, u32[]{:S(2)}, u32[]{:S(2)}) collective-permute-start(bf16[8,128,128]{2,1,0:T(8,128)(2,1)S(1)} %bitcast.42), channel_id=1, source_target_pairs={{0,4},{4,0},{1,5},{5,1},{2,6},{6,2},{3,7},{7,3},{8,12},{12,8},{9,1... | collective-permute-start | bytes 786440 | tf_op jit(solution)/shard_map/ppermute | solution.py:28
  89.3 6.5 %all-to-all-start.4 = ((bf16[16,16,128]{2,1,0:T(8,128)(2,1)}), bf16[16,16,128]{2,1,0:T(8,128)(2,1)S(1)}, u32[]{:S(2)}, u32[]{:S(2)}) async-start(bf16[16,16,128]{2,1,0:T(8,128)(2,1)} %bitcast.23), calls=%async_computation.4 | async-start | bytes 131072 | tf_op jit(solution)/shard_map/all_to_all | solution.py:346
  95.8 7.2 %all-to-all-done.4.refs_0_ = bf16[16,16,128]{2,1,0:T(8,128)(2,1)S(1)} async-done(((bf16[16,16,128]{2,1,0:T(8,128)(2,1)}), bf16[16,16,128]{2,1,0:T(8,128)(2,1)S(1)}, u32[]{:S(2)}, u32[]{:S(2)}) %all-to-all-start.4) | async-done | bytes 65568 | tf_op jit(solution)/shard_map/all_to_all | solution.py:346
  103.8 5.5 %all-to-all-start.5 = ((bf16[64,16,128]{2,1,0:T(8,128)(2,1)}), bf16[64,16,128]{2,1,0:T(8,128)(2,1)}, u32[]{:S(2)}, u32[]{:S(2)}) async-start(bf16[64,16,128]{2,1,0:T(8,128)(2,1)} %get-tuple-element.63), calls=%async_computation.5 | async-start | bytes 524288 | tf_op jit(solution)/shard_map/all_to_all | solution.py:284
  113.4 12.1 %collective-permute-done.4.got = bf16[768,128]{1,0:T(8,128)(2,1)S(1)} collective-permute-done((bf16[768,128]{1,0:T(8,128)(2,1)S(1)}, bf16[768,128]{1,0:T(8,128)(2,1)S(1)}, u32[]{:S(2)}, u32[]{:S(2)}) %collective-permute-start.4) | collective-permute-done | bytes 196640 | tf_op jit(solution)/shard_map/ppermute | solution.py:24
  137.0 5.3 %shard_map.71 = (f32[768,128]{1,0:T(8,128)S(1)}, bf16[768,128]{1,0:T(8,128)(2,1)S(1)}, f32[8,128,128]{2,1,0:T(8,128)S(1)}, bf16[8,128,128]{2,1,0:T(8,128)(2,1)S(1)}) custom-call(s32[1]{0:T(128)} %bitcast.core.refs_0_, bf16[768,2048]{1,0:T(8,128)(2,1)S(1)} %copy-done.2, bf16[8,128,128]{2,1,0:T(8,128)(2,1)} %bitcast.24.refs_2_, ...), custom_call_target="tpu_custom_call" | custom-call | flops 402653184 | bytes 3145728 | tf_op jit(solution)/shard_map/pallas_call | solution.py:372
  146.6 10.8 %all-to-all-start.6 = ((bf16[64,16,128]{2,1,0:T(8,128)(2,1)}), bf16[64,16,128]{2,1,0:T(8,128)(2,1)}, u32[]{:S(2)}, u32[]{:S(2)}) async-start(bf16[64,16,128]{2,1,0:T(8,128)(2,1)} %bitcast.50), calls=%async_computation.6 | async-start | bytes 524288 | tf_op jit(solution)/shard_map/all_to_all | solution.py:281
  165.9 6.1 %all-to-all-done.6.refs_0_ = bf16[64,16,128]{2,1,0:T(8,128)(2,1)} async-done(((bf16[64,16,128]{2,1,0:T(8,128)(2,1)}), bf16[64,16,128]{2,1,0:T(8,128)(2,1)}, u32[]{:S(2)}, u32[]{:S(2)}) %all-to-all-start.6) | async-done | bytes 262176 | tf_op jit(solution)/shard_map/all_to_all | solution.py:281
  172.0 4.1 %collective-permute-start.8 = (bf16[768,128]{1,0:T(8,128)(2,1)}, bf16[768,128]{1,0:T(8,128)(2,1)S(1)}, u32[]{:S(2)}, u32[]{:S(2)}) collective-permute-start(bf16[768,128]{1,0:T(8,128)(2,1)} %copy-done.15), channel_id=1, source_target_pairs={{0,128},{64,192},{128,0},{192,64},{256,384},{320,448},{384,256},{4... | collective-permute-start | bytes 589832 | tf_op jit(solution)/shard_map/ppermute | solution.py:24
  178.5 4.7 %all-to-all-start.7 = ((bf16[16,16,128]{2,1,0:T(8,128)(2,1)}), bf16[16,16,128]{2,1,0:T(8,128)(2,1)S(1)}, u32[]{:S(2)}, u32[]{:S(2)}) async-start(bf16[16,16,128]{2,1,0:T(8,128)(2,1)} %get-tuple-element.80), calls=%async_computation.7 | async-start | bytes 131072 | tf_op jit(solution)/shard_map/all_to_all | solution.py:393
  184.1 6.3 %all-to-all-done.7 = bf16[16,16,128]{2,1,0:T(8,128)(2,1)S(1)} async-done(((bf16[16,16,128]{2,1,0:T(8,128)(2,1)}), bf16[16,16,128]{2,1,0:T(8,128)(2,1)S(1)}, u32[]{:S(2)}, u32[]{:S(2)}) %all-to-all-start.7) | async-done | bytes 65568 | tf_op jit(solution)/shard_map/all_to_all | solution.py:393
  194.0 4.6 %all-to-all-start.8 = ((bf16[64,16,128]{2,1,0:T(8,128)(2,1)}), bf16[64,16,128]{2,1,0:T(8,128)(2,1)S(1)}, u32[]{:S(2)}, u32[]{:S(2)}) async-start(bf16[64,16,128]{2,1,0:T(8,128)(2,1)} %bitcast.28), calls=%async_computation.8 | async-start | bytes 524288 | tf_op jit(solution)/shard_map/all_to_all | solution.py:281
  199.0 12.4 %all-to-all-done.8.refs_0_ = bf16[64,16,128]{2,1,0:T(8,128)(2,1)S(1)} async-done(((bf16[64,16,128]{2,1,0:T(8,128)(2,1)}), bf16[64,16,128]{2,1,0:T(8,128)(2,1)S(1)}, u32[]{:S(2)}, u32[]{:S(2)}) %all-to-all-start.8) | async-done | bytes 262176 | tf_op jit(solution)/shard_map/all_to_all | solution.py:281
  211.4 5.0 %collective-permute-start.9 = (bf16[768,128]{1,0:T(8,128)(2,1)S(1)}, bf16[768,128]{1,0:T(8,128)(2,1)S(1)}, u32[]{:S(2)}, u32[]{:S(2)}) collective-permute-start(bf16[768,128]{1,0:T(8,128)(2,1)S(1)} %get-tuple-element.94), channel_id=1, source_target_pairs={{0,256},{64,320},{128,384},{192,448},{256,0},{320,64},{384,128},{4... | collective-permute-start | bytes 589832 | tf_op jit(solution)/shard_map/ppermute | solution.py:24
  217.1 9.2 %all_to_all.56 = bf16[8,16,128]{2,1,0:T(8,128)(2,1)S(1)} all-to-all(bf16[8,16,128]{2,1,0:T(8,128)(2,1)S(1)} %get-tuple-element.93), channel_id=1, replica_groups=mesh['y'=8,'z'=8,'c'=2,'x'=4] {'z'}, dimensions={0} | all-to-all | bytes 65536 | tf_op jit(solution)/shard_map/all_to_all | solution.py:404
  227.5 8.7 %all-to-all-start.10 = ((bf16[16,32,128]{2,1,0:T(8,128)(2,1)}), bf16[16,32,128]{2,1,0:T(8,128)(2,1)S(1)}, u32[]{:S(2)}, u32[]{:S(2)}) async-start(bf16[16,32,128]{2,1,0:T(8,128)(2,1)} %shard_map.77), calls=%async_computation.10 | async-start | bytes 262144 | tf_op jit(solution)/shard_map/all_to_all | solution.py:412
  237.1 8.3 %all-to-all-done.10 = bf16[16,32,128]{2,1,0:T(8,128)(2,1)S(1)} async-done(((bf16[16,32,128]{2,1,0:T(8,128)(2,1)}), bf16[16,32,128]{2,1,0:T(8,128)(2,1)S(1)}, u32[]{:S(2)}, u32[]{:S(2)}) %all-to-all-start.10) | async-done | bytes 131104 | tf_op jit(solution)/shard_map/all_to_all | solution.py:412
  (124 shorter events, 61.2 us)
Async XLA Ops:
  6.5 56.7 %all-gather.9.cloned.1.call-start = ((), (), s32[]{:S(2)}) async-start(), calls=%async_computation.13 | async-start | bytes 3932160 | tf_op jit(solution)/shard_map/all_gather | solution.py:286
  11.1 24.8 %all-to-all-start = ((bf16[16,6,16,128]{3,2,1,0:T(8,128)(2,1)}), bf16[16,6,16,128]{3,2,1,0:T(8,128)(2,1)S(1)}, u32[]{:S(2)}, u32[]{:S(2)}) async-start(bf16[16,6,16,128]{3,2,1,0:T(8,128)(2,1)} %pad_maximum_fusion), calls=%async_computation | async-start | bytes 786432 | tf_op jit(solution)/shard_map/all_to_all | solution.py:300
  21.3 108.4 %all-gather.5.cloned.1.call-start = ((), (), s32[]{:S(2)}) async-start(), calls=%async_computation.11 | async-start | bytes 3932160 | tf_op jit(solution)/shard_map/all_gather | solution.py:329
  21.6 10.4 %collective-permute-start = (f32[32,128]{1,0:T(8,128)S(1)}, f32[32,128]{1,0:T(8,128)S(1)}, u32[]{:S(2)}, u32[]{:S(2)}) collective-permute-start(f32[32,128]{1,0:T(8,128)S(1)} %broadcast_in_dim.35), channel_id=1, source_target_pairs={{0,0},{4,8},{8,16},{12,24},{16,32},{20,40},{24,48},{28,56},{32,4},... | collective-permute-start | bytes 49160 | tf_op jit(solution)/shard_map/ppermute | solution.py:303
  35.8 19.3 %collective-permute-start.2 = (bf16[768,128]{1,0:T(8,128)(2,1)S(1)}, bf16[768,128]{1,0:T(8,128)(2,1)S(1)}, u32[]{:S(2)}, u32[]{:S(2)}) collective-permute-start(bf16[768,128]{1,0:T(8,128)(2,1)S(1)} %shard_map.64), channel_id=1, source_target_pairs={{0,256},{64,320},{128,384},{192,448},{256,0},{320,64},{384,128},{4... | collective-permute-start | bytes 589832 | tf_op jit(solution)/shard_map/ppermute | solution.py:24
  55.9 20.2 %all-to-all-start.2 = ((bf16[64,16,128]{2,1,0:T(8,128)(2,1)}), bf16[64,16,128]{2,1,0:T(8,128)(2,1)S(1)}, u32[]{:S(2)}, u32[]{:S(2)}) async-start(bf16[64,16,128]{2,1,0:T(8,128)(2,1)} %get-tuple-element.59), calls=%async_computation.2 | async-start | bytes 524288 | tf_op jit(solution)/shard_map/all_to_all | solution.py:284
  64.1 12.0 %collective-permute-start.1 = (bf16[16,2048]{1,0:T(8,128)(2,1)S(1)}, bf16[16,2048]{1,0:T(8,128)(2,1)S(1)}, u32[]{:S(2)}, u32[]{:S(2)}) collective-permute-start(bf16[16,2048]{1,0:T(8,128)(2,1)S(1)} %slice_bitcast_fusion.1.mine_rows), channel_id=1, source_target_pairs={{0,4},{4,0},{1,5},{5,1},{2,6},{6,2},{3,7},{7,3},{8,12},{12,8},{9,1... | collective-permute-start | bytes 196616 | tf_op jit(solution)/shard_map/ppermute | solution.py:28
  76.9 11.5 %all-to-all-start.3 = ((bf16[8,32,128]{2,1,0:T(8,128)(2,1)}), bf16[8,32,128]{2,1,0:T(8,128)(2,1)S(1)}, u32[]{:S(2)}, u32[]{:S(2)}) async-start(bf16[8,32,128]{2,1,0:T(8,128)(2,1)} %shard_map.67), calls=%async_computation.3 | async-start | bytes 131072 | tf_op jit(solution)/shard_map/all_to_all | solution.py:343
  81.9 13.9 %collective-permute-start.3 = (bf16[8,128,128]{2,1,0:T(8,128)(2,1)S(1)}, bf16[8,128,128]{2,1,0:T(8,128)(2,1)S(1)}, u32[]{:S(2)}, u32[]{:S(2)}) collective-permute-start(bf16[8,128,128]{2,1,0:T(8,128)(2,1)S(1)} %bitcast.42), channel_id=1, source_target_pairs={{0,4},{4,0},{1,5},{5,1},{2,6},{6,2},{3,7},{7,3},{8,12},{12,8},{9,1... | collective-permute-start | bytes 786440 | tf_op jit(solution)/shard_map/ppermute | solution.py:28
  89.3 13.7 %all-to-all-start.4 = ((bf16[16,16,128]{2,1,0:T(8,128)(2,1)}), bf16[16,16,128]{2,1,0:T(8,128)(2,1)S(1)}, u32[]{:S(2)}, u32[]{:S(2)}) async-start(bf16[16,16,128]{2,1,0:T(8,128)(2,1)} %bitcast.23), calls=%async_computation.4 | async-start | bytes 131072 | tf_op jit(solution)/shard_map/all_to_all | solution.py:346
  103.8 25.9 %all-to-all-start.5 = ((bf16[64,16,128]{2,1,0:T(8,128)(2,1)}), bf16[64,16,128]{2,1,0:T(8,128)(2,1)}, u32[]{:S(2)}, u32[]{:S(2)}) async-start(bf16[64,16,128]{2,1,0:T(8,128)(2,1)} %get-tuple-element.63), calls=%async_computation.5 | async-start | bytes 524288 | tf_op jit(solution)/shard_map/all_to_all | solution.py:284
  109.3 81.1 %all-gather.7.cloned.1.call-start = ((), (), s32[]{:S(2)}) async-start(), calls=%async_computation.12 | async-start | bytes 1114112 | tf_op jit(solution)/shard_map/all_gather | solution.py:369
  109.7 15.8 %collective-permute-start.4 = (bf16[768,128]{1,0:T(8,128)(2,1)S(1)}, bf16[768,128]{1,0:T(8,128)(2,1)S(1)}, u32[]{:S(2)}, u32[]{:S(2)}) collective-permute-start(bf16[768,128]{1,0:T(8,128)(2,1)S(1)} %get-tuple-element.67), channel_id=1, source_target_pairs={{0,128},{64,192},{128,0},{192,64},{256,384},{320,448},{384,256},{4... | collective-permute-start | bytes 589832 | tf_op jit(solution)/shard_map/ppermute | solution.py:24
  129.7 4.4 %collective-permute-start.5 = (bf16[8,128,128]{2,1,0:T(8,128)(2,1)}, bf16[8,128,128]{2,1,0:T(8,128)(2,1)S(1)}, u32[]{:S(2)}, u32[]{:S(2)}) collective-permute-start(bf16[8,128,128]{2,1,0:T(8,128)(2,1)} %bitcast.24.refs_2_), channel_id=1, source_target_pairs={{0,4},{4,0},{1,5},{5,1},{2,6},{6,2},{3,7},{7,3},{8,12},{12,8},{9,1... | collective-permute-start | bytes 786440 | tf_op jit(solution)/shard_map/ppermute | solution.py:28
  142.3 3.4 %collective-permute-start.6 = (bf16[8,128,128]{2,1,0:T(8,128)(2,1)S(1)}, bf16[8,128,128]{2,1,0:T(8,128)(2,1)S(1)}, u32[]{:S(2)}, u32[]{:S(2)}) collective-permute-start(bf16[8,128,128]{2,1,0:T(8,128)(2,1)S(1)} %get-tuple-element.73), channel_id=1, source_target_pairs={{0,4},{4,0},{1,5},{5,1},{2,6},{6,2},{3,7},{7,3},{8,12},{12,8},{9,1... | collective-permute-start | bytes 786440 | tf_op jit(solution)/shard_map/ppermute | solution.py:28
  146.6 25.4 %all-to-all-start.6 = ((bf16[64,16,128]{2,1,0:T(8,128)(2,1)}), bf16[64,16,128]{2,1,0:T(8,128)(2,1)}, u32[]{:S(2)}, u32[]{:S(2)}) async-start(bf16[64,16,128]{2,1,0:T(8,128)(2,1)} %bitcast.50), calls=%async_computation.6 | async-start | bytes 524288 | tf_op jit(solution)/shard_map/all_to_all | solution.py:281
  162.1 64.2 %copy-start.6 = (f32[16,16,32]{2,1,0:T(8,128)S(1)}, f32[16,16,32]{2,1,0:T(8,128)}, u32[]{:S(2)}) copy-start(f32[16,16,32]{2,1,0:T(8,128)} %copy-done.5) | copy-start | bytes 98308
  162.1 64.2 %copy-start.14 = (bf16[16,1,16,128]{3,2,1,0:T(8,128)(2,1)S(1)}, bf16[16,1,16,128]{3,2,1,0:T(8,128)(2,1)}, u32[]{:S(2)}) copy-start(bf16[16,1,16,128]{3,2,1,0:T(8,128)(2,1)} %get-tuple-element.107) | copy-start | bytes 196612
  162.1 3.8 %collective-permute-start.7 = (bf16[8,128,128]{2,1,0:T(8,128)(2,1)S(1)}, bf16[8,128,128]{2,1,0:T(8,128)(2,1)S(1)}, u32[]{:S(2)}, u32[]{:S(2)}) collective-permute-start(bf16[8,128,128]{2,1,0:T(8,128)(2,1)S(1)} %get-tuple-element.76), channel_id=1, source_target_pairs={{0,4},{4,0},{1,5},{5,1},{2,6},{6,2},{3,7},{7,3},{8,12},{12,8},{9,1... | collective-permute-start | bytes 786440 | tf_op jit(solution)/shard_map/ppermute | solution.py:28
  172.0 18.4 %collective-permute-start.8 = (bf16[768,128]{1,0:T(8,128)(2,1)}, bf16[768,128]{1,0:T(8,128)(2,1)S(1)}, u32[]{:S(2)}, u32[]{:S(2)}) collective-permute-start(bf16[768,128]{1,0:T(8,128)(2,1)} %copy-done.15), channel_id=1, source_target_pairs={{0,128},{64,192},{128,0},{192,64},{256,384},{320,448},{384,256},{4... | collective-permute-start | bytes 589832 | tf_op jit(solution)/shard_map/ppermute | solution.py:24
  178.5 11.9 %all-to-all-start.7 = ((bf16[16,16,128]{2,1,0:T(8,128)(2,1)}), bf16[16,16,128]{2,1,0:T(8,128)(2,1)S(1)}, u32[]{:S(2)}, u32[]{:S(2)}) async-start(bf16[16,16,128]{2,1,0:T(8,128)(2,1)} %get-tuple-element.80), calls=%async_computation.7 | async-start | bytes 131072 | tf_op jit(solution)/shard_map/all_to_all | solution.py:393
  194.0 17.4 %all-to-all-start.8 = ((bf16[64,16,128]{2,1,0:T(8,128)(2,1)}), bf16[64,16,128]{2,1,0:T(8,128)(2,1)S(1)}, u32[]{:S(2)}, u32[]{:S(2)}) async-start(bf16[64,16,128]{2,1,0:T(8,128)(2,1)} %bitcast.28), calls=%async_computation.8 | async-start | bytes 524288 | tf_op jit(solution)/shard_map/all_to_all | solution.py:281
  211.4 14.9 %collective-permute-start.9 = (bf16[768,128]{1,0:T(8,128)(2,1)S(1)}, bf16[768,128]{1,0:T(8,128)(2,1)S(1)}, u32[]{:S(2)}, u32[]{:S(2)}) collective-permute-start(bf16[768,128]{1,0:T(8,128)(2,1)S(1)} %get-tuple-element.94), channel_id=1, source_target_pairs={{0,256},{64,320},{128,384},{192,448},{256,0},{320,64},{384,128},{4... | collective-permute-start | bytes 589832 | tf_op jit(solution)/shard_map/ppermute | solution.py:24
  227.5 17.8 %all-to-all-start.10 = ((bf16[16,32,128]{2,1,0:T(8,128)(2,1)}), bf16[16,32,128]{2,1,0:T(8,128)(2,1)S(1)}, u32[]{:S(2)}, u32[]{:S(2)}) async-start(bf16[16,32,128]{2,1,0:T(8,128)(2,1)} %shard_map.77), calls=%async_computation.10 | async-start | bytes 262144 | tf_op jit(solution)/shard_map/all_to_all | solution.py:412
  (23 other events, 253.5 us)
Sparse Core Ops, SparseCore 0:
  9.6 50.3 all-gather.8
  62.1 45.1 all-gather.4
  129.8 41.1 all-gather.6

commit v6 on v5

--- a/solution.py
+++ b/solution.py
@@ -344,7 +344,7 @@
     other0 = swap_core(mine0)
     part = down(tile1, x1).astype(BF).reshape(2 * nz, rb, width)
     met = lax.all_to_all(part, ("c", "z"), 0, 0)
-    met, other0 = lax.optimization_barrier((met, other0))
+    met, other0, crossed = lax.optimization_barrier((met, other0, crossed))
     own1, spread = spread_sum(met, ny * nz)
 
     tile = rows // 3
@@ -361,7 +361,7 @@
         first_update, out_shape=whole, grid=(steps,),
         in_specs=[core_spec, panel_spec, half_spec, half_spec, row_spec, row_spec],
         out_specs=row_spec, scratch_shapes=[solved_ref],
-        compiler_params=params, cost_estimate=cost,
+        cost_estimate=cost,
     )(core_ref, gathered0, mine0, other0, value, crossed)
 
     mine1 = gather_yz(spread)
@@ -375,7 +375,7 @@
         in_specs=[core_spec, panel_spec, half_spec, half_spec, row_spec, table_spec],
         out_specs=(row_spec, row_spec, half_spec, half_spec),
         scratch_shapes=[pltpu.VMEM((width, band), F32), solved_ref],
-        compiler_params=params, cost_estimate=cost,
+        cost_estimate=cost,
     )(core_ref, gathered1, mine1, other1, base, table)
     met = reduce_yz(term1 + swap_core(away1).astype(F32))
 
@@ -386,7 +386,7 @@
         compiler_params=params, cost_estimate=cost,
     )(core_ref, gathered0, rounded)
     away0 = swap_core(away0)
-    met, rounded, term0, away0 = lax.optimization_barrier((met, rounded, term0, away0))
+    met, term0, away0 = lax.optimization_barrier((met, term0, away0))
     _, spread = spread_sum(met, 2 * nz, own1, own_pivots[rb:])
 
     got = swap_y(rounded, inner, ny)

time: 254 us -> 242 us (0.953)
  waiting for transfers between devices: 79.5 us -> 67.6 us
  Pallas kernels: 19.3 us -> 25.9 us
  local copies, waits for them, and re-layouts: 16.7 us -> 11 us
    all_to_all x2, waiting for transfers between devices: 9.18 us -> 17.2 us  [gather_yz(): return lax.all_to_all(spread, ('y', 'z'), 0, 0).reshape(ny, half, width)]
    ppermute x4, waiting for transfers between devices: 12.1 us -> 4.99 us  [swap_y(): return lax.ppermute(v, 'y', [(i, i ^ bit) for i in range(count)])]
    unnamed x48, local copies, waits for them, and re-layouts: 10.2 us -> 4.54 us
    all_to_all x1, waiting for transfers between devices: 7.17 us -> 2.18 us  [shards(): met = lax.all_to_all(part, ('c', 'z'), 0, 0)]
    all_to_all x2, waiting for transfers between devices: 18.5 us -> 14.3 us  [reduce_yz(): lax.all_to_all(mine.astype(BF).reshape(ny * nz, rb, width), ('y', 'z'), 0...]
    all_to_all x2, starting transfers between devices: 15.4 us -> 11.7 us  [reduce_yz(): lax.all_to_all(mine.astype(BF).reshape(ny * nz, rb, width), ('y', 'z'), 0...]
    pallas_call x1, Pallas kernels: 1.49 us -> 4.87 us  [shards(): pl.pallas_call(first_update, out_shape=whole, grid=(steps,), in_specs=[co...]
    all_to_all x1, starting transfers between devices: 6.5 us -> 3.62 us  [shards(): met = lax.all_to_all(part, ('c', 'z'), 0, 0)]
  transfers between devices with their start and end apart: 22 -> 22, of which waited for: 13 -> 12; matrix products, arithmetic and copies ran while one was open for 3% -> 3% of each run, Pallas kernels for 7% -> 10%
where the time goes in v6:
time: 242 us; the launch traced here: 240 us
  starting transfers between devices  93.9 us (39%)
  waiting for transfers between devices  67.6 us (28%)
  Pallas kernels  25.9 us (11%)
  blocking collectives  23.7 us (10%)
  between operations  13.6 us (6%)
  local copies, waits for them, and re-layouts  11 us (5%)
  other arithmetic  3.71 us (2%)
    all_to_all x2, waiting for transfers between devices, gather_yz(): return lax.all_to_all(spread, ('y', 'z'), 0, 0).reshape(ny, half, width)  17.2 us
    ppermute x4, starting transfers between devices, swap_y(): return lax.ppermute(v, 'y', [(i, i ^ bit) for i in range(count)])  17 us
    ppermute x5, starting transfers between devices, swap_core(): return lax.ppermute(v, 'c', [(0, 1), (1, 0)])  16.2 us
    all_to_all x1, blocking collectives, shards(): met = lax.all_to_all(part.reshape(nz, rb, width), 'z', 0, 0)  14.4 us
    all_to_all x2, waiting for transfers between devices, reduce_yz(): lax.all_to_all(mine.astype(BF).reshape(ny * nz, rb, width), ('y', 'z'), 0...  14.3 us
    all_to_all x2, starting transfers between devices, gather_yz(): return lax.all_to_all(spread, ('y', 'z'), 0, 0).reshape(ny, half, width)  14.1 us
    all_to_all x2, starting transfers between devices, reduce_yz(): lax.all_to_all(mine.astype(BF).reshape(ny * nz, rb, width), ('y', 'z'), 0...  11.7 us
    all_to_all x1, starting transfers between devices, shards(): arrived = lax.all_to_all(message, ('y', 'c'), 0, 0)  10.2 us
  transfers between devices with their start and end apart: 22, of which 12 were waited for; matrix products, arithmetic and copies ran while one was open for 3% of the time, Pallas kernels for 10%

profile of v6, /device:TPU:1, one launch (start us, length us, event | category | flops | bytes accessed | tf_op | source)
XLA Modules:
  0.0 240.3 jit_solution(7483680412218756428)
XLA Ops:
  11.1 10.2 %all-to-all-start = ((bf16[16,6,16,128]{3,2,1,0:T(8,128)(2,1)}), bf16[16,6,16,128]{3,2,1,0:T(8,128)(2,1)S(1)}, u32[]{:S(2)}, u32[]{:S(2)}) async-start(bf16[16,6,16,128]{3,2,1,0:T(8,128)(2,1)} %pad_maximum_fusion), calls=%async_computation | async-start | bytes 786432 | tf_op jit(solution)/shard_map/all_to_all | solution.py:300
  24.2 7.9 %collective-permute-done = f32[32,128]{1,0:T(8,128)S(1)} collective-permute-done((f32[32,128]{1,0:T(8,128)S(1)}, f32[32,128]{1,0:T(8,128)S(1)}, u32[]{:S(2)}, u32[]{:S(2)}) %collective-permute-start) | collective-permute-done | bytes 16416 | tf_op jit(solution)/shard_map/ppermute | solution.py:303
  40.8 14.4 %all_to_all.55.refs_0_ = bf16[8,16,128]{2,1,0:T(8,128)(2,1)S(1)} all-to-all(bf16[8,16,128]{2,1,0:T(8,128)(2,1)S(1)} %bitcast.49), channel_id=1, replica_groups=mesh['y'=8,'z'=8,'c'=2,'x'=4] {'z'}, dimensions={0} | all-to-all | bytes 65536 | tf_op jit(solution)/shard_map/all_to_all | solution.py:325
  55.9 7.3 %all-to-all-start.2 = ((bf16[64,16,128]{2,1,0:T(8,128)(2,1)}), bf16[64,16,128]{2,1,0:T(8,128)(2,1)S(1)}, u32[]{:S(2)}, u32[]{:S(2)}) async-start(bf16[64,16,128]{2,1,0:T(8,128)(2,1)} %get-tuple-element.59), calls=%async_computation.2 | async-start | bytes 524288 | tf_op jit(solution)/shard_map/all_to_all | solution.py:284
  66.9 9.2 %all-to-all-done.2 = bf16[64,16,128]{2,1,0:T(8,128)(2,1)S(1)} async-done(((bf16[64,16,128]{2,1,0:T(8,128)(2,1)}), bf16[64,16,128]{2,1,0:T(8,128)(2,1)S(1)}, u32[]{:S(2)}, u32[]{:S(2)}) %all-to-all-start.2) | async-done | bytes 262176 | tf_op jit(solution)/shard_map/all_to_all | solution.py:284
  76.9 4.3 %all-to-all-start.3 = ((bf16[8,32,128]{2,1,0:T(8,128)(2,1)}), bf16[8,32,128]{2,1,0:T(8,128)(2,1)S(1)}, u32[]{:S(2)}, u32[]{:S(2)}) async-start(bf16[8,32,128]{2,1,0:T(8,128)(2,1)} %shard_map.67), calls=%async_computation.3 | async-start | bytes 131072 | tf_op jit(solution)/shard_map/all_to_all | solution.py:343
  87.0 4.4 %collective-permute-start.4 = (bf16[768,128]{1,0:T(8,128)(2,1)S(1)}, bf16[768,128]{1,0:T(8,128)(2,1)S(1)}, u32[]{:S(2)}, u32[]{:S(2)}) collective-permute-start(bf16[768,128]{1,0:T(8,128)(2,1)S(1)} %get-tuple-element.63), channel_id=1, source_target_pairs={{0,128},{64,192},{128,0},{192,64},{256,384},{320,448},{384,256},{4... | collective-permute-start | bytes 589832 | tf_op jit(solution)/shard_map/ppermute | solution.py:24
  95.9 5.0 %collective-permute-done.4.got = bf16[768,128]{1,0:T(8,128)(2,1)S(1)} collective-permute-done((bf16[768,128]{1,0:T(8,128)(2,1)S(1)}, bf16[768,128]{1,0:T(8,128)(2,1)S(1)}, u32[]{:S(2)}, u32[]{:S(2)}) %collective-permute-start.4) | collective-permute-done | bytes 196640 | tf_op jit(solution)/shard_map/ppermute | solution.py:24
  103.9 6.8 %all-to-all-start.5 = ((bf16[64,16,128]{2,1,0:T(8,128)(2,1)}), bf16[64,16,128]{2,1,0:T(8,128)(2,1)S(1)}, u32[]{:S(2)}, u32[]{:S(2)}) async-start(bf16[64,16,128]{2,1,0:T(8,128)(2,1)} %get-tuple-element.65), calls=%async_computation.5 | async-start | bytes 524288 | tf_op jit(solution)/shard_map/all_to_all | solution.py:284
  110.8 4.9 %shard_map.70.refs_4_ = f32[768,128]{1,0:T(8,128)} custom-call(s32[1]{0:T(128)} %bitcast.core.refs_0_, bf16[768,2048]{1,0:T(8,128)(2,1)} %bitcast.39, bf16[8,128,128]{2,1,0:T(8,128)(2,1)} %bitcast.43, bf16[8,128,128]{2,1,0:T(8,128)(2,1)} %copy-done.15, f32[768,128]{1,0:T(8,128)} %copy-done.11, bf16[768,128]{1,0:T(8,128)(2,1)} %copy-done.18), custom_call_target="tpu_custom_call" | custom-call | flops 402653184 | bytes 3145728 | tf_op jit(solution)/shard_map/pallas_call | solution.py:360
  115.7 8.1 %all-to-all-done.5 = bf16[64,16,128]{2,1,0:T(8,128)(2,1)S(1)} async-done(((bf16[64,16,128]{2,1,0:T(8,128)(2,1)}), bf16[64,16,128]{2,1,0:T(8,128)(2,1)S(1)}, u32[]{:S(2)}, u32[]{:S(2)}) %all-to-all-start.5) | async-done | bytes 262176 | tf_op jit(solution)/shard_map/all_to_all | solution.py:284
  123.8 4.8 %collective-permute-start.5 = (bf16[8,128,128]{2,1,0:T(8,128)(2,1)S(1)}, bf16[8,128,128]{2,1,0:T(8,128)(2,1)}, u32[]{:S(2)}, u32[]{:S(2)}) collective-permute-start(bf16[8,128,128]{2,1,0:T(8,128)(2,1)S(1)} %bitcast.50), channel_id=1, source_target_pairs={{0,4},{4,0},{1,5},{5,1},{2,6},{6,2},{3,7},{7,3},{8,12},{12,8},{9,1... | collective-permute-start | bytes 786440 | tf_op jit(solution)/shard_map/ppermute | solution.py:28
  129.8 7.3 %shard_map.71 = (f32[768,128]{1,0:T(8,128)}, bf16[768,128]{1,0:T(8,128)(2,1)}, f32[8,128,128]{2,1,0:T(8,128)}, bf16[8,128,128]{2,1,0:T(8,128)(2,1)}) custom-call(s32[1]{0:T(128)} %bitcast.core.refs_0_, bf16[768,2048]{1,0:T(8,128)(2,1)} %all-gather.5.cloned.1.call-done.refs_1_, bf16[8,128,128]{2,1,0:T(8,128)(2,1)} %bitcast.51, ...), custom_call_target="tpu_custom_call" | custom-call | flops 402653184 | bytes 3145728 | tf_op jit(solution)/shard_map/pallas_call | solution.py:372
  142.6 5.5 %all-to-all-start.6 = ((bf16[64,16,128]{2,1,0:T(8,128)(2,1)}), bf16[64,16,128]{2,1,0:T(8,128)(2,1)}, u32[]{:S(2)}, u32[]{:S(2)}) async-start(bf16[64,16,128]{2,1,0:T(8,128)(2,1)} %bitcast.26), calls=%async_computation.6 | async-start | bytes 524288 | tf_op jit(solution)/shard_map/all_to_all | solution.py:281
  148.1 4.2 %shard_map.72 = (f32[8,128,128]{2,1,0:T(8,128)S(1)}, bf16[8,128,128]{2,1,0:T(8,128)(2,1)S(1)}) custom-call(s32[1]{0:T(128)} %bitcast.core.refs_0_, bf16[768,2048]{1,0:T(8,128)(2,1)S(1)} %bitcast.40, bf16[768,128]{1,0:T(8,128)(2,1)} %get-tuple-element.75.rounded), custom_call_target="tpu_custom_call" | custom-call | flops 402653184 | bytes 3145728 | tf_op jit(solution)/shard_map/pallas_call | solution.py:382
  155.6 4.0 %collective-permute-start.8 = (bf16[768,128]{1,0:T(8,128)(2,1)}, bf16[768,128]{1,0:T(8,128)(2,1)S(1)}, u32[]{:S(2)}, u32[]{:S(2)}) collective-permute-start(bf16[768,128]{1,0:T(8,128)(2,1)} %get-tuple-element.75.rounded), channel_id=1, source_target_pairs={{0,128},{64,192},{128,0},{192,64},{256,384},{320,448},{384,256},{4... | collective-permute-start | bytes 589832 | tf_op jit(solution)/shard_map/ppermute | solution.py:24
  163.8 5.6 %all-to-all-start.7 = ((bf16[16,16,128]{2,1,0:T(8,128)(2,1)}), bf16[16,16,128]{2,1,0:T(8,128)(2,1)S(1)}, u32[]{:S(2)}, u32[]{:S(2)}) async-start(bf16[16,16,128]{2,1,0:T(8,128)(2,1)} %get-tuple-element.81), calls=%async_computation.7 | async-start | bytes 131072 | tf_op jit(solution)/shard_map/all_to_all | solution.py:393
  170.3 6.3 %all-to-all-done.7 = bf16[16,16,128]{2,1,0:T(8,128)(2,1)S(1)} async-done(((bf16[16,16,128]{2,1,0:T(8,128)(2,1)}), bf16[16,16,128]{2,1,0:T(8,128)(2,1)S(1)}, u32[]{:S(2)}, u32[]{:S(2)}) %all-to-all-start.7) | async-done | bytes 65568 | tf_op jit(solution)/shard_map/all_to_all | solution.py:393
  180.2 6.2 %all-to-all-start.8 = ((bf16[64,16,128]{2,1,0:T(8,128)(2,1)}), bf16[64,16,128]{2,1,0:T(8,128)(2,1)S(1)}, u32[]{:S(2)}, u32[]{:S(2)}) async-start(bf16[64,16,128]{2,1,0:T(8,128)(2,1)} %bitcast.28), calls=%async_computation.8 | async-start | bytes 524288 | tf_op jit(solution)/shard_map/all_to_all | solution.py:281
  186.8 12.5 %all-to-all-done.8.refs_0_ = bf16[64,16,128]{2,1,0:T(8,128)(2,1)S(1)} async-done(((bf16[64,16,128]{2,1,0:T(8,128)(2,1)}), bf16[64,16,128]{2,1,0:T(8,128)(2,1)S(1)}, u32[]{:S(2)}, u32[]{:S(2)}) %all-to-all-start.8) | async-done | bytes 262176 | tf_op jit(solution)/shard_map/all_to_all | solution.py:281
  199.3 5.0 %collective-permute-start.9 = (bf16[768,128]{1,0:T(8,128)(2,1)S(1)}, bf16[768,128]{1,0:T(8,128)(2,1)S(1)}, u32[]{:S(2)}, u32[]{:S(2)}) collective-permute-start(bf16[768,128]{1,0:T(8,128)(2,1)S(1)} %get-tuple-element.94), channel_id=1, source_target_pairs={{0,256},{64,320},{128,384},{192,448},{256,0},{320,64},{384,128},{4... | collective-permute-start | bytes 589832 | tf_op jit(solution)/shard_map/ppermute | solution.py:24
  204.9 9.3 %all_to_all.56 = bf16[8,16,128]{2,1,0:T(8,128)(2,1)S(1)} all-to-all(bf16[8,16,128]{2,1,0:T(8,128)(2,1)S(1)} %get-tuple-element.93), channel_id=1, replica_groups=mesh['y'=8,'z'=8,'c'=2,'x'=4] {'z'}, dimensions={0} | all-to-all | bytes 65536 | tf_op jit(solution)/shard_map/all_to_all | solution.py:404
  215.4 8.5 %all-to-all-start.10 = ((bf16[16,32,128]{2,1,0:T(8,128)(2,1)}), bf16[16,32,128]{2,1,0:T(8,128)(2,1)S(1)}, u32[]{:S(2)}, u32[]{:S(2)}) async-start(bf16[16,32,128]{2,1,0:T(8,128)(2,1)} %shard_map.77), calls=%async_computation.10 | async-start | bytes 262144 | tf_op jit(solution)/shard_map/all_to_all | solution.py:412
  224.9 8.3 %all-to-all-done.10 = bf16[16,32,128]{2,1,0:T(8,128)(2,1)S(1)} async-done(((bf16[16,32,128]{2,1,0:T(8,128)(2,1)}), bf16[16,32,128]{2,1,0:T(8,128)(2,1)S(1)}, u32[]{:S(2)}, u32[]{:S(2)}) %all-to-all-start.10) | async-done | bytes 131104 | tf_op jit(solution)/shard_map/all_to_all | solution.py:412
  (124 shorter events, 56.8 us)
Async XLA Ops:
  6.5 56.7 %all-gather.9.cloned.1.call-start = ((), (), s32[]{:S(2)}) async-start(), calls=%async_computation.13 | async-start | bytes 3932160 | tf_op jit(solution)/shard_map/all_gather | solution.py:286
  9.8 76.0 %copy-start = (f32[768,16]{1,0:T(8,128)}, f32[768,16]{1,0:T(8,128)S(1)}, u32[]{:S(2)}) copy-start(f32[768,16]{1,0:T(8,128)S(1)} %pad_bitcast_fusion.table.refs_5_) | copy-start | bytes 147460
  11.1 24.8 %all-to-all-start = ((bf16[16,6,16,128]{3,2,1,0:T(8,128)(2,1)}), bf16[16,6,16,128]{3,2,1,0:T(8,128)(2,1)S(1)}, u32[]{:S(2)}, u32[]{:S(2)}) async-start(bf16[16,6,16,128]{3,2,1,0:T(8,128)(2,1)} %pad_maximum_fusion), calls=%async_computation | async-start | bytes 786432 | tf_op jit(solution)/shard_map/all_to_all | solution.py:300
  21.3 102.4 %all-gather.5.cloned.1.call-start = ((), (), s32[]{:S(2)}) async-start(), calls=%async_computation.11 | async-start | bytes 3932160 | tf_op jit(solution)/shard_map/all_gather | solution.py:329
  21.6 10.4 %collective-permute-start = (f32[32,128]{1,0:T(8,128)S(1)}, f32[32,128]{1,0:T(8,128)S(1)}, u32[]{:S(2)}, u32[]{:S(2)}) collective-permute-start(f32[32,128]{1,0:T(8,128)S(1)} %broadcast_in_dim.35), channel_id=1, source_target_pairs={{0,0},{4,8},{8,16},{12,24},{16,32},{20,40},{24,48},{28,56},{32,4},... | collective-permute-start | bytes 49160 | tf_op jit(solution)/shard_map/ppermute | solution.py:303
  35.8 19.3 %collective-permute-start.2 = (bf16[768,128]{1,0:T(8,128)(2,1)S(1)}, bf16[768,128]{1,0:T(8,128)(2,1)S(1)}, u32[]{:S(2)}, u32[]{:S(2)}) collective-permute-start(bf16[768,128]{1,0:T(8,128)(2,1)S(1)} %shard_map.64), channel_id=1, source_target_pairs={{0,256},{64,320},{128,384},{192,448},{256,0},{320,64},{384,128},{4... | collective-permute-start | bytes 589832 | tf_op jit(solution)/shard_map/ppermute | solution.py:24
  55.9 20.1 %all-to-all-start.2 = ((bf16[64,16,128]{2,1,0:T(8,128)(2,1)}), bf16[64,16,128]{2,1,0:T(8,128)(2,1)S(1)}, u32[]{:S(2)}, u32[]{:S(2)}) async-start(bf16[64,16,128]{2,1,0:T(8,128)(2,1)} %get-tuple-element.59), calls=%async_computation.2 | async-start | bytes 524288 | tf_op jit(solution)/shard_map/all_to_all | solution.py:284
  64.1 12.0 %collective-permute-start.1 = (bf16[16,2048]{1,0:T(8,128)(2,1)S(1)}, bf16[16,2048]{1,0:T(8,128)(2,1)S(1)}, u32[]{:S(2)}, u32[]{:S(2)}) collective-permute-start(bf16[16,2048]{1,0:T(8,128)(2,1)S(1)} %slice_bitcast_fusion.1.mine_rows), channel_id=1, source_target_pairs={{0,4},{4,0},{1,5},{5,1},{2,6},{6,2},{3,7},{7,3},{8,12},{12,8},{9,1... | collective-permute-start | bytes 196616 | tf_op jit(solution)/shard_map/ppermute | solution.py:28
  76.9 14.5 %all-to-all-start.3 = ((bf16[8,32,128]{2,1,0:T(8,128)(2,1)}), bf16[8,32,128]{2,1,0:T(8,128)(2,1)S(1)}, u32[]{:S(2)}, u32[]{:S(2)}) async-start(bf16[8,32,128]{2,1,0:T(8,128)(2,1)} %shard_map.67), calls=%async_computation.3 | async-start | bytes 131072 | tf_op jit(solution)/shard_map/all_to_all | solution.py:343
  81.9 19.1 %collective-permute-start.3 = (bf16[8,128,128]{2,1,0:T(8,128)(2,1)S(1)}, bf16[8,128,128]{2,1,0:T(8,128)(2,1)S(1)}, u32[]{:S(2)}, u32[]{:S(2)}) collective-permute-start(bf16[8,128,128]{2,1,0:T(8,128)(2,1)S(1)} %bitcast.42), channel_id=1, source_target_pairs={{0,4},{4,0},{1,5},{5,1},{2,6},{6,2},{3,7},{7,3},{8,12},{12,8},{9,1... | collective-permute-start | bytes 786440 | tf_op jit(solution)/shard_map/ppermute | solution.py:28
  87.0 13.9 %collective-permute-start.4 = (bf16[768,128]{1,0:T(8,128)(2,1)S(1)}, bf16[768,128]{1,0:T(8,128)(2,1)S(1)}, u32[]{:S(2)}, u32[]{:S(2)}) collective-permute-start(bf16[768,128]{1,0:T(8,128)(2,1)S(1)} %get-tuple-element.63), channel_id=1, source_target_pairs={{0,128},{64,192},{128,0},{192,64},{256,384},{320,448},{384,256},{4... | collective-permute-start | bytes 589832 | tf_op jit(solution)/shard_map/ppermute | solution.py:24
  92.3 10.8 %all-to-all-start.4 = ((bf16[16,16,128]{2,1,0:T(8,128)(2,1)}), bf16[16,16,128]{2,1,0:T(8,128)(2,1)S(1)}, u32[]{:S(2)}, u32[]{:S(2)}) async-start(bf16[16,16,128]{2,1,0:T(8,128)(2,1)} %bitcast.23), calls=%async_computation.4 | async-start | bytes 131072 | tf_op jit(solution)/shard_map/all_to_all | solution.py:346
  103.9 19.9 %all-to-all-start.5 = ((bf16[64,16,128]{2,1,0:T(8,128)(2,1)}), bf16[64,16,128]{2,1,0:T(8,128)(2,1)S(1)}, u32[]{:S(2)}, u32[]{:S(2)}) async-start(bf16[64,16,128]{2,1,0:T(8,128)(2,1)} %get-tuple-element.65), calls=%async_computation.5 | async-start | bytes 524288 | tf_op jit(solution)/shard_map/all_to_all | solution.py:284
  110.7 65.9 %all-gather.7.cloned.1.call-start = ((), (), s32[]{:S(2)}) async-start(), calls=%async_computation.12 | async-start | bytes 1114112 | tf_op jit(solution)/shard_map/all_gather | solution.py:369
  123.8 6.1 %collective-permute-start.5 = (bf16[8,128,128]{2,1,0:T(8,128)(2,1)S(1)}, bf16[8,128,128]{2,1,0:T(8,128)(2,1)}, u32[]{:S(2)}, u32[]{:S(2)}) collective-permute-start(bf16[8,128,128]{2,1,0:T(8,128)(2,1)S(1)} %bitcast.50), channel_id=1, source_target_pairs={{0,4},{4,0},{1,5},{5,1},{2,6},{6,2},{3,7},{7,3},{8,12},{12,8},{9,1... | collective-permute-start | bytes 786440 | tf_op jit(solution)/shard_map/ppermute | solution.py:28
  137.1 3.7 %collective-permute-start.6 = (bf16[8,128,128]{2,1,0:T(8,128)(2,1)}, bf16[8,128,128]{2,1,0:T(8,128)(2,1)S(1)}, u32[]{:S(2)}, u32[]{:S(2)}) collective-permute-start(bf16[8,128,128]{2,1,0:T(8,128)(2,1)} %get-tuple-element.74), channel_id=1, source_target_pairs={{0,4},{4,0},{1,5},{5,1},{2,6},{6,2},{3,7},{7,3},{8,12},{12,8},{9,1... | collective-permute-start | bytes 786440 | tf_op jit(solution)/shard_map/ppermute | solution.py:28
  142.6 19.5 %all-to-all-start.6 = ((bf16[64,16,128]{2,1,0:T(8,128)(2,1)}), bf16[64,16,128]{2,1,0:T(8,128)(2,1)}, u32[]{:S(2)}, u32[]{:S(2)}) async-start(bf16[64,16,128]{2,1,0:T(8,128)(2,1)} %bitcast.26), calls=%async_computation.6 | async-start | bytes 524288 | tf_op jit(solution)/shard_map/all_to_all | solution.py:281
  153.2 61.1 %copy-start.13 = (bf16[16,1,16,128]{3,2,1,0:T(8,128)(2,1)S(1)}, bf16[16,1,16,128]{3,2,1,0:T(8,128)(2,1)}, u32[]{:S(2)}) copy-start(bf16[16,1,16,128]{3,2,1,0:T(8,128)(2,1)} %get-tuple-element.107) | copy-start | bytes 196612
  153.2 7.1 %collective-permute-start.7 = (bf16[8,128,128]{2,1,0:T(8,128)(2,1)S(1)}, bf16[8,128,128]{2,1,0:T(8,128)(2,1)S(1)}, u32[]{:S(2)}, u32[]{:S(2)}) collective-permute-start(bf16[8,128,128]{2,1,0:T(8,128)(2,1)S(1)} %get-tuple-element.77), channel_id=1, source_target_pairs={{0,4},{4,0},{1,5},{5,1},{2,6},{6,2},{3,7},{7,3},{8,12},{12,8},{9,1... | collective-permute-start | bytes 786440 | tf_op jit(solution)/shard_map/ppermute | solution.py:28
  155.6 14.7 %collective-permute-start.8 = (bf16[768,128]{1,0:T(8,128)(2,1)}, bf16[768,128]{1,0:T(8,128)(2,1)S(1)}, u32[]{:S(2)}, u32[]{:S(2)}) collective-permute-start(bf16[768,128]{1,0:T(8,128)(2,1)} %get-tuple-element.75.rounded), channel_id=1, source_target_pairs={{0,128},{64,192},{128,0},{192,64},{256,384},{320,448},{384,256},{4... | collective-permute-start | bytes 589832 | tf_op jit(solution)/shard_map/ppermute | solution.py:24
  163.8 12.8 %all-to-all-start.7 = ((bf16[16,16,128]{2,1,0:T(8,128)(2,1)}), bf16[16,16,128]{2,1,0:T(8,128)(2,1)S(1)}, u32[]{:S(2)}, u32[]{:S(2)}) async-start(bf16[16,16,128]{2,1,0:T(8,128)(2,1)} %get-tuple-element.81), calls=%async_computation.7 | async-start | bytes 131072 | tf_op jit(solution)/shard_map/all_to_all | solution.py:393
  180.2 19.1 %all-to-all-start.8 = ((bf16[64,16,128]{2,1,0:T(8,128)(2,1)}), bf16[64,16,128]{2,1,0:T(8,128)(2,1)S(1)}, u32[]{:S(2)}, u32[]{:S(2)}) async-start(bf16[64,16,128]{2,1,0:T(8,128)(2,1)} %bitcast.28), calls=%async_computation.8 | async-start | bytes 524288 | tf_op jit(solution)/shard_map/all_to_all | solution.py:281
  199.3 15.0 %collective-permute-start.9 = (bf16[768,128]{1,0:T(8,128)(2,1)S(1)}, bf16[768,128]{1,0:T(8,128)(2,1)S(1)}, u32[]{:S(2)}, u32[]{:S(2)}) collective-permute-start(bf16[768,128]{1,0:T(8,128)(2,1)S(1)} %get-tuple-element.94), channel_id=1, source_target_pairs={{0,256},{64,320},{128,384},{192,448},{256,0},{320,64},{384,128},{4... | collective-permute-start | bytes 589832 | tf_op jit(solution)/shard_map/ppermute | solution.py:24
  215.4 17.7 %all-to-all-start.10 = ((bf16[16,32,128]{2,1,0:T(8,128)(2,1)}), bf16[16,32,128]{2,1,0:T(8,128)(2,1)S(1)}, u32[]{:S(2)}, u32[]{:S(2)}) async-start(bf16[16,32,128]{2,1,0:T(8,128)(2,1)} %shard_map.77), calls=%async_computation.10 | async-start | bytes 262144 | tf_op jit(solution)/shard_map/all_to_all | solution.py:412
  (23 other events, 389.0 us)
Sparse Core Ops, SparseCore 0:
  9.6 50.3 all-gather.8
  62.1 45.1 all-gather.4
  123.9 36.1 all-gather.6

commit v7 on v6

--- a/solution.py
+++ b/solution.py
@@ -396,10 +396,8 @@
     back1, term0 = pl.pallas_call(
         cross_back, out_shape=(shape((chunk, width), F32), shape((ny, half, width), BF)),
         in_specs=[core_spec] + [vmem] * 5, out_specs=(vmem, vmem),
-        compiler_params=params,
     )(core_ref, tile1, t1, cross, term0, away0)
     met = reduce_yz(term0)
-    met, send = lax.optimization_barrier((met, send))
     _, spread = spread_sum(met, nz, own0, own_pivots[:rb])
     t0 = lax.all_to_all(spread, "z", 0, 0).reshape(half, width)
     t0, got = lax.optimization_barrier((t0, swap_y(send, outer, ny)))

time: 242 us -> 239 us (0.988)
  blocking collectives: 23.7 us -> 14.4 us
  starting transfers between devices: 93.9 us -> 101 us
    all_to_all x1 -> x0, blocking collectives: 9.33 us -> none  [shards(): t0 = lax.all_to_all(spread, 'z', 0, 0).reshape(half, width)]
    all_to_all x2, waiting for transfers between devices: 14.3 us -> 7.45 us  [reduce_yz(): lax.all_to_all(mine.astype(BF).reshape(ny * nz, rb, width), ('y', 'z'), 0...]
    all_to_all x0 -> x1, waiting for transfers between devices: none -> 4.8 us  [shards(): t0 = lax.all_to_all(spread, 'z', 0, 0).reshape(half, width)]
    all_to_all x0 -> x1, starting transfers between devices: none -> 3.58 us  [shards(): t0 = lax.all_to_all(spread, 'z', 0, 0).reshape(half, width)]
  transfers between devices with their start and end apart: 22 -> 23, of which waited for: 12 -> 14; matrix products, arithmetic and copies ran while one was open for 3% -> 3% of each run, Pallas kernels for 10% -> 10%
where the time goes in v7:
time: 239 us; the launch traced here: 238 us
  starting transfers between devices  101 us (42%)
  waiting for transfers between devices  67 us (28%)
  Pallas kernels  27.4 us (11%)
  blocking collectives  14.4 us (6%)
  between operations  13.6 us (6%)
  local copies, waits for them, and re-layouts  9.55 us (4%)
  other arithmetic  4.37 us (2%)
    ppermute x4, starting transfers between devices, swap_y(): return lax.ppermute(v, 'y', [(i, i ^ bit) for i in range(count)])  19 us
    all_to_all x2, waiting for transfers between devices, gather_yz(): return lax.all_to_all(spread, ('y', 'z'), 0, 0).reshape(ny, half, width)  17.2 us
    ppermute x5, starting transfers between devices, swap_core(): return lax.ppermute(v, 'c', [(0, 1), (1, 0)])  16.2 us
    all_to_all x1, blocking collectives, shards(): met = lax.all_to_all(part.reshape(nz, rb, width), 'z', 0, 0)  14.4 us
    all_to_all x2, starting transfers between devices, gather_yz(): return lax.all_to_all(spread, ('y', 'z'), 0, 0).reshape(ny, half, width)  13.5 us
    all_to_all x2, starting transfers between devices, reduce_yz(): lax.all_to_all(mine.astype(BF).reshape(ny * nz, rb, width), ('y', 'z'), 0...  11.8 us
    all_to_all x1, starting transfers between devices, shards(): arrived = lax.all_to_all(message, ('y', 'c'), 0, 0)  10.2 us
    all_to_all x1, starting transfers between devices, shards(): lax.all_to_all(last, ('y', 'c'), 0, 0)  9.84 us
  transfers between devices with their start and end apart: 23, of which 14 were waited for; matrix products, arithmetic and copies ran while one was open for 3% of the time, Pallas kernels for 10%

profile of v7, /device:TPU:1, one launch (start us, length us, event | category | flops | bytes accessed | tf_op | source)
XLA Modules:
  0.0 237.9 jit_solution(1535309145861177178)
XLA Ops:
  11.1 10.2 %all-to-all-start = ((bf16[16,6,16,128]{3,2,1,0:T(8,128)(2,1)}), bf16[16,6,16,128]{3,2,1,0:T(8,128)(2,1)S(1)}, u32[]{:S(2)}, u32[]{:S(2)}) async-start(bf16[16,6,16,128]{3,2,1,0:T(8,128)(2,1)} %pad_maximum_fusion), calls=%async_computation | async-start | bytes 786432 | tf_op jit(solution)/shard_map/all_to_all | solution.py:300
  24.2 7.9 %collective-permute-done = f32[32,128]{1,0:T(8,128)S(1)} collective-permute-done((f32[32,128]{1,0:T(8,128)S(1)}, f32[32,128]{1,0:T(8,128)S(1)}, u32[]{:S(2)}, u32[]{:S(2)}) %collective-permute-start) | collective-permute-done | bytes 16416 | tf_op jit(solution)/shard_map/ppermute | solution.py:303
  40.8 14.4 %all_to_all.55.refs_0_ = bf16[8,16,128]{2,1,0:T(8,128)(2,1)S(1)} all-to-all(bf16[8,16,128]{2,1,0:T(8,128)(2,1)S(1)} %bitcast.48), channel_id=1, replica_groups=mesh['y'=8,'z'=8,'c'=2,'x'=4] {'z'}, dimensions={0} | all-to-all | bytes 65536 | tf_op jit(solution)/shard_map/all_to_all | solution.py:325
  55.9 7.3 %all-to-all-start.2 = ((bf16[64,16,128]{2,1,0:T(8,128)(2,1)}), bf16[64,16,128]{2,1,0:T(8,128)(2,1)S(1)}, u32[]{:S(2)}, u32[]{:S(2)}) async-start(bf16[64,16,128]{2,1,0:T(8,128)(2,1)} %get-tuple-element.57), calls=%async_computation.2 | async-start | bytes 524288 | tf_op jit(solution)/shard_map/all_to_all | solution.py:284
  66.9 9.2 %all-to-all-done.2 = bf16[64,16,128]{2,1,0:T(8,128)(2,1)S(1)} async-done(((bf16[64,16,128]{2,1,0:T(8,128)(2,1)}), bf16[64,16,128]{2,1,0:T(8,128)(2,1)S(1)}, u32[]{:S(2)}, u32[]{:S(2)}) %all-to-all-start.2) | async-done | bytes 262176 | tf_op jit(solution)/shard_map/all_to_all | solution.py:284
  76.9 4.3 %all-to-all-start.3 = ((bf16[8,32,128]{2,1,0:T(8,128)(2,1)}), bf16[8,32,128]{2,1,0:T(8,128)(2,1)S(1)}, u32[]{:S(2)}, u32[]{:S(2)}) async-start(bf16[8,32,128]{2,1,0:T(8,128)(2,1)} %shard_map.67), calls=%async_computation.3 | async-start | bytes 131072 | tf_op jit(solution)/shard_map/all_to_all | solution.py:343
  86.2 4.5 %collective-permute-start.4 = (bf16[768,128]{1,0:T(8,128)(2,1)S(1)}, bf16[768,128]{1,0:T(8,128)(2,1)S(1)}, u32[]{:S(2)}, u32[]{:S(2)}) collective-permute-start(bf16[768,128]{1,0:T(8,128)(2,1)S(1)} %get-tuple-element.61), channel_id=1, source_target_pairs={{0,128},{64,192},{128,0},{192,64},{256,384},{320,448},{384,256},{4... | collective-permute-start | bytes 589832 | tf_op jit(solution)/shard_map/ppermute | solution.py:24
  91.6 4.2 %all-to-all-start.4 = ((bf16[16,16,128]{2,1,0:T(8,128)(2,1)}), bf16[16,16,128]{2,1,0:T(8,128)(2,1)S(1)}, u32[]{:S(2)}, u32[]{:S(2)}) async-start(bf16[16,16,128]{2,1,0:T(8,128)(2,1)} %bitcast.23), calls=%async_computation.4 | async-start | bytes 131072 | tf_op jit(solution)/shard_map/all_to_all | solution.py:346
  95.8 4.4 %collective-permute-done.4.got = bf16[768,128]{1,0:T(8,128)(2,1)S(1)} collective-permute-done((bf16[768,128]{1,0:T(8,128)(2,1)S(1)}, bf16[768,128]{1,0:T(8,128)(2,1)S(1)}, u32[]{:S(2)}, u32[]{:S(2)}) %collective-permute-start.4) | collective-permute-done | bytes 196640 | tf_op jit(solution)/shard_map/ppermute | solution.py:24
  103.7 6.2 %all-to-all-start.5 = ((bf16[64,16,128]{2,1,0:T(8,128)(2,1)}), bf16[64,16,128]{2,1,0:T(8,128)(2,1)S(1)}, u32[]{:S(2)}, u32[]{:S(2)}) async-start(bf16[64,16,128]{2,1,0:T(8,128)(2,1)} %get-tuple-element.63), calls=%async_computation.5 | async-start | bytes 524288 | tf_op jit(solution)/shard_map/all_to_all | solution.py:284
  110.1 4.9 %shard_map.70.refs_4_ = f32[768,128]{1,0:T(8,128)} custom-call(s32[1]{0:T(128)} %bitcast.core.refs_0_, bf16[768,2048]{1,0:T(8,128)(2,1)} %bitcast.39, bf16[8,128,128]{2,1,0:T(8,128)(2,1)} %bitcast.43, bf16[8,128,128]{2,1,0:T(8,128)(2,1)} %copy-done.15, f32[768,128]{1,0:T(8,128)} %copy-done.9, bf16[768,128]{1,0:T(8,128)(2,1)} %copy-done.19), custom_call_target="tpu_custom_call" | custom-call | flops 402653184 | bytes 3145728 | tf_op jit(solution)/shard_map/pallas_call | solution.py:360
  114.9 8.1 %all-to-all-done.5 = bf16[64,16,128]{2,1,0:T(8,128)(2,1)S(1)} async-done(((bf16[64,16,128]{2,1,0:T(8,128)(2,1)}), bf16[64,16,128]{2,1,0:T(8,128)(2,1)S(1)}, u32[]{:S(2)}, u32[]{:S(2)}) %all-to-all-start.5) | async-done | bytes 262176 | tf_op jit(solution)/shard_map/all_to_all | solution.py:284
  123.0 4.8 %collective-permute-start.5 = (bf16[8,128,128]{2,1,0:T(8,128)(2,1)S(1)}, bf16[8,128,128]{2,1,0:T(8,128)(2,1)}, u32[]{:S(2)}, u32[]{:S(2)}) collective-permute-start(bf16[8,128,128]{2,1,0:T(8,128)(2,1)S(1)} %bitcast.49), channel_id=1, source_target_pairs={{0,4},{4,0},{1,5},{5,1},{2,6},{6,2},{3,7},{7,3},{8,12},{12,8},{9,1... | collective-permute-start | bytes 786440 | tf_op jit(solution)/shard_map/ppermute | solution.py:28
  129.1 7.3 %shard_map.71 = (f32[768,128]{1,0:T(8,128)}, bf16[768,128]{1,0:T(8,128)(2,1)}, f32[8,128,128]{2,1,0:T(8,128)}, bf16[8,128,128]{2,1,0:T(8,128)(2,1)}) custom-call(s32[1]{0:T(128)} %bitcast.core.refs_0_, bf16[768,2048]{1,0:T(8,128)(2,1)} %all-gather.5.cloned.1.call-done.refs_1_, bf16[8,128,128]{2,1,0:T(8,128)(2,1)} %bitcast.50, ...), custom_call_target="tpu_custom_call" | custom-call | flops 402653184 | bytes 3145728 | tf_op jit(solution)/shard_map/pallas_call | solution.py:372
  141.9 5.5 %all-to-all-start.6 = ((bf16[64,16,128]{2,1,0:T(8,128)(2,1)}), bf16[64,16,128]{2,1,0:T(8,128)(2,1)}, u32[]{:S(2)}, u32[]{:S(2)}) async-start(bf16[64,16,128]{2,1,0:T(8,128)(2,1)} %bitcast.26), calls=%async_computation.6 | async-start | bytes 524288 | tf_op jit(solution)/shard_map/all_to_all | solution.py:281
  147.4 4.2 %shard_map.72 = (f32[8,128,128]{2,1,0:T(8,128)S(1)}, bf16[8,128,128]{2,1,0:T(8,128)(2,1)S(1)}) custom-call(s32[1]{0:T(128)} %bitcast.core.refs_0_, bf16[768,2048]{1,0:T(8,128)(2,1)S(1)} %bitcast.40, bf16[768,128]{1,0:T(8,128)(2,1)} %get-tuple-element.73.rounded), custom_call_target="tpu_custom_call" | custom-call | flops 402653184 | bytes 3145728 | tf_op jit(solution)/shard_map/pallas_call | solution.py:382
  163.2 5.5 %all-to-all-start.7 = ((bf16[16,16,128]{2,1,0:T(8,128)(2,1)}), bf16[16,16,128]{2,1,0:T(8,128)(2,1)S(1)}, u32[]{:S(2)}, u32[]{:S(2)}) async-start(bf16[16,16,128]{2,1,0:T(8,128)(2,1)} %get-tuple-element.79), calls=%async_computation.7 | async-start | bytes 131072 | tf_op jit(solution)/shard_map/all_to_all | solution.py:393
  170.2 5.6 %all-to-all-done.7 = bf16[16,16,128]{2,1,0:T(8,128)(2,1)S(1)} async-done(((bf16[16,16,128]{2,1,0:T(8,128)(2,1)}), bf16[16,16,128]{2,1,0:T(8,128)(2,1)S(1)}, u32[]{:S(2)}, u32[]{:S(2)}) %all-to-all-start.7) | async-done | bytes 65568 | tf_op jit(solution)/shard_map/all_to_all | solution.py:393
  179.3 6.3 %all-to-all-start.8 = ((bf16[64,16,128]{2,1,0:T(8,128)(2,1)}), bf16[64,16,128]{2,1,0:T(8,128)(2,1)S(1)}, u32[]{:S(2)}, u32[]{:S(2)}) async-start(bf16[64,16,128]{2,1,0:T(8,128)(2,1)} %bitcast.54), calls=%async_computation.8 | async-start | bytes 524288 | tf_op jit(solution)/shard_map/all_to_all | solution.py:281
  186.0 6.9 %collective-permute-start.9 = (bf16[768,128]{1,0:T(8,128)(2,1)S(1)}, bf16[768,128]{1,0:T(8,128)(2,1)S(1)}, u32[]{:S(2)}, u32[]{:S(2)}) collective-permute-start(bf16[768,128]{1,0:T(8,128)(2,1)S(1)} %get-tuple-element.90), channel_id=1, source_target_pairs={{0,256},{64,320},{128,384},{192,448},{256,0},{320,64},{384,128},{4... | collective-permute-start | bytes 589832 | tf_op jit(solution)/shard_map/ppermute | solution.py:24
  193.0 5.5 %all-to-all-done.8.refs_0_ = bf16[64,16,128]{2,1,0:T(8,128)(2,1)S(1)} async-done(((bf16[64,16,128]{2,1,0:T(8,128)(2,1)}), bf16[64,16,128]{2,1,0:T(8,128)(2,1)S(1)}, u32[]{:S(2)}, u32[]{:S(2)}) %all-to-all-start.8) | async-done | bytes 262176 | tf_op jit(solution)/shard_map/all_to_all | solution.py:281
  204.9 4.8 %all-to-all-done.9 = bf16[8,16,128]{2,1,0:T(8,128)(2,1)S(1)} async-done(((bf16[8,16,128]{2,1,0:T(8,128)(2,1)}), bf16[8,16,128]{2,1,0:T(8,128)(2,1)S(1)}, u32[]{:S(2)}, u32[]{:S(2)}) %all-to-all-start.9) | async-done | bytes 32800 | tf_op jit(solution)/shard_map/all_to_all | solution.py:402
  211.7 9.8 %all-to-all-start.10 = ((bf16[16,32,128]{2,1,0:T(8,128)(2,1)}), bf16[16,32,128]{2,1,0:T(8,128)(2,1)S(1)}, u32[]{:S(2)}, u32[]{:S(2)}) async-start(bf16[16,32,128]{2,1,0:T(8,128)(2,1)} %shard_map.77), calls=%async_computation.10 | async-start | bytes 262144 | tf_op jit(solution)/shard_map/all_to_all | solution.py:410
  222.5 8.3 %all-to-all-done.10 = bf16[16,32,128]{2,1,0:T(8,128)(2,1)S(1)} async-done(((bf16[16,32,128]{2,1,0:T(8,128)(2,1)}), bf16[16,32,128]{2,1,0:T(8,128)(2,1)S(1)}, u32[]{:S(2)}, u32[]{:S(2)}) %all-to-all-start.10) | async-done | bytes 131104 | tf_op jit(solution)/shard_map/all_to_all | solution.py:410
  (127 shorter events, 64.2 us)
Async XLA Ops:
  6.5 56.7 %all-gather.9.cloned.1.call-start = ((), (), s32[]{:S(2)}) async-start(), calls=%async_computation.13 | async-start | bytes 3932160 | tf_op jit(solution)/shard_map/all_gather | solution.py:286
  9.8 76.0 %copy-start = (f32[768,16]{1,0:T(8,128)}, f32[768,16]{1,0:T(8,128)S(1)}, u32[]{:S(2)}) copy-start(f32[768,16]{1,0:T(8,128)S(1)} %pad_bitcast_fusion.table.refs_5_) | copy-start | bytes 147460
  11.1 24.8 %all-to-all-start = ((bf16[16,6,16,128]{3,2,1,0:T(8,128)(2,1)}), bf16[16,6,16,128]{3,2,1,0:T(8,128)(2,1)S(1)}, u32[]{:S(2)}, u32[]{:S(2)}) async-start(bf16[16,6,16,128]{3,2,1,0:T(8,128)(2,1)} %pad_maximum_fusion), calls=%async_computation | async-start | bytes 786432 | tf_op jit(solution)/shard_map/all_to_all | solution.py:300
  21.3 101.7 %all-gather.5.cloned.1.call-start = ((), (), s32[]{:S(2)}) async-start(), calls=%async_computation.11 | async-start | bytes 3932160 | tf_op jit(solution)/shard_map/all_gather | solution.py:329
  21.6 10.4 %collective-permute-start = (f32[32,128]{1,0:T(8,128)S(1)}, f32[32,128]{1,0:T(8,128)S(1)}, u32[]{:S(2)}, u32[]{:S(2)}) collective-permute-start(f32[32,128]{1,0:T(8,128)S(1)} %broadcast_in_dim.35), channel_id=1, source_target_pairs={{0,0},{4,8},{8,16},{12,24},{16,32},{20,40},{24,48},{28,56},{32,4},... | collective-permute-start | bytes 49160 | tf_op jit(solution)/shard_map/ppermute | solution.py:303
  35.8 19.3 %collective-permute-start.2 = (bf16[768,128]{1,0:T(8,128)(2,1)S(1)}, bf16[768,128]{1,0:T(8,128)(2,1)S(1)}, u32[]{:S(2)}, u32[]{:S(2)}) collective-permute-start(bf16[768,128]{1,0:T(8,128)(2,1)S(1)} %shard_map.64), channel_id=1, source_target_pairs={{0,256},{64,320},{128,384},{192,448},{256,0},{320,64},{384,128},{4... | collective-permute-start | bytes 589832 | tf_op jit(solution)/shard_map/ppermute | solution.py:24
  55.9 20.1 %all-to-all-start.2 = ((bf16[64,16,128]{2,1,0:T(8,128)(2,1)}), bf16[64,16,128]{2,1,0:T(8,128)(2,1)S(1)}, u32[]{:S(2)}, u32[]{:S(2)}) async-start(bf16[64,16,128]{2,1,0:T(8,128)(2,1)} %get-tuple-element.57), calls=%async_computation.2 | async-start | bytes 524288 | tf_op jit(solution)/shard_map/all_to_all | solution.py:284
  64.1 12.0 %collective-permute-start.1 = (bf16[16,2048]{1,0:T(8,128)(2,1)S(1)}, bf16[16,2048]{1,0:T(8,128)(2,1)S(1)}, u32[]{:S(2)}, u32[]{:S(2)}) collective-permute-start(bf16[16,2048]{1,0:T(8,128)(2,1)S(1)} %slice_bitcast_fusion.1.mine_rows), channel_id=1, source_target_pairs={{0,4},{4,0},{1,5},{5,1},{2,6},{6,2},{3,7},{7,3},{8,12},{12,8},{9,1... | collective-permute-start | bytes 196616 | tf_op jit(solution)/shard_map/ppermute | solution.py:28
  76.9 13.8 %all-to-all-start.3 = ((bf16[8,32,128]{2,1,0:T(8,128)(2,1)}), bf16[8,32,128]{2,1,0:T(8,128)(2,1)S(1)}, u32[]{:S(2)}, u32[]{:S(2)}) async-start(bf16[8,32,128]{2,1,0:T(8,128)(2,1)} %shard_map.67), calls=%async_computation.3 | async-start | bytes 131072 | tf_op jit(solution)/shard_map/all_to_all | solution.py:343
  81.8 18.4 %collective-permute-start.3 = (bf16[8,128,128]{2,1,0:T(8,128)(2,1)S(1)}, bf16[8,128,128]{2,1,0:T(8,128)(2,1)S(1)}, u32[]{:S(2)}, u32[]{:S(2)}) collective-permute-start(bf16[8,128,128]{2,1,0:T(8,128)(2,1)S(1)} %bitcast.42), channel_id=1, source_target_pairs={{0,4},{4,0},{1,5},{5,1},{2,6},{6,2},{3,7},{7,3},{8,12},{12,8},{9,1... | collective-permute-start | bytes 786440 | tf_op jit(solution)/shard_map/ppermute | solution.py:28
  86.2 13.9 %collective-permute-start.4 = (bf16[768,128]{1,0:T(8,128)(2,1)S(1)}, bf16[768,128]{1,0:T(8,128)(2,1)S(1)}, u32[]{:S(2)}, u32[]{:S(2)}) collective-permute-start(bf16[768,128]{1,0:T(8,128)(2,1)S(1)} %get-tuple-element.61), channel_id=1, source_target_pairs={{0,128},{64,192},{128,0},{192,64},{256,384},{320,448},{384,256},{4... | collective-permute-start | bytes 589832 | tf_op jit(solution)/shard_map/ppermute | solution.py:24
  91.6 11.4 %all-to-all-start.4 = ((bf16[16,16,128]{2,1,0:T(8,128)(2,1)}), bf16[16,16,128]{2,1,0:T(8,128)(2,1)S(1)}, u32[]{:S(2)}, u32[]{:S(2)}) async-start(bf16[16,16,128]{2,1,0:T(8,128)(2,1)} %bitcast.23), calls=%async_computation.4 | async-start | bytes 131072 | tf_op jit(solution)/shard_map/all_to_all | solution.py:346
  103.7 19.3 %all-to-all-start.5 = ((bf16[64,16,128]{2,1,0:T(8,128)(2,1)}), bf16[64,16,128]{2,1,0:T(8,128)(2,1)S(1)}, u32[]{:S(2)}, u32[]{:S(2)}) async-start(bf16[64,16,128]{2,1,0:T(8,128)(2,1)} %get-tuple-element.63), calls=%async_computation.5 | async-start | bytes 524288 | tf_op jit(solution)/shard_map/all_to_all | solution.py:284
  109.9 65.9 %all-gather.7.cloned.1.call-start = ((), (), s32[]{:S(2)}) async-start(), calls=%async_computation.12 | async-start | bytes 1114112 | tf_op jit(solution)/shard_map/all_gather | solution.py:369
  123.0 6.1 %collective-permute-start.5 = (bf16[8,128,128]{2,1,0:T(8,128)(2,1)S(1)}, bf16[8,128,128]{2,1,0:T(8,128)(2,1)}, u32[]{:S(2)}, u32[]{:S(2)}) collective-permute-start(bf16[8,128,128]{2,1,0:T(8,128)(2,1)S(1)} %bitcast.49), channel_id=1, source_target_pairs={{0,4},{4,0},{1,5},{5,1},{2,6},{6,2},{3,7},{7,3},{8,12},{12,8},{9,1... | collective-permute-start | bytes 786440 | tf_op jit(solution)/shard_map/ppermute | solution.py:28
  136.4 3.7 %collective-permute-start.6 = (bf16[8,128,128]{2,1,0:T(8,128)(2,1)}, bf16[8,128,128]{2,1,0:T(8,128)(2,1)S(1)}, u32[]{:S(2)}, u32[]{:S(2)}) collective-permute-start(bf16[8,128,128]{2,1,0:T(8,128)(2,1)} %get-tuple-element.72), channel_id=1, source_target_pairs={{0,4},{4,0},{1,5},{5,1},{2,6},{6,2},{3,7},{7,3},{8,12},{12,8},{9,1... | collective-permute-start | bytes 786440 | tf_op jit(solution)/shard_map/ppermute | solution.py:28
  141.9 19.6 %all-to-all-start.6 = ((bf16[64,16,128]{2,1,0:T(8,128)(2,1)}), bf16[64,16,128]{2,1,0:T(8,128)(2,1)}, u32[]{:S(2)}, u32[]{:S(2)}) async-start(bf16[64,16,128]{2,1,0:T(8,128)(2,1)} %bitcast.26), calls=%async_computation.6 | async-start | bytes 524288 | tf_op jit(solution)/shard_map/all_to_all | solution.py:281
  152.4 7.1 %collective-permute-start.7 = (bf16[8,128,128]{2,1,0:T(8,128)(2,1)S(1)}, bf16[8,128,128]{2,1,0:T(8,128)(2,1)S(1)}, u32[]{:S(2)}, u32[]{:S(2)}) collective-permute-start(bf16[8,128,128]{2,1,0:T(8,128)(2,1)S(1)} %get-tuple-element.75), channel_id=1, source_target_pairs={{0,4},{4,0},{1,5},{5,1},{2,6},{6,2},{3,7},{7,3},{8,12},{12,8},{9,1... | collective-permute-start | bytes 786440 | tf_op jit(solution)/shard_map/ppermute | solution.py:28
  154.8 15.4 %collective-permute-start.8 = (bf16[768,128]{1,0:T(8,128)(2,1)}, bf16[768,128]{1,0:T(8,128)(2,1)S(1)}, u32[]{:S(2)}, u32[]{:S(2)}) collective-permute-start(bf16[768,128]{1,0:T(8,128)(2,1)} %get-tuple-element.73.rounded), channel_id=1, source_target_pairs={{0,128},{64,192},{128,0},{192,64},{256,384},{320,448},{384,256},{4... | collective-permute-start | bytes 589832 | tf_op jit(solution)/shard_map/ppermute | solution.py:24
  163.2 12.7 %all-to-all-start.7 = ((bf16[16,16,128]{2,1,0:T(8,128)(2,1)}), bf16[16,16,128]{2,1,0:T(8,128)(2,1)S(1)}, u32[]{:S(2)}, u32[]{:S(2)}) async-start(bf16[16,16,128]{2,1,0:T(8,128)(2,1)} %get-tuple-element.79), calls=%async_computation.7 | async-start | bytes 131072 | tf_op jit(solution)/shard_map/all_to_all | solution.py:393
  179.3 19.2 %all-to-all-start.8 = ((bf16[64,16,128]{2,1,0:T(8,128)(2,1)}), bf16[64,16,128]{2,1,0:T(8,128)(2,1)S(1)}, u32[]{:S(2)}, u32[]{:S(2)}) async-start(bf16[64,16,128]{2,1,0:T(8,128)(2,1)} %bitcast.54), calls=%async_computation.8 | async-start | bytes 524288 | tf_op jit(solution)/shard_map/all_to_all | solution.py:281
  186.0 18.8 %collective-permute-start.9 = (bf16[768,128]{1,0:T(8,128)(2,1)S(1)}, bf16[768,128]{1,0:T(8,128)(2,1)S(1)}, u32[]{:S(2)}, u32[]{:S(2)}) collective-permute-start(bf16[768,128]{1,0:T(8,128)(2,1)S(1)} %get-tuple-element.90), channel_id=1, source_target_pairs={{0,256},{64,320},{128,384},{192,448},{256,0},{320,64},{384,128},{4... | collective-permute-start | bytes 589832 | tf_op jit(solution)/shard_map/ppermute | solution.py:24
  199.2 10.5 %all-to-all-start.9 = ((bf16[8,16,128]{2,1,0:T(8,128)(2,1)}), bf16[8,16,128]{2,1,0:T(8,128)(2,1)S(1)}, u32[]{:S(2)}, u32[]{:S(2)}) async-start(bf16[8,16,128]{2,1,0:T(8,128)(2,1)} %get-tuple-element.87), calls=%async_computation.9 | async-start | bytes 65536 | tf_op jit(solution)/shard_map/all_to_all | solution.py:402
  211.7 19.0 %all-to-all-start.10 = ((bf16[16,32,128]{2,1,0:T(8,128)(2,1)}), bf16[16,32,128]{2,1,0:T(8,128)(2,1)S(1)}, u32[]{:S(2)}, u32[]{:S(2)}) async-start(bf16[16,32,128]{2,1,0:T(8,128)(2,1)} %shard_map.77), calls=%async_computation.10 | async-start | bytes 262144 | tf_op jit(solution)/shard_map/all_to_all | solution.py:410
  (25 other events, 477.9 us)
Sparse Core Ops, SparseCore 0:
  9.6 50.3 all-gather.8
  62.1 45.1 all-gather.4
  123.1 36.1 all-gather.6

commit v8 on v7

--- a/solution.py
+++ b/solution.py
@@ -306,7 +306,7 @@
     shape = jax.ShapeDtypeStruct
     whole, sent = shape((rows, width), F32), shape((rows, width), BF)
     send = elementwise(left_send, sent, rhs, table)
-    arrived, own_pivots, send = lax.optimization_barrier((arrived, own_pivots, send))
+    arrived, own_pivots = lax.optimization_barrier((arrived, own_pivots))
     got = swap_y(send, outer, ny)
 
     small = arrived[:, 5].astype(F32)

time: 239 us -> 236 us (0.987)
  blocking collectives: 14.4 us -> 0 us
  starting transfers between devices: 101 us -> 111 us
    all_to_all x1 -> x0, blocking collectives: 14.4 us -> none  [shards(): met = lax.all_to_all(part.reshape(nz, rb, width), 'z', 0, 0)]
    all_to_all x0 -> x1, starting transfers between devices: none -> 8.43 us  [shards(): met = lax.all_to_all(part.reshape(nz, rb, width), 'z', 0, 0)]
    ppermute x1, waiting for transfers between devices: 7.86 us -> 0.39 us  [shards(): lax.ppermute(jnp.broadcast_to(table[:low, PIV:PIV + 1], (low, width)), ('...]
    all_to_all x0 -> x1, waiting for transfers between devices: none -> 7.44 us  [shards(): met = lax.all_to_all(part.reshape(nz, rb, width), 'z', 0, 0)]
    ppermute x4, starting transfers between devices: 19 us -> 22.9 us  [swap_y(): return lax.ppermute(v, 'y', [(i, i ^ bit) for i in range(count)])]
  transfers between devices with their start and end apart: 23 -> 24, of which waited for: 14 -> 15; matrix products, arithmetic and copies ran while one was open for 3% -> 4% of each run, Pallas kernels for 10% -> 10%
where the time goes in v8:
time: 236 us; the launch traced here: 235 us
  starting transfers between devices  111 us (47%)
  waiting for transfers between devices  67.1 us (28%)
  Pallas kernels  28 us (12%)
  between operations  13.6 us (6%)
  local copies, waits for them, and re-layouts  9.57 us (4%)
  other arithmetic  4.37 us (2%)
    ppermute x4, starting transfers between devices, swap_y(): return lax.ppermute(v, 'y', [(i, i ^ bit) for i in range(count)])  22.9 us
    all_to_all x2, waiting for transfers between devices, gather_yz(): return lax.all_to_all(spread, ('y', 'z'), 0, 0).reshape(ny, half, width)  17.1 us
    ppermute x5, starting transfers between devices, swap_core(): return lax.ppermute(v, 'c', [(0, 1), (1, 0)])  16.5 us
    all_to_all x2, starting transfers between devices, gather_yz(): return lax.all_to_all(spread, ('y', 'z'), 0, 0).reshape(ny, half, width)  11.9 us
    all_to_all x2, starting transfers between devices, reduce_yz(): lax.all_to_all(mine.astype(BF).reshape(ny * nz, rb, width), ('y', 'z'), 0...  11.8 us
    all_to_all x1, starting transfers between devices, shards(): arrived = lax.all_to_all(message, ('y', 'c'), 0, 0)  10.2 us
    all_to_all x1, starting transfers between devices, shards(): lax.all_to_all(last, ('y', 'c'), 0, 0)  9.77 us
    all_to_all x1, starting transfers between devices, shards(): met = lax.all_to_all(part.reshape(nz, rb, width), 'z', 0, 0)  8.43 us
  transfers between devices with their start and end apart: 24, of which 15 were waited for; matrix products, arithmetic and copies ran while one was open for 4% of the time, Pallas kernels for 10%

profile of v8, /device:TPU:1, one launch (start us, length us, event | category | flops | bytes accessed | tf_op | source)
XLA Modules:
  0.0 234.7 jit_solution(10337058527985146958)
XLA Ops:
  11.1 10.2 %all-to-all-start = ((bf16[16,6,16,128]{3,2,1,0:T(8,128)(2,1)}), bf16[16,6,16,128]{3,2,1,0:T(8,128)(2,1)S(1)}, u32[]{:S(2)}, u32[]{:S(2)}) async-start(bf16[16,6,16,128]{3,2,1,0:T(8,128)(2,1)} %pad_maximum_fusion), calls=%async_computation | async-start | bytes 786432 | tf_op jit(solution)/shard_map/all_to_all | solution.py:300
  24.1 7.5 %collective-permute-start.2 = (bf16[768,128]{1,0:T(8,128)(2,1)S(1)}, bf16[768,128]{1,0:T(8,128)(2,1)S(1)}, u32[]{:S(2)}, u32[]{:S(2)}) collective-permute-start(bf16[768,128]{1,0:T(8,128)(2,1)S(1)} %shard_map.65), channel_id=1, source_target_pairs={{0,256},{64,320},{128,384},{192,448},{256,0},{320,64},{384,128},{4... | collective-permute-start | bytes 589832 | tf_op jit(solution)/shard_map/ppermute | solution.py:24
  37.7 8.4 %all-to-all-start.1 = ((bf16[8,16,128]{2,1,0:T(8,128)(2,1)}), bf16[8,16,128]{2,1,0:T(8,128)(2,1)S(1)}, u32[]{:S(2)}, u32[]{:S(2)}) async-start(bf16[8,16,128]{2,1,0:T(8,128)(2,1)} %bitcast.19), calls=%async_computation.1 | async-start | bytes 65536 | tf_op jit(solution)/shard_map/all_to_all | solution.py:325
  46.1 7.4 %all-to-all-done.1.refs_0_ = bf16[8,16,128]{2,1,0:T(8,128)(2,1)S(1)} async-done(((bf16[8,16,128]{2,1,0:T(8,128)(2,1)}), bf16[8,16,128]{2,1,0:T(8,128)(2,1)S(1)}, u32[]{:S(2)}, u32[]{:S(2)}) %all-to-all-start.1) | async-done | bytes 32800 | tf_op jit(solution)/shard_map/all_to_all | solution.py:325
  54.3 5.7 %all-to-all-start.2 = ((bf16[64,16,128]{2,1,0:T(8,128)(2,1)}), bf16[64,16,128]{2,1,0:T(8,128)(2,1)S(1)}, u32[]{:S(2)}, u32[]{:S(2)}) async-start(bf16[64,16,128]{2,1,0:T(8,128)(2,1)} %get-tuple-element.55), calls=%async_computation.2 | async-start | bytes 524288 | tf_op jit(solution)/shard_map/all_to_all | solution.py:284
  63.7 9.1 %all-to-all-done.2 = bf16[64,16,128]{2,1,0:T(8,128)(2,1)S(1)} async-done(((bf16[64,16,128]{2,1,0:T(8,128)(2,1)}), bf16[64,16,128]{2,1,0:T(8,128)(2,1)S(1)}, u32[]{:S(2)}, u32[]{:S(2)}) %all-to-all-start.2) | async-done | bytes 262176 | tf_op jit(solution)/shard_map/all_to_all | solution.py:284
  78.5 4.2 %collective-permute-start.3 = (bf16[8,128,128]{2,1,0:T(8,128)(2,1)S(1)}, bf16[8,128,128]{2,1,0:T(8,128)(2,1)S(1)}, u32[]{:S(2)}, u32[]{:S(2)}) collective-permute-start(bf16[8,128,128]{2,1,0:T(8,128)(2,1)S(1)} %bitcast.42), channel_id=1, source_target_pairs={{0,4},{4,0},{1,5},{5,1},{2,6},{6,2},{3,7},{7,3},{8,12},{12,8},{9,1... | collective-permute-start | bytes 786440 | tf_op jit(solution)/shard_map/ppermute | solution.py:28
  83.1 4.5 %collective-permute-start.4 = (bf16[768,128]{1,0:T(8,128)(2,1)S(1)}, bf16[768,128]{1,0:T(8,128)(2,1)S(1)}, u32[]{:S(2)}, u32[]{:S(2)}) collective-permute-start(bf16[768,128]{1,0:T(8,128)(2,1)S(1)} %get-tuple-element.59), channel_id=1, source_target_pairs={{0,128},{64,192},{128,0},{192,64},{256,384},{320,448},{384,256},{4... | collective-permute-start | bytes 589832 | tf_op jit(solution)/shard_map/ppermute | solution.py:24
  92.6 4.4 %collective-permute-done.4.got = bf16[768,128]{1,0:T(8,128)(2,1)S(1)} collective-permute-done((bf16[768,128]{1,0:T(8,128)(2,1)S(1)}, bf16[768,128]{1,0:T(8,128)(2,1)S(1)}, u32[]{:S(2)}, u32[]{:S(2)}) %collective-permute-start.4) | collective-permute-done | bytes 196640 | tf_op jit(solution)/shard_map/ppermute | solution.py:24
  100.5 6.2 %all-to-all-start.5 = ((bf16[64,16,128]{2,1,0:T(8,128)(2,1)}), bf16[64,16,128]{2,1,0:T(8,128)(2,1)S(1)}, u32[]{:S(2)}, u32[]{:S(2)}) async-start(bf16[64,16,128]{2,1,0:T(8,128)(2,1)} %get-tuple-element.61), calls=%async_computation.5 | async-start | bytes 524288 | tf_op jit(solution)/shard_map/all_to_all | solution.py:284
  106.9 4.9 %shard_map.70.refs_4_ = f32[768,128]{1,0:T(8,128)} custom-call(s32[1]{0:T(128)} %bitcast.core.refs_0_, bf16[768,2048]{1,0:T(8,128)(2,1)} %bitcast.39, bf16[8,128,128]{2,1,0:T(8,128)(2,1)} %bitcast.43, bf16[8,128,128]{2,1,0:T(8,128)(2,1)} %copy-done.15, f32[768,128]{1,0:T(8,128)} %copy-done.9, bf16[768,128]{1,0:T(8,128)(2,1)} %copy-done.19), custom_call_target="tpu_custom_call" | custom-call | flops 402653184 | bytes 3145728 | tf_op jit(solution)/shard_map/pallas_call | solution.py:360
  111.7 8.1 %all-to-all-done.5 = bf16[64,16,128]{2,1,0:T(8,128)(2,1)S(1)} async-done(((bf16[64,16,128]{2,1,0:T(8,128)(2,1)}), bf16[64,16,128]{2,1,0:T(8,128)(2,1)S(1)}, u32[]{:S(2)}, u32[]{:S(2)}) %all-to-all-start.5) | async-done | bytes 262176 | tf_op jit(solution)/shard_map/all_to_all | solution.py:284
  119.8 4.8 %collective-permute-start.5 = (bf16[8,128,128]{2,1,0:T(8,128)(2,1)S(1)}, bf16[8,128,128]{2,1,0:T(8,128)(2,1)}, u32[]{:S(2)}, u32[]{:S(2)}) collective-permute-start(bf16[8,128,128]{2,1,0:T(8,128)(2,1)S(1)} %bitcast.48), channel_id=1, source_target_pairs={{0,4},{4,0},{1,5},{5,1},{2,6},{6,2},{3,7},{7,3},{8,12},{12,8},{9,1... | collective-permute-start | bytes 786440 | tf_op jit(solution)/shard_map/ppermute | solution.py:28
  125.9 7.3 %shard_map.71 = (f32[768,128]{1,0:T(8,128)}, bf16[768,128]{1,0:T(8,128)(2,1)}, f32[8,128,128]{2,1,0:T(8,128)}, bf16[8,128,128]{2,1,0:T(8,128)(2,1)}) custom-call(s32[1]{0:T(128)} %bitcast.core.refs_0_, bf16[768,2048]{1,0:T(8,128)(2,1)} %all-gather.5.cloned.1.call-done.refs_1_, bf16[8,128,128]{2,1,0:T(8,128)(2,1)} %bitcast.49, ...), custom_call_target="tpu_custom_call" | custom-call | flops 402653184 | bytes 3145728 | tf_op jit(solution)/shard_map/pallas_call | solution.py:372
  138.7 5.5 %all-to-all-start.6 = ((bf16[64,16,128]{2,1,0:T(8,128)(2,1)}), bf16[64,16,128]{2,1,0:T(8,128)(2,1)}, u32[]{:S(2)}, u32[]{:S(2)}) async-start(bf16[64,16,128]{2,1,0:T(8,128)(2,1)} %bitcast.26), calls=%async_computation.6 | async-start | bytes 524288 | tf_op jit(solution)/shard_map/all_to_all | solution.py:281
  144.2 4.2 %shard_map.72 = (f32[8,128,128]{2,1,0:T(8,128)S(1)}, bf16[8,128,128]{2,1,0:T(8,128)(2,1)S(1)}) custom-call(s32[1]{0:T(128)} %bitcast.core.refs_0_, bf16[768,2048]{1,0:T(8,128)(2,1)S(1)} %bitcast.40, bf16[768,128]{1,0:T(8,128)(2,1)} %get-tuple-element.71.rounded), custom_call_target="tpu_custom_call" | custom-call | flops 402653184 | bytes 3145728 | tf_op jit(solution)/shard_map/pallas_call | solution.py:382
  160.1 5.4 %all-to-all-start.7 = ((bf16[16,16,128]{2,1,0:T(8,128)(2,1)}), bf16[16,16,128]{2,1,0:T(8,128)(2,1)S(1)}, u32[]{:S(2)}, u32[]{:S(2)}) async-start(bf16[16,16,128]{2,1,0:T(8,128)(2,1)} %get-tuple-element.77), calls=%async_computation.7 | async-start | bytes 131072 | tf_op jit(solution)/shard_map/all_to_all | solution.py:393
  167.0 5.6 %all-to-all-done.7 = bf16[16,16,128]{2,1,0:T(8,128)(2,1)S(1)} async-done(((bf16[16,16,128]{2,1,0:T(8,128)(2,1)}), bf16[16,16,128]{2,1,0:T(8,128)(2,1)S(1)}, u32[]{:S(2)}, u32[]{:S(2)}) %all-to-all-start.7) | async-done | bytes 65568 | tf_op jit(solution)/shard_map/all_to_all | solution.py:393
  176.2 6.3 %all-to-all-start.8 = ((bf16[64,16,128]{2,1,0:T(8,128)(2,1)}), bf16[64,16,128]{2,1,0:T(8,128)(2,1)S(1)}, u32[]{:S(2)}, u32[]{:S(2)}) async-start(bf16[64,16,128]{2,1,0:T(8,128)(2,1)} %bitcast.53), calls=%async_computation.8 | async-start | bytes 524288 | tf_op jit(solution)/shard_map/all_to_all | solution.py:281
  182.9 6.9 %collective-permute-start.9 = (bf16[768,128]{1,0:T(8,128)(2,1)S(1)}, bf16[768,128]{1,0:T(8,128)(2,1)S(1)}, u32[]{:S(2)}, u32[]{:S(2)}) collective-permute-start(bf16[768,128]{1,0:T(8,128)(2,1)S(1)} %get-tuple-element.88), channel_id=1, source_target_pairs={{0,256},{64,320},{128,384},{192,448},{256,0},{320,64},{384,128},{4... | collective-permute-start | bytes 589832 | tf_op jit(solution)/shard_map/ppermute | solution.py:24
  189.8 5.6 %all-to-all-done.8.refs_0_ = bf16[64,16,128]{2,1,0:T(8,128)(2,1)S(1)} async-done(((bf16[64,16,128]{2,1,0:T(8,128)(2,1)}), bf16[64,16,128]{2,1,0:T(8,128)(2,1)S(1)}, u32[]{:S(2)}, u32[]{:S(2)}) %all-to-all-start.8) | async-done | bytes 262176 | tf_op jit(solution)/shard_map/all_to_all | solution.py:281
  201.7 4.8 %all-to-all-done.9 = bf16[8,16,128]{2,1,0:T(8,128)(2,1)S(1)} async-done(((bf16[8,16,128]{2,1,0:T(8,128)(2,1)}), bf16[8,16,128]{2,1,0:T(8,128)(2,1)S(1)}, u32[]{:S(2)}, u32[]{:S(2)}) %all-to-all-start.9) | async-done | bytes 32800 | tf_op jit(solution)/shard_map/all_to_all | solution.py:402
  208.6 9.8 %all-to-all-start.10 = ((bf16[16,32,128]{2,1,0:T(8,128)(2,1)}), bf16[16,32,128]{2,1,0:T(8,128)(2,1)S(1)}, u32[]{:S(2)}, u32[]{:S(2)}) async-start(bf16[16,32,128]{2,1,0:T(8,128)(2,1)} %shard_map.77), calls=%async_computation.10 | async-start | bytes 262144 | tf_op jit(solution)/shard_map/all_to_all | solution.py:410
  219.2 8.3 %all-to-all-done.10 = bf16[16,32,128]{2,1,0:T(8,128)(2,1)S(1)} async-done(((bf16[16,32,128]{2,1,0:T(8,128)(2,1)}), bf16[16,32,128]{2,1,0:T(8,128)(2,1)S(1)}, u32[]{:S(2)}, u32[]{:S(2)}) %all-to-all-start.10) | async-done | bytes 131104 | tf_op jit(solution)/shard_map/all_to_all | solution.py:410
  (128 shorter events, 66.1 us)
Async XLA Ops:
  6.5 53.5 %all-gather.9.cloned.1.call-start = ((), (), s32[]{:S(2)}) async-start(), calls=%async_computation.13 | async-start | bytes 3932160 | tf_op jit(solution)/shard_map/all_gather | solution.py:286
  11.1 24.8 %all-to-all-start = ((bf16[16,6,16,128]{3,2,1,0:T(8,128)(2,1)}), bf16[16,6,16,128]{3,2,1,0:T(8,128)(2,1)S(1)}, u32[]{:S(2)}, u32[]{:S(2)}) async-start(bf16[16,6,16,128]{3,2,1,0:T(8,128)(2,1)} %pad_maximum_fusion), calls=%async_computation | async-start | bytes 786432 | tf_op jit(solution)/shard_map/all_to_all | solution.py:300
  21.5 10.4 %collective-permute-start = (f32[32,128]{1,0:T(8,128)S(1)}, f32[32,128]{1,0:T(8,128)S(1)}, u32[]{:S(2)}, u32[]{:S(2)}) collective-permute-start(f32[32,128]{1,0:T(8,128)S(1)} %broadcast_in_dim.35), channel_id=1, source_target_pairs={{0,0},{4,8},{8,16},{12,24},{16,32},{20,40},{24,48},{28,56},{32,4},... | collective-permute-start | bytes 49160 | tf_op jit(solution)/shard_map/ppermute | solution.py:303
  24.1 22.0 %collective-permute-start.2 = (bf16[768,128]{1,0:T(8,128)(2,1)S(1)}, bf16[768,128]{1,0:T(8,128)(2,1)S(1)}, u32[]{:S(2)}, u32[]{:S(2)}) collective-permute-start(bf16[768,128]{1,0:T(8,128)(2,1)S(1)} %shard_map.65), channel_id=1, source_target_pairs={{0,256},{64,320},{128,384},{192,448},{256,0},{320,64},{384,128},{4... | collective-permute-start | bytes 589832 | tf_op jit(solution)/shard_map/ppermute | solution.py:24
  37.7 15.9 %all-to-all-start.1 = ((bf16[8,16,128]{2,1,0:T(8,128)(2,1)}), bf16[8,16,128]{2,1,0:T(8,128)(2,1)S(1)}, u32[]{:S(2)}, u32[]{:S(2)}) async-start(bf16[8,16,128]{2,1,0:T(8,128)(2,1)} %bitcast.19), calls=%async_computation.1 | async-start | bytes 65536 | tf_op jit(solution)/shard_map/all_to_all | solution.py:325
  46.1 65.6 %all-gather.5.cloned.1.call-start = ((), (), s32[]{:S(2)}) async-start(), calls=%async_computation.11 | async-start | bytes 3932160 | tf_op jit(solution)/shard_map/all_gather | solution.py:329
  54.3 18.5 %all-to-all-start.2 = ((bf16[64,16,128]{2,1,0:T(8,128)(2,1)}), bf16[64,16,128]{2,1,0:T(8,128)(2,1)S(1)}, u32[]{:S(2)}, u32[]{:S(2)}) async-start(bf16[64,16,128]{2,1,0:T(8,128)(2,1)} %get-tuple-element.55), calls=%async_computation.2 | async-start | bytes 524288 | tf_op jit(solution)/shard_map/all_to_all | solution.py:284
  60.9 11.9 %collective-permute-start.1 = (bf16[16,2048]{1,0:T(8,128)(2,1)S(1)}, bf16[16,2048]{1,0:T(8,128)(2,1)S(1)}, u32[]{:S(2)}, u32[]{:S(2)}) collective-permute-start(bf16[16,2048]{1,0:T(8,128)(2,1)S(1)} %slice_bitcast_fusion.1.mine_rows), channel_id=1, source_target_pairs={{0,4},{4,0},{1,5},{5,1},{2,6},{6,2},{3,7},{7,3},{8,12},{12,8},{9,1... | collective-permute-start | bytes 196616 | tf_op jit(solution)/shard_map/ppermute | solution.py:28
  73.7 13.9 %all-to-all-start.3 = ((bf16[8,32,128]{2,1,0:T(8,128)(2,1)}), bf16[8,32,128]{2,1,0:T(8,128)(2,1)S(1)}, u32[]{:S(2)}, u32[]{:S(2)}) async-start(bf16[8,32,128]{2,1,0:T(8,128)(2,1)} %shard_map.67), calls=%async_computation.3 | async-start | bytes 131072 | tf_op jit(solution)/shard_map/all_to_all | solution.py:343
  78.5 18.6 %collective-permute-start.3 = (bf16[8,128,128]{2,1,0:T(8,128)(2,1)S(1)}, bf16[8,128,128]{2,1,0:T(8,128)(2,1)S(1)}, u32[]{:S(2)}, u32[]{:S(2)}) collective-permute-start(bf16[8,128,128]{2,1,0:T(8,128)(2,1)S(1)} %bitcast.42), channel_id=1, source_target_pairs={{0,4},{4,0},{1,5},{5,1},{2,6},{6,2},{3,7},{7,3},{8,12},{12,8},{9,1... | collective-permute-start | bytes 786440 | tf_op jit(solution)/shard_map/ppermute | solution.py:28
  83.1 13.9 %collective-permute-start.4 = (bf16[768,128]{1,0:T(8,128)(2,1)S(1)}, bf16[768,128]{1,0:T(8,128)(2,1)S(1)}, u32[]{:S(2)}, u32[]{:S(2)}) collective-permute-start(bf16[768,128]{1,0:T(8,128)(2,1)S(1)} %get-tuple-element.59), channel_id=1, source_target_pairs={{0,128},{64,192},{128,0},{192,64},{256,384},{320,448},{384,256},{4... | collective-permute-start | bytes 589832 | tf_op jit(solution)/shard_map/ppermute | solution.py:24
  88.4 11.4 %all-to-all-start.4 = ((bf16[16,16,128]{2,1,0:T(8,128)(2,1)}), bf16[16,16,128]{2,1,0:T(8,128)(2,1)S(1)}, u32[]{:S(2)}, u32[]{:S(2)}) async-start(bf16[16,16,128]{2,1,0:T(8,128)(2,1)} %bitcast.23), calls=%async_computation.4 | async-start | bytes 131072 | tf_op jit(solution)/shard_map/all_to_all | solution.py:346
  100.5 19.3 %all-to-all-start.5 = ((bf16[64,16,128]{2,1,0:T(8,128)(2,1)}), bf16[64,16,128]{2,1,0:T(8,128)(2,1)S(1)}, u32[]{:S(2)}, u32[]{:S(2)}) async-start(bf16[64,16,128]{2,1,0:T(8,128)(2,1)} %get-tuple-element.61), calls=%async_computation.5 | async-start | bytes 524288 | tf_op jit(solution)/shard_map/all_to_all | solution.py:284
  106.7 65.9 %all-gather.7.cloned.1.call-start = ((), (), s32[]{:S(2)}) async-start(), calls=%async_computation.12 | async-start | bytes 1114112 | tf_op jit(solution)/shard_map/all_gather | solution.py:369
  119.8 6.1 %collective-permute-start.5 = (bf16[8,128,128]{2,1,0:T(8,128)(2,1)S(1)}, bf16[8,128,128]{2,1,0:T(8,128)(2,1)}, u32[]{:S(2)}, u32[]{:S(2)}) collective-permute-start(bf16[8,128,128]{2,1,0:T(8,128)(2,1)S(1)} %bitcast.48), channel_id=1, source_target_pairs={{0,4},{4,0},{1,5},{5,1},{2,6},{6,2},{3,7},{7,3},{8,12},{12,8},{9,1... | collective-permute-start | bytes 786440 | tf_op jit(solution)/shard_map/ppermute | solution.py:28
  133.2 3.7 %collective-permute-start.6 = (bf16[8,128,128]{2,1,0:T(8,128)(2,1)}, bf16[8,128,128]{2,1,0:T(8,128)(2,1)S(1)}, u32[]{:S(2)}, u32[]{:S(2)}) collective-permute-start(bf16[8,128,128]{2,1,0:T(8,128)(2,1)} %get-tuple-element.70), channel_id=1, source_target_pairs={{0,4},{4,0},{1,5},{5,1},{2,6},{6,2},{3,7},{7,3},{8,12},{12,8},{9,1... | collective-permute-start | bytes 786440 | tf_op jit(solution)/shard_map/ppermute | solution.py:28
  138.7 19.8 %all-to-all-start.6 = ((bf16[64,16,128]{2,1,0:T(8,128)(2,1)}), bf16[64,16,128]{2,1,0:T(8,128)(2,1)}, u32[]{:S(2)}, u32[]{:S(2)}) async-start(bf16[64,16,128]{2,1,0:T(8,128)(2,1)} %bitcast.26), calls=%async_computation.6 | async-start | bytes 524288 | tf_op jit(solution)/shard_map/all_to_all | solution.py:281
  149.3 7.1 %collective-permute-start.7 = (bf16[8,128,128]{2,1,0:T(8,128)(2,1)S(1)}, bf16[8,128,128]{2,1,0:T(8,128)(2,1)S(1)}, u32[]{:S(2)}, u32[]{:S(2)}) collective-permute-start(bf16[8,128,128]{2,1,0:T(8,128)(2,1)S(1)} %get-tuple-element.73), channel_id=1, source_target_pairs={{0,4},{4,0},{1,5},{5,1},{2,6},{6,2},{3,7},{7,3},{8,12},{12,8},{9,1... | collective-permute-start | bytes 786440 | tf_op jit(solution)/shard_map/ppermute | solution.py:28
  151.7 15.4 %collective-permute-start.8 = (bf16[768,128]{1,0:T(8,128)(2,1)}, bf16[768,128]{1,0:T(8,128)(2,1)S(1)}, u32[]{:S(2)}, u32[]{:S(2)}) collective-permute-start(bf16[768,128]{1,0:T(8,128)(2,1)} %get-tuple-element.71.rounded), channel_id=1, source_target_pairs={{0,128},{64,192},{128,0},{192,64},{256,384},{320,448},{384,256},{4... | collective-permute-start | bytes 589832 | tf_op jit(solution)/shard_map/ppermute | solution.py:24
  160.1 12.6 %all-to-all-start.7 = ((bf16[16,16,128]{2,1,0:T(8,128)(2,1)}), bf16[16,16,128]{2,1,0:T(8,128)(2,1)S(1)}, u32[]{:S(2)}, u32[]{:S(2)}) async-start(bf16[16,16,128]{2,1,0:T(8,128)(2,1)} %get-tuple-element.77), calls=%async_computation.7 | async-start | bytes 131072 | tf_op jit(solution)/shard_map/all_to_all | solution.py:393
  176.2 19.2 %all-to-all-start.8 = ((bf16[64,16,128]{2,1,0:T(8,128)(2,1)}), bf16[64,16,128]{2,1,0:T(8,128)(2,1)S(1)}, u32[]{:S(2)}, u32[]{:S(2)}) async-start(bf16[64,16,128]{2,1,0:T(8,128)(2,1)} %bitcast.53), calls=%async_computation.8 | async-start | bytes 524288 | tf_op jit(solution)/shard_map/all_to_all | solution.py:281
  182.9 18.8 %collective-permute-start.9 = (bf16[768,128]{1,0:T(8,128)(2,1)S(1)}, bf16[768,128]{1,0:T(8,128)(2,1)S(1)}, u32[]{:S(2)}, u32[]{:S(2)}) collective-permute-start(bf16[768,128]{1,0:T(8,128)(2,1)S(1)} %get-tuple-element.88), channel_id=1, source_target_pairs={{0,256},{64,320},{128,384},{192,448},{256,0},{320,64},{384,128},{4... | collective-permute-start | bytes 589832 | tf_op jit(solution)/shard_map/ppermute | solution.py:24
  196.1 10.5 %all-to-all-start.9 = ((bf16[8,16,128]{2,1,0:T(8,128)(2,1)}), bf16[8,16,128]{2,1,0:T(8,128)(2,1)S(1)}, u32[]{:S(2)}, u32[]{:S(2)}) async-start(bf16[8,16,128]{2,1,0:T(8,128)(2,1)} %get-tuple-element.85), calls=%async_computation.9 | async-start | bytes 65536 | tf_op jit(solution)/shard_map/all_to_all | solution.py:402
  208.6 18.9 %all-to-all-start.10 = ((bf16[16,32,128]{2,1,0:T(8,128)(2,1)}), bf16[16,32,128]{2,1,0:T(8,128)(2,1)S(1)}, u32[]{:S(2)}, u32[]{:S(2)}) async-start(bf16[16,32,128]{2,1,0:T(8,128)(2,1)} %shard_map.77), calls=%async_computation.10 | async-start | bytes 262144 | tf_op jit(solution)/shard_map/all_to_all | solution.py:410
  (26 other events, 532.9 us)
Sparse Core Ops, SparseCore 0:
  9.6 50.3 all-gather.8
  62.1 45.1 all-gather.4
  119.9 36.1 all-gather.6
